TPU v7x, 32 devices: a whole 2x2x4 slice. The times are simulated.
32 devices in a mesh: seq: 8 (over y, x, core), head: 4 (over z).
Axes of the slice: x: 2, y: 2, z: 4, core: 2. Of those that a mesh axis runs over, the one named last changes fastest.
Arguments:
- queries: bfloat16 [16384, 4096], P('seq', 'head'), may hold values from -2 to 2
- key_rows: bfloat16 [16384, 4096], P('seq', 'head'), may hold values from -2 to 2
- value_rows: bfloat16 [16384, 4096], P('seq', 'head'), may hold values from -128 to 128
- decay_log: float32 [32, 16384], P('head', 'seq'), may hold values from -0.8 to 0
- norm_gain: float32 [4096], P('head'), may hold values from 0.1 to 1.9
- page_owner: int32 [16], replicated, may hold values from 0 to 7, as said below
Outputs:
- attended: bfloat16 [16384, 4096], P('seq', 'head')
- page_cache: bfloat16 [40, 32, 128, 128], P('seq', 'head')
Inputs may be any that keep to these rules, and one draw needn't show every extreme that they name: `page_owner`: the 2 pages p = i * 2 to (i + 1) * 2 - 1 have different owners for every i; no owner keeps more than 5 pages and one keeps exactly 5.
All inputs are finite; a program needn't handle non-finite values.
Results may differ from a plain program's by a relative error of at most 0.0042.
Values may be sent and summed in bfloat16 or wider, within the bound.
No kernel may reach another device: no remote copies, remote signals or barrier semaphores. Data moves between devices by JAX's collectives and lax.ppermute only.
A program may use at most 128 MiB of HBM per device.

v0:
```python
import jax
import jax.numpy as jnp
from jax import lax
from jax.sharding import PartitionSpec as P

BLOCK = 512
PAGE = 1024
SLOTS = 5


def from_behind(value, axis, steps):
    count = lax.axis_size(axis)
    first, last = (max(0, -steps), min(count, count - steps))
    return lax.ppermute(value, axis, [(source, source + steps) for source in range(first, last)])


def block_terms(query_blk, key_blk, value_blk, cumulative, carry_state):
    length = cumulative.shape[1]
    token_positions = jnp.arange(length)
    causal = (token_positions[:, None] >= token_positions[None, :])[None]
    spread = cumulative[:, :, None] - cumulative[:, None, :]
    damping = jnp.where(causal, jnp.exp(jnp.where(causal, spread, 0.0)), 0.0)
    scores = jnp.einsum("thd,shd->hts", query_blk, key_blk, preferred_element_type=jnp.float32)
    weights = (scores * damping).astype(jnp.bfloat16)
    inner_sum = jnp.einsum("hts,shd->thd", weights, value_blk, preferred_element_type=jnp.float32)
    carried = jnp.einsum(
        "thd,hde->the", query_blk.astype(jnp.float32), carry_state, precision=lax.Precision.HIGHEST
    )
    output = inner_sum + carried * jnp.exp(cumulative).T[:, :, None]
    scaled_keys = (
        key_blk.astype(jnp.float32) * jnp.exp(cumulative[:, -1:] - cumulative).T[:, :, None]
    ).astype(jnp.bfloat16)
    update = jnp.einsum("shd,she->hde", scaled_keys, value_blk, preferred_element_type=jnp.float32)
    new_state = jnp.exp(cumulative[:, -1])[:, None, None] * carry_state + update
    return (output, new_state)


def combine(earlier, following):
    return (
        earlier[0] + following[0],
        jnp.exp(following[0])[:, None, None] * earlier[1] + following[1],
    )


def shards(queries, key_rows, value_rows, decay_log, norm_gain, page_owner):
    tok_rows, width_dev = queries.shape
    head_count = decay_log.shape[0]
    head_dim = width_dev // head_count
    block_count = tok_rows // BLOCK
    grid_shape = (block_count, BLOCK, head_count, head_dim)
    query_blocks = queries.reshape(grid_shape)
    key_blocks = key_rows.reshape(grid_shape)
    value_blocks = value_rows.reshape(grid_shape)
    cumulative = jnp.cumsum(decay_log.reshape(head_count, block_count, BLOCK), axis=2)
    block_decay = cumulative[:, :, -1]
    reached = jnp.cumsum(block_decay, axis=1)

    def local_step(carry_state, pieces):
        query_blk, key_blk, value_blk, decay_blk = pieces
        output, new_state = block_terms(query_blk, key_blk, value_blk, decay_blk, carry_state)
        return (new_state, (output, new_state))

    zero_state = jnp.zeros((head_count, head_dim, head_dim), jnp.float32)
    local_end, (local_out, block_states) = lax.scan(
        local_step,
        zero_state,
        (query_blocks, key_blocks, value_blocks, cumulative.transpose(1, 0, 2)),
    )
    own_part = (reached[:, -1], local_end)
    identity = (jnp.zeros((head_count,), jnp.float32), zero_state)

    def relay_turn(turn_index, incoming):
        return from_behind(combine(incoming, own_part), "seq", 1)

    incoming = lax.fori_loop(0, lax.axis_size("seq") - 1, relay_turn, identity)
    entry_state = incoming[1]
    start_log = reached - block_decay
    total_log = (cumulative + start_log[:, :, None]).reshape(head_count, tok_rows).T
    entry_term = jnp.einsum(
        "thd,hde->the",
        queries.reshape(tok_rows, head_count, head_dim).astype(jnp.float32),
        entry_state,
        precision=lax.Precision.HIGHEST,
    )
    output = (
        local_out.reshape(tok_rows, head_count, head_dim)
        + entry_term * jnp.exp(total_log)[:, :, None]
    )
    square_sum = jnp.sum(output * output, axis=(1, 2))
    total_square = lax.psum(square_sum, "head")
    scale_row = lax.rsqrt(total_square / (head_count * head_dim * lax.axis_size("head")) + 1e-06)
    normed = output * scale_row[:, None, None] * norm_gain.reshape(head_count, head_dim)[None]
    attended = normed.astype(jnp.bfloat16).reshape(tok_rows, width_dev)
    per_page = PAGE // BLOCK
    page_decay = jnp.exp(reached[:, per_page - 1 :: per_page]).T
    snapshots = (
        page_decay[:, :, None, None] * entry_state[None] + block_states[per_page - 1 :: per_page]
    ).astype(jnp.bfloat16)
    page_order = jnp.arange(page_owner.shape[0])
    earlier = (page_owner[:, None] == page_owner[None, :]) & (
        page_order[None, :] < page_order[:, None]
    )
    slot_index = jnp.sum(earlier.astype(jnp.int32), axis=1)
    seq_index = lax.axis_index("seq")
    slot_ids = jnp.arange(SLOTS)
    chosen = (page_owner[None, :] == seq_index) & (slot_index[None, :] == slot_ids[:, None])
    gathered = jnp.einsum(
        "sn,nhde->shde",
        chosen.astype(jnp.bfloat16),
        lax.all_gather(snapshots, "seq", axis=0, tiled=True),
        preferred_element_type=jnp.float32,
    )
    page_cache = gathered.astype(jnp.bfloat16)
    return (attended, page_cache)


def solution(mesh):
    return jax.shard_map(
        shards,
        mesh=mesh,
        in_specs=(
            P("seq", "head"),
            P("seq", "head"),
            P("seq", "head"),
            P("head", "seq"),
            P("head"),
            P(),
        ),
        out_specs=(P("seq", "head"), P("seq", "head", None, None)),
        check_vma=False,
    )
```

profile of v0, /device:TPU:4, one launch (start us, length us, event | category | flops | bytes accessed | tf_op | source)
XLA Modules:
  0.0 427.6 jit_solution(8657997811497120332)
XLA Ops:
  8.1 4.5 %reduce-window.6 = f32[8,4,4,128]{3,0,1,2:T(8,128)S(1)} reduce-window(f32[8,4,4,128]{3,0,1,2:T(8,128)S(1)} %copy.102, f32[]{:T(128)} %constant.45.clone.1), window={size=1x1x1x128 pad=0_0x0_0x0_0x127_0}, to_apply=%region_0.0 | reduce-window | flops 2080768 | bytes 131076 | tf_op jit(solution)/shard_map/reduce-window
  15.6 5.5 %copy.136 = bf16[256,8,8,128]{3,2,1,0:T(8,128)(2,1)} copy(bf16[256,8,8,128]{3,1,2,0:T(8,128)(2,1)} %bitcast.139) | data formatting | bytes 8388608
  21.1 3.1 copy.137
  24.2 3.0 copy.138
  27.2 248.1 %while.28 = (s32[]{:T(128)}, f32[8,128,128]{2,1,0:T(8,128)}, f32[4,512,8,128]{1,0,3,2:T(4,128)}, f32[4,8,128,128]{3,2,1,0:T(8,128)}, f32[4,8,512]{2,1,0:T(8,128)...) while((s32[]{:T(128)}, f32[8,128,128]{2,1,0:T(8,128)}, ...), condition=%wide.region_3.4_spmd.clone, body=%wide.region_2.3_spmd.clone.sunk | while | flops 2027163648 | bytes 38535560 | solution.py:64
  28.6 2.1 constant_dynamic-slice_fusion.7
  30.7 5.2 %fusion.41 = f32[8,128,512]{2,1,0:T(8,128)} fusion(f32[8,512]{1,0:T(8,128)S(1)} %fusion.40, pred[512,512]{1,0:T(8,128)(4,1)S(1)} %iota_compare_fusion.4, bf16[1,512,8,128]{3,2,1,0:T(8,128)(2,1)S(1)} %constant_dynamic-slice_fusion.9, bf16[1,512,8,128]{3,2,1,0:T(8,128)(2,1)S(1)} %get-tuple-element.291, bf16[1,512,8,128]{3,2,1,0:T(8,128)(2,1)S(1)} %get-tuple-element.294), kind=kOutput, calls=%fused_computation.2.clone.1 | convolution fusion | flops 1084227584 | bytes 5521408 | tf_op jit(solution)/shard_map/while/body/eval_jaxpr/hts,shd->thd/dot_general | solution.py:25
  37.0 2.7 fusion.42
  40.7 3.9 bitcast_dynamic-update-slice_fusion.2
  44.6 3.5 copy.188
  48.1 41.0 %dynamic_update_slice.14 = f32[4,512,8,128]{1,0,3,2:T(4,128)} dynamic-update-slice(f32[4,512,8,128]{1,0,3,2:T(4,128)} %get-tuple-element.309, f32[1,512,8,128]{1,0,3,2:T(1,128)} %copy.188, s32[]{:T(128)S(6)} %copy.195, s32[]{:T(128)} %constant.44.clone.1..sunk, s32[]{:T(128)} %constant.44.clone.1..sunk, s32[]{:T(128)} %constant.44.clone.1..sunk) | dynamic-update-slice | bytes 4194308 | tf_op jit(solution)/shard_map/while/body/jit(dynamic_update_index_in_dim)/dynamic_update_slice | solution.py:64
  90.5 2.1 constant_dynamic-slice_fusion.7
  92.5 5.2 %fusion.41 = f32[8,128,512]{2,1,0:T(8,128)} fusion(f32[8,512]{1,0:T(8,128)S(1)} %fusion.40, pred[512,512]{1,0:T(8,128)(4,1)S(1)} %iota_compare_fusion.4, bf16[1,512,8,128]{3,2,1,0:T(8,128)(2,1)S(1)} %constant_dynamic-slice_fusion.9, bf16[1,512,8,128]{3,2,1,0:T(8,128)(2,1)S(1)} %get-tuple-element.291, bf16[1,512,8,128]{3,2,1,0:T(8,128)(2,1)S(1)} %get-tuple-element.294), kind=kOutput, calls=%fused_computation.2.clone.1 | convolution fusion | flops 1084227584 | bytes 5521408 | tf_op jit(solution)/shard_map/while/body/eval_jaxpr/hts,shd->thd/dot_general | solution.py:25
  98.7 2.9 fusion.42
  102.7 4.1 bitcast_dynamic-update-slice_fusion.2
  106.8 3.5 copy.188
  110.2 41.0 %dynamic_update_slice.14 = f32[4,512,8,128]{1,0,3,2:T(4,128)} dynamic-update-slice(f32[4,512,8,128]{1,0,3,2:T(4,128)} %get-tuple-element.309, f32[1,512,8,128]{1,0,3,2:T(1,128)} %copy.188, s32[]{:T(128)S(6)} %copy.195, s32[]{:T(128)} %constant.44.clone.1..sunk, s32[]{:T(128)} %constant.44.clone.1..sunk, s32[]{:T(128)} %constant.44.clone.1..sunk) | dynamic-update-slice | bytes 4194308 | tf_op jit(solution)/shard_map/while/body/jit(dynamic_update_index_in_dim)/dynamic_update_slice | solution.py:64
  152.6 2.1 constant_dynamic-slice_fusion.7
  154.6 5.2 %fusion.41 = f32[8,128,512]{2,1,0:T(8,128)} fusion(f32[8,512]{1,0:T(8,128)S(1)} %fusion.40, pred[512,512]{1,0:T(8,128)(4,1)S(1)} %iota_compare_fusion.4, bf16[1,512,8,128]{3,2,1,0:T(8,128)(2,1)S(1)} %constant_dynamic-slice_fusion.9, bf16[1,512,8,128]{3,2,1,0:T(8,128)(2,1)S(1)} %get-tuple-element.291, bf16[1,512,8,128]{3,2,1,0:T(8,128)(2,1)S(1)} %get-tuple-element.294), kind=kOutput, calls=%fused_computation.2.clone.1 | convolution fusion | flops 1084227584 | bytes 5521408 | tf_op jit(solution)/shard_map/while/body/eval_jaxpr/hts,shd->thd/dot_general | solution.py:25
  160.9 2.9 fusion.42
  164.8 4.0 bitcast_dynamic-update-slice_fusion.2
  168.9 3.5 copy.188
  172.3 41.0 %dynamic_update_slice.14 = f32[4,512,8,128]{1,0,3,2:T(4,128)} dynamic-update-slice(f32[4,512,8,128]{1,0,3,2:T(4,128)} %get-tuple-element.309, f32[1,512,8,128]{1,0,3,2:T(1,128)} %copy.188, s32[]{:T(128)S(6)} %copy.195, s32[]{:T(128)} %constant.44.clone.1..sunk, s32[]{:T(128)} %constant.44.clone.1..sunk, s32[]{:T(128)} %constant.44.clone.1..sunk) | dynamic-update-slice | bytes 4194308 | tf_op jit(solution)/shard_map/while/body/jit(dynamic_update_index_in_dim)/dynamic_update_slice | solution.py:64
  214.7 2.1 constant_dynamic-slice_fusion.7
  216.8 5.2 %fusion.41 = f32[8,128,512]{2,1,0:T(8,128)} fusion(f32[8,512]{1,0:T(8,128)S(1)} %fusion.40, pred[512,512]{1,0:T(8,128)(4,1)S(1)} %iota_compare_fusion.4, bf16[1,512,8,128]{3,2,1,0:T(8,128)(2,1)S(1)} %constant_dynamic-slice_fusion.9, bf16[1,512,8,128]{3,2,1,0:T(8,128)(2,1)S(1)} %get-tuple-element.291, bf16[1,512,8,128]{3,2,1,0:T(8,128)(2,1)S(1)} %get-tuple-element.294), kind=kOutput, calls=%fused_computation.2.clone.1 | convolution fusion | flops 1084227584 | bytes 5521408 | tf_op jit(solution)/shard_map/while/body/eval_jaxpr/hts,shd->thd/dot_general | solution.py:25
  223.0 2.9 fusion.42
  226.9 4.0 bitcast_dynamic-update-slice_fusion.2
  231.0 3.5 copy.188
  234.4 41.0 %dynamic_update_slice.14 = f32[4,512,8,128]{1,0,3,2:T(4,128)} dynamic-update-slice(f32[4,512,8,128]{1,0,3,2:T(4,128)} %get-tuple-element.309, f32[1,512,8,128]{1,0,3,2:T(1,128)} %copy.188, s32[]{:T(128)S(6)} %copy.195, s32[]{:T(128)} %constant.44.clone.1..sunk, s32[]{:T(128)} %constant.44.clone.1..sunk, s32[]{:T(128)} %constant.44.clone.1..sunk) | dynamic-update-slice | bytes 4194308 | tf_op jit(solution)/shard_map/while/body/jit(dynamic_update_index_in_dim)/dynamic_update_slice | solution.py:64
  276.1 88.1 %while.27 = (s32[]{:T(128)}, f32[8,128,128]{2,1,0:T(8,128)S(1)}, f32[8,1,1]{0,2,1:T(1,128)}, f32[8,128,128]{2,1,0:T(8,128)}, s32[]{:T(128)}) while((s32[]{:T(128)}, f32[8,128,128]{2,1,0:T(8,128)S(1)}, f32[8,1,1]{0,2,1:T(1,128)}, f32[8,128,128]{2,1,0:T(8,128)}, s32[]{:T(128)}) %tuple.70), condition=%wide.region_6.7_spmd, body=%wide.region_5.6_spmd.sunk | while | flops 262146 | bytes 3670149 | solution.py:75
  277.4 1.9 collective-permute-start
  279.3 9.5 %collective-permute-done = f32[8,128,128]{2,1,0:T(8,128)S(1)} collective-permute-done((f32[8,128,128]{2,1,0:T(8,128)S(1)}, f32[8,128,128]{2,1,0:T(8,128)S(1)}, u32[]{:S(2)}, u32[]{:S(2)}) %collective-permute-start) | collective-permute-done | bytes 524320 | tf_op jit(solution)/shard_map/while/body/eval_jaxpr/ppermute | solution.py:14
  290.0 1.9 collective-permute-start
  291.9 9.5 %collective-permute-done = f32[8,128,128]{2,1,0:T(8,128)S(1)} collective-permute-done((f32[8,128,128]{2,1,0:T(8,128)S(1)}, f32[8,128,128]{2,1,0:T(8,128)S(1)}, u32[]{:S(2)}, u32[]{:S(2)}) %collective-permute-start) | collective-permute-done | bytes 524320 | tf_op jit(solution)/shard_map/while/body/eval_jaxpr/ppermute | solution.py:14
  304.5 9.5 %collective-permute-done = f32[8,128,128]{2,1,0:T(8,128)S(1)} collective-permute-done((f32[8,128,128]{2,1,0:T(8,128)S(1)}, f32[8,128,128]{2,1,0:T(8,128)S(1)}, u32[]{:S(2)}, u32[]{:S(2)}) %collective-permute-start) | collective-permute-done | bytes 524320 | tf_op jit(solution)/shard_map/while/body/eval_jaxpr/ppermute | solution.py:14
  317.0 9.5 %collective-permute-done = f32[8,128,128]{2,1,0:T(8,128)S(1)} collective-permute-done((f32[8,128,128]{2,1,0:T(8,128)S(1)}, f32[8,128,128]{2,1,0:T(8,128)S(1)}, u32[]{:S(2)}, u32[]{:S(2)}) %collective-permute-start) | collective-permute-done | bytes 524320 | tf_op jit(solution)/shard_map/while/body/eval_jaxpr/ppermute | solution.py:14
  327.7 1.9 collective-permute-start
  329.6 9.5 %collective-permute-done = f32[8,128,128]{2,1,0:T(8,128)S(1)} collective-permute-done((f32[8,128,128]{2,1,0:T(8,128)S(1)}, f32[8,128,128]{2,1,0:T(8,128)S(1)}, u32[]{:S(2)}, u32[]{:S(2)}) %collective-permute-start) | collective-permute-done | bytes 524320 | tf_op jit(solution)/shard_map/while/body/eval_jaxpr/ppermute | solution.py:14
  340.2 1.9 collective-permute-start
  342.2 9.5 %collective-permute-done = f32[8,128,128]{2,1,0:T(8,128)S(1)} collective-permute-done((f32[8,128,128]{2,1,0:T(8,128)S(1)}, f32[8,128,128]{2,1,0:T(8,128)S(1)}, u32[]{:S(2)}, u32[]{:S(2)}) %collective-permute-start) | collective-permute-done | bytes 524320 | tf_op jit(solution)/shard_map/while/body/eval_jaxpr/ppermute | solution.py:14
  352.8 1.9 collective-permute-start
  354.7 9.5 %collective-permute-done = f32[8,128,128]{2,1,0:T(8,128)S(1)} collective-permute-done((f32[8,128,128]{2,1,0:T(8,128)S(1)}, f32[8,128,128]{2,1,0:T(8,128)S(1)}, u32[]{:S(2)}, u32[]{:S(2)}) %collective-permute-start) | collective-permute-done | bytes 524320 | tf_op jit(solution)/shard_map/while/body/eval_jaxpr/ppermute | solution.py:14
  365.2 11.0 %reshape.92 = f32[2048,8,128]{0,2,1:T(8,128)} reshape(f32[4,512,8,128]{1,0,3,2:T(4,128)} %get-tuple-element.96) | data formatting | bytes 16777216 | tf_op jit(solution)/shard_map/reshape | solution.py:86
  377.4 12.6 %multiply_reduce_fusion = (f32[2048]{0:T(1024)S(1)}, f32[2048,8,128]{0,2,1:T(8,128)}) fusion(f32[2048,8,128]{0,2,1:T(8,128)} %reshape.92, f32[2048,8]{0,1:T(8,128)S(1)} %exponential_bitcast_fusion.2, f32[8,128,128]{2,1,0:T(8,128)S(1)} %get-tuple-element.98, bf16[2048,1024]{1,0:T(8,128)(2,1)} %param.10), kind=kOutput, calls=%fused_computation.32 | convolution fusion | flops 3229612032 | bytes 21569536 | tf_op jit(solution)/shard_map/thd,hde->the/dot_general | solution.py:79
  390.0 12.1 %psum.7 = f32[2048]{0:T(1024)S(1)} all-reduce(f32[2048]{0:T(1024)S(1)} %get-tuple-element.209), channel_id=1, replica_groups=mesh['seq'=8,'head'=4] {'head'}, use_global_device_ids=true, to_apply=%region_8.9 | all-reduce | flops 2048 | bytes 16384 | tf_op jit(solution)/shard_map/psum | solution.py:90
  402.1 6.1 %multiply_convert_fusion.4 = bf16[2048,8,128]{0,2,1:T(8,128)(2,1)} fusion(f32[2048,8,128]{0,2,1:T(8,128)} %get-tuple-element.210, f32[8,128]{1,0:T(8,128)S(1)} %bitcast.147, f32[2048]{0:T(1024)S(1)} %add_rsqrt_fusion), kind=kLoop, calls=%fused_computation.31 | loop fusion | flops 6291456 | bytes 12595200 | tf_op jit(solution)/shard_map/convert_element_type | solution.py:93
  408.2 6.4 %copy.116 = bf16[2048,1024]{1,0:T(8,128)(2,1)} copy(bf16[2048,1024]{0,1:T(8,128)(2,1)} %bitcast.138) | data formatting | bytes 8388608
  414.8 4.6 %fusion.18 = bf16[5,8,128,128]{3,0,2,1:T(8,128)(2,1)S(1)} fusion(bf16[16,8,128,128]{3,2,1,0:T(8,128)(2,1)} %all-gather.2.cloned.1.call-done, s32[16]{0:T(128)S(1)} %convert_reduce_fusion, pred[16]{0:T(512)(128)(4,1)S(1)} %broadcast_compare_fusion), kind=kOutput, calls=%fused_computation.37 | convolution fusion | flops 21627040 | bytes 5505104 | tf_op jit(solution)/shard_map/sn,nhde->shde/dot_general | solution.py:107
  (115 shorter events, 34.2 us)
Async XLA Ops:
  7.2 407.6 %all-gather.2.cloned.1.call-start = ((), (), s32[]{:S(2)}) async-start(), calls=%async_computation | async-start | bytes 4718592 | tf_op jit(solution)/shard_map/all_gather | solution.py:110
  12.9 0.6 copy-start.6
  13.6 0.6 copy-start.5
  14.4 6.7 %copy-start.8 = (f32[8,4]{0,1:T(4,128)}, f32[8,4]{0,1:T(4,128)S(1)}, u32[]{:S(2)}) copy-start(f32[8,4]{0,1:T(4,128)S(1)} %reduce_window_sum.34) | copy-start | bytes 388
  15.6 5.5 %copy-start.3 = (bf16[2048,1024]{1,0:T(8,128)(2,1)S(1)}, bf16[2048,1024]{1,0:T(8,128)(2,1)}, u32[]{:S(2)}) copy-start(bf16[2048,1024]{1,0:T(8,128)(2,1)} %param.12) | copy-start | bytes 12582916
  21.1 3.1 copy-start.2
  28.6 7.3 %copy-start.1 = (bf16[1,512,8,128]{3,2,1,0:T(8,128)(2,1)}, bf16[1,512,8,128]{3,2,1,0:T(8,128)(2,1)S(1)}, u32[]{:S(2)}) copy-start(bf16[1,512,8,128]{3,2,1,0:T(8,128)(2,1)S(1)} %constant_dynamic-slice_fusion.9) | copy-start | bytes 3145732 | tf_op jit(solution)/shard_map/while
  30.7 5.2 %copy-start = (bf16[1,512,8,128]{3,2,1,0:T(8,128)(2,1)}, bf16[1,512,8,128]{3,2,1,0:T(8,128)(2,1)S(1)}, u32[]{:S(2)}) copy-start(bf16[1,512,8,128]{3,2,1,0:T(8,128)(2,1)S(1)} %get-tuple-element.291) | copy-start | bytes 3145732 | tf_op jit(solution)/shard_map/while
  90.4 7.3 %copy-start.1 = (bf16[1,512,8,128]{3,2,1,0:T(8,128)(2,1)}, bf16[1,512,8,128]{3,2,1,0:T(8,128)(2,1)S(1)}, u32[]{:S(2)}) copy-start(bf16[1,512,8,128]{3,2,1,0:T(8,128)(2,1)S(1)} %constant_dynamic-slice_fusion.9) | copy-start | bytes 3145732 | tf_op jit(solution)/shard_map/while
  92.5 5.2 %copy-start = (bf16[1,512,8,128]{3,2,1,0:T(8,128)(2,1)}, bf16[1,512,8,128]{3,2,1,0:T(8,128)(2,1)S(1)}, u32[]{:S(2)}) copy-start(bf16[1,512,8,128]{3,2,1,0:T(8,128)(2,1)S(1)} %get-tuple-element.291) | copy-start | bytes 3145732 | tf_op jit(solution)/shard_map/while
  152.6 7.3 %copy-start.1 = (bf16[1,512,8,128]{3,2,1,0:T(8,128)(2,1)}, bf16[1,512,8,128]{3,2,1,0:T(8,128)(2,1)S(1)}, u32[]{:S(2)}) copy-start(bf16[1,512,8,128]{3,2,1,0:T(8,128)(2,1)S(1)} %constant_dynamic-slice_fusion.9) | copy-start | bytes 3145732 | tf_op jit(solution)/shard_map/while
  154.6 5.2 %copy-start = (bf16[1,512,8,128]{3,2,1,0:T(8,128)(2,1)}, bf16[1,512,8,128]{3,2,1,0:T(8,128)(2,1)S(1)}, u32[]{:S(2)}) copy-start(bf16[1,512,8,128]{3,2,1,0:T(8,128)(2,1)S(1)} %get-tuple-element.291) | copy-start | bytes 3145732 | tf_op jit(solution)/shard_map/while
  214.7 7.3 %copy-start.1 = (bf16[1,512,8,128]{3,2,1,0:T(8,128)(2,1)}, bf16[1,512,8,128]{3,2,1,0:T(8,128)(2,1)S(1)}, u32[]{:S(2)}) copy-start(bf16[1,512,8,128]{3,2,1,0:T(8,128)(2,1)S(1)} %constant_dynamic-slice_fusion.9) | copy-start | bytes 3145732 | tf_op jit(solution)/shard_map/while
  216.7 5.2 %copy-start = (bf16[1,512,8,128]{3,2,1,0:T(8,128)(2,1)}, bf16[1,512,8,128]{3,2,1,0:T(8,128)(2,1)S(1)}, u32[]{:S(2)}) copy-start(bf16[1,512,8,128]{3,2,1,0:T(8,128)(2,1)S(1)} %get-tuple-element.291) | copy-start | bytes 3145732 | tf_op jit(solution)/shard_map/while
  276.1 88.1 %copy-start.4 = (f32[4,8,128,128]{3,2,1,0:T(8,128)S(1)}, f32[4,8,128,128]{3,2,1,0:T(8,128)}, u32[]{:S(2)}) copy-start(f32[4,8,128,128]{3,2,1,0:T(8,128)} %get-tuple-element.99) | copy-start | bytes 6291460
  277.4 11.4 %collective-permute-start = (f32[8,128,128]{2,1,0:T(8,128)S(1)}, f32[8,128,128]{2,1,0:T(8,128)S(1)}, u32[]{:S(2)}, u32[]{:S(2)}) collective-permute-start(f32[8,128,128]{2,1,0:T(8,128)S(1)} %multiply_add_fusion.2), channel_id=1, source_target_pairs={{0,4},{4,8},{8,12},{12,16},{16,20},{20,24},{24,28},{1,5},{5,9},{9,... | collective-permute-start | bytes 1572872 | tf_op jit(solution)/shard_map/while/body/eval_jaxpr/ppermute | solution.py:14
  290.0 11.4 %collective-permute-start = (f32[8,128,128]{2,1,0:T(8,128)S(1)}, f32[8,128,128]{2,1,0:T(8,128)S(1)}, u32[]{:S(2)}, u32[]{:S(2)}) collective-permute-start(f32[8,128,128]{2,1,0:T(8,128)S(1)} %multiply_add_fusion.2), channel_id=1, source_target_pairs={{0,4},{4,8},{8,12},{12,16},{16,20},{20,24},{24,28},{1,5},{5,9},{9,... | collective-permute-start | bytes 1572872 | tf_op jit(solution)/shard_map/while/body/eval_jaxpr/ppermute | solution.py:14
  302.5 11.4 %collective-permute-start = (f32[8,128,128]{2,1,0:T(8,128)S(1)}, f32[8,128,128]{2,1,0:T(8,128)S(1)}, u32[]{:S(2)}, u32[]{:S(2)}) collective-permute-start(f32[8,128,128]{2,1,0:T(8,128)S(1)} %multiply_add_fusion.2), channel_id=1, source_target_pairs={{0,4},{4,8},{8,12},{12,16},{16,20},{20,24},{24,28},{1,5},{5,9},{9,... | collective-permute-start | bytes 1572872 | tf_op jit(solution)/shard_map/while/body/eval_jaxpr/ppermute | solution.py:14
  315.1 11.4 %collective-permute-start = (f32[8,128,128]{2,1,0:T(8,128)S(1)}, f32[8,128,128]{2,1,0:T(8,128)S(1)}, u32[]{:S(2)}, u32[]{:S(2)}) collective-permute-start(f32[8,128,128]{2,1,0:T(8,128)S(1)} %multiply_add_fusion.2), channel_id=1, source_target_pairs={{0,4},{4,8},{8,12},{12,16},{16,20},{20,24},{24,28},{1,5},{5,9},{9,... | collective-permute-start | bytes 1572872 | tf_op jit(solution)/shard_map/while/body/eval_jaxpr/ppermute | solution.py:14
  327.7 11.4 %collective-permute-start = (f32[8,128,128]{2,1,0:T(8,128)S(1)}, f32[8,128,128]{2,1,0:T(8,128)S(1)}, u32[]{:S(2)}, u32[]{:S(2)}) collective-permute-start(f32[8,128,128]{2,1,0:T(8,128)S(1)} %multiply_add_fusion.2), channel_id=1, source_target_pairs={{0,4},{4,8},{8,12},{12,16},{16,20},{20,24},{24,28},{1,5},{5,9},{9,... | collective-permute-start | bytes 1572872 | tf_op jit(solution)/shard_map/while/body/eval_jaxpr/ppermute | solution.py:14
  340.2 11.4 %collective-permute-start = (f32[8,128,128]{2,1,0:T(8,128)S(1)}, f32[8,128,128]{2,1,0:T(8,128)S(1)}, u32[]{:S(2)}, u32[]{:S(2)}) collective-permute-start(f32[8,128,128]{2,1,0:T(8,128)S(1)} %multiply_add_fusion.2), channel_id=1, source_target_pairs={{0,4},{4,8},{8,12},{12,16},{16,20},{20,24},{24,28},{1,5},{5,9},{9,... | collective-permute-start | bytes 1572872 | tf_op jit(solution)/shard_map/while/body/eval_jaxpr/ppermute | solution.py:14
  352.8 11.4 %collective-permute-start = (f32[8,128,128]{2,1,0:T(8,128)S(1)}, f32[8,128,128]{2,1,0:T(8,128)S(1)}, u32[]{:S(2)}, u32[]{:S(2)}) collective-permute-start(f32[8,128,128]{2,1,0:T(8,128)S(1)} %multiply_add_fusion.2), channel_id=1, source_target_pairs={{0,4},{4,8},{8,12},{12,16},{16,20},{20,24},{24,28},{1,5},{5,9},{9,... | collective-permute-start | bytes 1572872 | tf_op jit(solution)/shard_map/while/body/eval_jaxpr/ppermute | solution.py:14
  365.2 11.0 %copy-start.7 = (f32[8,4,4]{0,1,2:T(4,128)S(1)}, f32[8,4,4]{0,1,2:T(4,128)}, u32[]{:S(2)}) copy-start(f32[8,4,4]{0,1,2:T(4,128)} %copy-done.6) | copy-start | bytes 1540
  365.2 11.1 %copy-start.9 = (f32[8,4]{0,1:T(4,128)S(1)}, f32[8,4]{0,1:T(4,128)}, u32[]{:S(2)}) copy-start(f32[8,4]{0,1:T(4,128)} %copy-done.8) | copy-start | bytes 388
  377.4 24.7 %copy-start.10 = (f32[1024]{0:T(1024)S(1)}, f32[1024]{0:T(1024)}, u32[]{:S(2)}) copy-start(f32[1024]{0:T(1024)} %param.14) | copy-start | bytes 12292
  408.2 6.4 %copy-start.11 = (s32[16]{0:T(128)S(1)}, s32[16]{0:T(128)}, u32[]{:S(2)}) copy-start(s32[16]{0:T(128)} %param.15) | copy-start | bytes 196
Sparse Core Ops, SparseCore 0:
  365.3 36.8 all-gather.1
where the time goes:
time: 433 us; the launch traced here: 428 us
  local copies, waits for them, and re-layouts  231 us (53%)
  waiting for transfers between devices  66.3 us (15%)
  matrix products  65.4 us (15%)
  other arithmetic  24.6 us (6%)
  between operations  14.2 us (3%)
  starting transfers between devices  13.5 us (3%)
  blocking collectives  12.1 us (3%)
    dynamic_update_slice x8, local copies, waits for them, and re-layouts, shards(): lax.scan(local_step, zero_state, (query_blocks, key_blocks, value_blocks,...  178 us
    ppermute x7, waiting for transfers between devices, from_behind(): lax.ppermute(value, axis, [(source, source + steps) for source in range(f...  66.3 us
    dot_general x4, matrix products, block_terms(): jnp.einsum('hts,shd->thd', weights, value_blk, preferred_element_type=jnp...  20.8 us
    unnamed x25, local copies, waits for them, and re-layouts  20.7 us
    dot_general x4, matrix products, block_terms(): jnp.einsum('shd,she->hde', scaled_keys, value_blk, preferred_element_type...  16 us
    dynamic_slice x16, local copies, waits for them, and re-layouts, shards(): lax.scan(local_step, zero_state, (query_blocks, key_blocks, value_blocks,...  14 us
    ppermute x7, starting transfers between devices, from_behind(): lax.ppermute(value, axis, [(source, source + steps) for source in range(f...  13.4 us
    dot_general x1, matrix products, shards(): jnp.einsum('thd,hde->the', queries.reshape(tok_rows, head_count, head_dim...  12.6 us
  transfers between devices with their start and end apart: 8, of which 7 were waited for; matrix products, arithmetic and copies ran while one was open for 9% of the time, Pallas kernels for 0%

commit v1 on v0

v1 whole, which is shorter than its diff:
```python
import functools
import math

import jax
import jax.numpy as jnp
from jax import lax
from jax.experimental import pallas as pl
from jax.experimental.pallas import tpu as pltpu
from jax.sharding import PartitionSpec as P

BLOCK = 512
PAGE = 1024
SLOTS = 5
TILE = 256
LOG2E = math.log2(math.e)
MIB = 1 << 20

NT = (((1,), (1,)), ((), ()))
TN = (((0,), (0,)), ((), ()))


def split3(x):
    high = x.astype(jnp.bfloat16)
    rest = x - high.astype(jnp.float32)
    middle = rest.astype(jnp.bfloat16)
    low = (rest - middle.astype(jnp.float32)).astype(jnp.bfloat16)
    return high, middle, low


def state_kernel(heads, key_ref, value_ref, decay_ref, cum_ref, states_ref, reached_ref, end_ref, mid_ref, state, reached, upper):
    blk = pl.program_id(0)
    count = pl.num_programs(0)
    length, width = key_ref.shape
    dim = width // heads

    @pl.when(blk == 0)
    def _():
        state[...] = jnp.zeros_like(state)
        reached[...] = jnp.zeros_like(reached)
        rows = lax.broadcasted_iota(jnp.int32, (length, length), 0)
        cols = lax.broadcasted_iota(jnp.int32, (length, length), 1)
        upper[...] = jnp.where(rows <= cols, 1.0, 0.0).astype(jnp.bfloat16)

    parts = jnp.concatenate(split3(decay_ref[...] * LOG2E), axis=0)
    sums = jnp.dot(parts, upper[...], preferred_element_type=jnp.float32)
    cum = sums[:heads] + sums[heads : 2 * heads] + sums[2 * heads :]
    cum_ref[...] = cum
    last = cum[:, length - 1 :]
    to_last = jnp.exp2(last - cum).T
    decay = jnp.exp2(jnp.broadcast_to(last, (heads, dim)))
    for pair in range(heads // 2):
        scaled = []
        for head in (2 * pair, 2 * pair + 1):
            keys = key_ref[:, head * dim : (head + 1) * dim].astype(jnp.float32)
            scaled.append((keys * to_last[:, head : head + 1]).astype(jnp.bfloat16))
        update = lax.dot_general(
            jnp.concatenate(scaled, axis=1),
            value_ref[:, 2 * pair * dim : 2 * (pair + 1) * dim],
            TN,
            preferred_element_type=jnp.float32,
        )
        for which, head in enumerate((2 * pair, 2 * pair + 1)):
            rows = slice(head * dim, (head + 1) * dim)
            cols = slice(which * dim, (which + 1) * dim)
            state[rows] = decay[head : head + 1] * state[rows] + update[cols, cols]
    reached[...] += jnp.broadcast_to(last, (heads, dim))
    states_ref[0] = state[...]
    reached_ref[0] = reached[...]
    size = heads * dim

    @pl.when(blk == PAGE // BLOCK - 1)
    def _():
        mid_ref[...] = state[...].astype(jnp.bfloat16)
        end_ref[size + 3 * heads :] = jnp.concatenate(split3(reached[...]), axis=0)

    @pl.when(blk == count - 1)
    def _():
        end_ref[:size] = state[...].astype(jnp.bfloat16)
        end_ref[size : size + 3 * heads] = jnp.concatenate(split3(reached[...]), axis=0)


def run_states(key_rows, value_rows, decay_log):
    tokens, width = key_rows.shape
    heads = decay_log.shape[0]
    dim = width // heads
    blocks = tokens // BLOCK
    size = heads * dim
    return pl.pallas_call(
        functools.partial(state_kernel, heads),
        grid=(blocks,),
        in_specs=[
            pl.BlockSpec((BLOCK, width), lambda b: (b, 0)),
            pl.BlockSpec((BLOCK, width), lambda b: (b, 0)),
            pl.BlockSpec((heads, BLOCK), lambda b: (0, b)),
        ],
        out_specs=[
            pl.BlockSpec((heads, BLOCK), lambda b: (0, b)),
            pl.BlockSpec((1, size, dim), lambda b: (b, 0, 0)),
            pl.BlockSpec((1, heads, dim), lambda b: (b, 0, 0)),
            pl.BlockSpec((size + 6 * heads, dim), lambda b: (0, 0)),
            pl.BlockSpec((size, dim), lambda b: (0, 0)),
        ],
        out_shape=[
            jax.ShapeDtypeStruct((heads, tokens), jnp.float32),
            jax.ShapeDtypeStruct((blocks, size, dim), jnp.float32),
            jax.ShapeDtypeStruct((blocks, heads, dim), jnp.float32),
            jax.ShapeDtypeStruct((size + 6 * heads, dim), jnp.bfloat16),
            jax.ShapeDtypeStruct((size, dim), jnp.bfloat16),
        ],
        scratch_shapes=[
            pltpu.VMEM((size, dim), jnp.float32),
            pltpu.VMEM((heads, dim), jnp.float32),
            pltpu.VMEM((BLOCK, BLOCK), jnp.bfloat16),
        ],
        compiler_params=pltpu.CompilerParams(vmem_limit_bytes=24 * MIB),
        cost_estimate=pl.CostEstimate(flops=4 * tokens * width * dim, bytes_accessed=4 * tokens * width, transcendentals=0),
        name="states",
    )(key_rows, value_rows, decay_log)


def inner_kernel(heads, query_ref, key_ref, value_ref, cum_ref, out_ref):
    length, width = query_ref.shape
    dim = width // heads
    cum = cum_ref[...]
    cum_cols = cum.T
    causal = lax.broadcasted_iota(jnp.int32, (TILE, TILE), 0) >= lax.broadcasted_iota(jnp.int32, (TILE, TILE), 1)
    for head in range(heads):
        lanes = slice(head * dim, (head + 1) * dim)
        for tile in range(length // TILE):
            start, stop = tile * TILE, (tile + 1) * TILE
            scores = lax.dot_general(
                query_ref[start:stop, lanes], key_ref[:stop, lanes], NT, preferred_element_type=jnp.float32
            )
            damping = jnp.exp2(cum_cols[start:stop, head : head + 1] - cum[head : head + 1, :stop])
            weights = scores * damping
            diagonal = jnp.where(causal, weights[:, start:], 0.0)
            if tile:
                weights = jnp.concatenate([weights[:, :start], diagonal], axis=1)
            else:
                weights = diagonal
            out_ref[start:stop, lanes] = jnp.dot(
                weights.astype(jnp.bfloat16), value_ref[:stop, lanes], preferred_element_type=jnp.float32
            )


def run_inner(queries, key_rows, value_rows, cumulative):
    tokens, width = queries.shape
    heads = cumulative.shape[0]
    rows = pl.BlockSpec((BLOCK, width), lambda b: (b, 0))
    return pl.pallas_call(
        functools.partial(inner_kernel, heads),
        grid=(tokens // BLOCK,),
        in_specs=[rows, rows, rows, pl.BlockSpec((heads, BLOCK), lambda b: (0, b))],
        out_specs=rows,
        out_shape=jax.ShapeDtypeStruct((tokens, width), jnp.float32),
        compiler_params=pltpu.CompilerParams(vmem_limit_bytes=32 * MIB),
        cost_estimate=pl.CostEstimate(flops=4 * tokens * width * BLOCK, bytes_accessed=10 * tokens * width, transcendentals=0),
        name="inner",
    )(queries, key_rows, value_rows, cumulative)


def read_logs(ends, size, heads):
    whole, first = [], []
    for end in ends:
        parts = end[size:].astype(jnp.float32)
        whole.append(parts[:heads] + parts[heads : 2 * heads] + parts[2 * heads : 3 * heads])
        first.append(parts[3 * heads : 4 * heads] + parts[4 * heads : 5 * heads] + parts[5 * heads :])
    return whole, first


def gather_states(total, ends, places, logs, place, extra, heads, dim):
    for source, end in enumerate(ends):

        @pl.when(places[source] < place)
        def _():
            log = extra
            for other, other_log in enumerate(logs):
                between = (places[other] > places[source]) & (places[other] < place)
                log = log + jnp.where(between, other_log, 0.0)
            factor = jnp.exp2(log)
            for head in range(heads):
                rows = slice(head * dim, (head + 1) * dim)
                total[rows] += factor[head : head + 1] * end[rows].astype(jnp.float32)


def finish_kernel(heads, index_ref, inner_ref, query_ref, cum_ref, states_ref, reached_ref, *refs):
    *ends, out_ref, square_ref, entry = refs
    blk = pl.program_id(0)
    length, width = query_ref.shape
    dim = width // heads
    size = heads * dim

    @pl.when(blk == 0)
    def _():
        place = index_ref[0]
        logs, _unused = read_logs(ends, size, heads)
        entry[...] = jnp.zeros_like(entry)
        places = [place ^ offset for offset in range(len(ends))]
        gather_states(entry, ends, places, logs, place, jnp.zeros((heads, dim), jnp.float32), heads, dim)

    started = blk > 0
    until = jnp.where(started, reached_ref[0], 0.0)
    factor = jnp.exp2(until)
    growth = jnp.exp2(cum_ref[...]).T
    squares = jnp.zeros((length, dim), jnp.float32)
    zero = jnp.zeros((dim, dim), jnp.bfloat16)
    for pair in range(heads // 2):
        highs, lows = [], []
        for head in (2 * pair, 2 * pair + 1):
            rows = slice(head * dim, (head + 1) * dim)
            state = factor[head : head + 1] * entry[rows] + jnp.where(started, states_ref[0, rows], 0.0)
            high = state.astype(jnp.bfloat16)
            highs.append(high)
            lows.append((state - high.astype(jnp.float32)).astype(jnp.bfloat16))
        query = query_ref[:, 2 * pair * dim : 2 * (pair + 1) * dim]
        carried = 0.0
        for one, two in (highs, lows):
            both = jnp.concatenate(
                [jnp.concatenate([one, zero], axis=1), jnp.concatenate([zero, two], axis=1)], axis=0
            )
            carried = carried + jnp.dot(query, both, preferred_element_type=jnp.float32)
        for which, head in enumerate((2 * pair, 2 * pair + 1)):
            lanes = slice(head * dim, (head + 1) * dim)
            out = inner_ref[:, lanes] + carried[:, which * dim : (which + 1) * dim] * growth[:, head : head + 1]
            out_ref[:, lanes] = out
            squares += out * out
    high = squares.astype(jnp.bfloat16)
    low = (squares - high.astype(jnp.float32)).astype(jnp.bfloat16)
    ones = jnp.ones((8, dim), jnp.bfloat16)
    sums = lax.dot_general(ones, high, NT, preferred_element_type=jnp.float32)
    sums = sums + lax.dot_general(ones, low, NT, preferred_element_type=jnp.float32)
    square_ref[0] = sums


def run_finish(index, inner, queries, cumulative, states, reached, ends):
    tokens, width = queries.shape
    heads = cumulative.shape[0]
    dim = width // heads
    size = heads * dim
    blocks = tokens // BLOCK
    rows = pl.BlockSpec((BLOCK, width), lambda b: (b, 0))
    before = lambda b: (jnp.maximum(b, 1) - 1, 0, 0)
    return pl.pallas_call(
        functools.partial(finish_kernel, heads),
        grid=(blocks,),
        in_specs=[
            pl.BlockSpec(memory_space=pltpu.SMEM),
            rows,
            rows,
            pl.BlockSpec((heads, BLOCK), lambda b: (0, b)),
            pl.BlockSpec((1, size, dim), before),
            pl.BlockSpec((1, heads, dim), before),
        ]
        + [pl.BlockSpec(end.shape, lambda b: (0, 0)) for end in ends],
        out_specs=[rows, pl.BlockSpec((1, 8, BLOCK), lambda b: (b, 0, 0))],
        out_shape=[
            jax.ShapeDtypeStruct((tokens, width), jnp.float32),
            jax.ShapeDtypeStruct((blocks, 8, BLOCK), jnp.float32),
        ],
        input_output_aliases={1: 0},
        scratch_shapes=[pltpu.VMEM((size, dim), jnp.float32)],
        compiler_params=pltpu.CompilerParams(vmem_limit_bytes=40 * MIB),
        cost_estimate=pl.CostEstimate(flops=4 * tokens * width * dim, bytes_accessed=10 * tokens * width, transcendentals=0),
        name="finish",
    )(index, inner, queries, cumulative, states, reached, *ends)


def scale_kernel(whole_width, out_ref, gain_ref, *refs):
    *squares, attended_ref = refs
    total = squares[0][0]
    for square in squares[1:]:
        total = total + square[0]
    scale = lax.rsqrt(total * (1.0 / whole_width) + 1e-06).T[:, :1]
    attended_ref[...] = (out_ref[...] * scale * gain_ref[...]).astype(jnp.bfloat16)


def run_scale(out, gain, squares, whole_width):
    tokens, width = out.shape
    rows = pl.BlockSpec((BLOCK, width), lambda b: (b, 0))
    return pl.pallas_call(
        functools.partial(scale_kernel, whole_width),
        grid=(tokens // BLOCK,),
        in_specs=[rows, pl.BlockSpec((1, width), lambda b: (0, 0))]
        + [pl.BlockSpec((1, 8, BLOCK), lambda b: (b, 0, 0)) for _ in squares],
        out_specs=rows,
        out_shape=jax.ShapeDtypeStruct((tokens, width), jnp.bfloat16),
        compiler_params=pltpu.CompilerParams(vmem_limit_bytes=24 * MIB),
        cost_estimate=pl.CostEstimate(flops=tokens * width, bytes_accessed=6 * tokens * width, transcendentals=0),
        name="scale",
    )(out, gain.reshape(1, width), *squares)


def cache_kernel(heads, count, index_ref, owner_ref, *refs):
    ends, mids = refs[:count], refs[count : 2 * count]
    cache_ref, total, logs_ref, first_ref, page_of = refs[2 * count :]
    size, dim = mids[0].shape
    place = index_ref[0]
    places = [place ^ offset for offset in range(count)]
    whole, first = read_logs(ends, size, heads)
    for source in range(count):
        logs_ref[source] = whole[source]
        first_ref[source] = first[source]
    for slot in range(SLOTS):
        page_of[slot] = -1

    def look(page, found):
        mine = owner_ref[page] == place

        @pl.when(mine)
        def _():
            page_of[found] = page

        return found + mine.astype(jnp.int32)

    lax.fori_loop(0, owner_ref.shape[0], look, jnp.int32(0))

    def fill(slot, carry):
        page = page_of[slot]
        total[...] = jnp.zeros_like(total)

        @pl.when(page >= 0)
        def _():
            at_end = page % 2 == 1
            until = page // 2 + page % 2
            logs = [logs_ref[source] for source in range(count)]
            extra = jnp.zeros((heads, dim), jnp.float32)
            for source in range(count):
                extra = extra + jnp.where((places[source] == until) & jnp.logical_not(at_end), first_ref[source], 0.0)
            gather_states(total, ends, places, logs, until, extra, heads, dim)
            for source in range(count):

                @pl.when((places[source] == until) & jnp.logical_not(at_end))
                def _():
                    total[...] += mids[source][...].astype(jnp.float32)

        cache_ref[slot] = total[...].astype(jnp.bfloat16)
        return carry

    lax.fori_loop(0, SLOTS, fill, 0)


def run_cache(index, page_owner, ends, mids, heads):
    size, dim = mids[0].shape
    count = len(ends)
    vmem = pl.BlockSpec(memory_space=pltpu.VMEM)
    smem = pl.BlockSpec(memory_space=pltpu.SMEM)
    return pl.pallas_call(
        functools.partial(cache_kernel, heads, count),
        in_specs=[smem, smem] + [vmem] * (2 * count),
        out_specs=vmem,
        out_shape=jax.ShapeDtypeStruct((SLOTS, size, dim), jnp.bfloat16),
        scratch_shapes=[
            pltpu.VMEM((size, dim), jnp.float32),
            pltpu.VMEM((count, heads, dim), jnp.float32),
            pltpu.VMEM((count, heads, dim), jnp.float32),
            pltpu.SMEM((SLOTS,), jnp.int32),
        ],
        compiler_params=pltpu.CompilerParams(vmem_limit_bytes=32 * MIB),
        cost_estimate=pl.CostEstimate(flops=20 * size * dim, bytes_accessed=20 * size * dim, transcendentals=0),
        name="cache",
    )(index, page_owner, *ends, *mids)


def swap(value, axis, offset):
    return lax.ppermute(value, axis, [(place, place ^ offset) for place in range(lax.axis_size(axis))])


def everyones(value, axis):
    count = lax.axis_size(axis)
    held = {0: value}
    for offset in range(2, count, 2):
        held[offset] = swap(value, axis, offset)
    for offset in range(0, count, 2):
        held[offset + 1] = swap(held[offset], axis, 1)
    return [held[offset] for offset in range(count)]


def shards(queries, key_rows, value_rows, decay_log, norm_gain, page_owner):
    heads = decay_log.shape[0]
    dim = queries.shape[1] // heads
    index = lax.axis_index("seq").astype(jnp.int32).reshape(1)
    cumulative, states, reached, end, mid = run_states(key_rows, value_rows, decay_log)
    ends = everyones(end, "seq")
    inner = run_inner(queries, key_rows, value_rows, cumulative)
    out, square = run_finish(index, inner, queries, cumulative, states, reached, ends)
    squares = [square] + [swap(square, "head", offset) for offset in range(1, lax.axis_size("head"))]
    mid, _ = lax.optimization_barrier((mid, ends[-1]))
    mids = everyones(mid, "seq")
    attended = run_scale(out, norm_gain, squares, queries.shape[1] * lax.axis_size("head"))
    page_cache = run_cache(index, page_owner, ends, mids, heads)
    return attended, page_cache.reshape(SLOTS, heads, dim, dim)


def solution(mesh):
    return jax.shard_map(
        shards,
        mesh=mesh,
        in_specs=(
            P("seq", "head"),
            P("seq", "head"),
            P("seq", "head"),
            P("head", "seq"),
            P("head"),
            P(),
        ),
        out_specs=(P("seq", "head"), P("seq", "head", None, None)),
        check_vma=False,
    )
```

time: 433 us -> 90.5 us (0.21)
  the two profiles are of different devices: /device:TPU:4 before, /device:TPU:0 now
where the time goes in v1:
time: 90.5 us; the launch traced here: 89.8 us
  Pallas kernels  32.3 us (36%)
  waiting for transfers between devices  19.2 us (21%)
  local copies, waits for them, and re-layouts  19.1 us (21%)
  starting transfers between devices  18.5 us (20%)
    ppermute x17, waiting for transfers between devices, swap(): lax.ppermute(value, axis, [(place, place ^ offset) for place in range(lax...  19.2 us
    unnamed x26, local copies, waits for them, and re-layouts  19.1 us
    ppermute x17, starting transfers between devices, swap(): lax.ppermute(value, axis, [(place, place ^ offset) for place in range(lax...  18.5 us
    pallas_call x1, Pallas kernels, run_inner(): pl.pallas_call(functools.partial(inner_kernel, heads), grid=(tokens // BL...  10.8 us
    pallas_call x1, Pallas kernels, run_finish(): pl.pallas_call(functools.partial(finish_kernel, heads), grid=(blocks,), i...  9.04 us
    pallas_call x1, Pallas kernels, run_states(): pl.pallas_call(functools.partial(state_kernel, heads), grid=(blocks,), in...  6.4 us
    pallas_call x1, Pallas kernels, run_scale(): pl.pallas_call(functools.partial(scale_kernel, whole_width), grid=(tokens...  3.05 us
    pallas_call x1, Pallas kernels, run_cache(): pl.pallas_call(functools.partial(cache_kernel, heads, count), in_specs=[s...  3.01 us
  transfers between devices with their start and end apart: 17, of which 5 were waited for; matrix products, arithmetic and copies ran while one was open for 0% of the time, Pallas kernels for 25%

profile of v1, /device:TPU:0, one launch (start us, length us, event | category | flops | bytes accessed | tf_op | source)
XLA Modules:
  0.0 89.8 jit_solution(5593220935685691796)
XLA Ops:
  0.6 0.0 copy-start.2
  0.6 2.2 %copy-done.2 = bf16[2048,1024]{1,0:T(8,128)(2,1)S(1)} copy-done((bf16[2048,1024]{1,0:T(8,128)(2,1)S(1)}, bf16[2048,1024]{1,0:T(8,128)(2,1)}, u32[]{:S(2)}) %copy-start.2) | copy-done | bytes 4194328
  2.8 2.2 %copy-done.4 = bf16[2048,1024]{1,0:T(8,128)(2,1)S(1)} copy-done((bf16[2048,1024]{1,0:T(8,128)(2,1)S(1)}, bf16[2048,1024]{1,0:T(8,128)(2,1)}, u32[]{:S(2)}) %copy-start.4) | copy-done | bytes 4194328
  5.0 0.8 copy-done.10
  5.8 6.4 %states.1 = (f32[8,2048]{1,0:T(8,128)S(1)}, f32[4,1024,128]{2,1,0:T(8,128)S(1)}, f32[4,8,128]{2,1,0:T(8,128)S(1)}, bf16[1072,128]{1,0:T(8,128)(2,1)S(1)}, bf16[1024,128]{1,0:T(8,128)(2,1)S(1)}) custom-call(bf16[2048,1024]{1,0:T(8,128)(2,1)S(1)} %copy-done.2, bf16[2048,1024]{1,0:T(8,128)(2,1)S(1)} %copy-done.4, f32[8,2048]{1,0:T(8,128)S(1)} %copy-done.10), custom_call_target="tpu_custom_call" | custom-call | flops 1073741824 | bytes 8388608 | tf_op jit(solution)/shard_map/states/pallas_call | solution.py:88
  12.3 0.0 copy-start.8
  12.3 0.7 copy-done.8
  13.0 3.9 %collective-permute-start.5 = (bf16[1072,128]{1,0:T(8,128)(2,1)S(1)}, bf16[1072,128]{1,0:T(8,128)(2,1)S(1)}, u32[]{:S(2)}, u32[]{:S(2)}) collective-permute-start(bf16[1072,128]{1,0:T(8,128)(2,1)S(1)} %get-tuple-element.13.refs_0_), channel_id=1, source_target_pairs={{0,24},{4,28},{8,16},{12,20},{16,8},{20,12},{24,0},{28,4},{1,25},{... | collective-permute-start | bytes 823304 | tf_op jit(solution)/shard_map/ppermute | solution.py:365
  16.9 0.5 collective-permute-start.1
  17.4 0.0 collective-permute-start.3
  17.4 6.9 %collective-permute-done.5.refs_6_ = bf16[1072,128]{1,0:T(8,128)(2,1)S(1)} collective-permute-done((bf16[1072,128]{1,0:T(8,128)(2,1)S(1)}, bf16[1072,128]{1,0:T(8,128)(2,1)S(1)}, u32[]{:S(2)}, u32[]{:S(2)}) %collective-permute-start.5) | collective-permute-done | bytes 274464 | tf_op jit(solution)/shard_map/ppermute | solution.py:365
  24.3 0.0 collective-permute-start.6
  24.3 0.5 collective-permute-start
  24.8 4.8 %collective-permute-done.1.refs_2_ = bf16[1072,128]{1,0:T(8,128)(2,1)S(1)} collective-permute-done((bf16[1072,128]{1,0:T(8,128)(2,1)S(1)}, bf16[1072,128]{1,0:T(8,128)(2,1)S(1)}, u32[]{:S(2)}, u32[]{:S(2)}) %collective-permute-start.1) | collective-permute-done | bytes 274464 | tf_op jit(solution)/shard_map/ppermute | solution.py:365
  29.6 0.0 collective-permute-start.2
  29.6 0.0 collective-permute-done.3.refs_4_
  29.6 0.5 collective-permute-start.4
  30.1 0.0 collective-permute-done.6.refs_7_
  30.1 1.5 %collective-permute-start.11 = (bf16[1024,128]{1,0:T(8,128)(2,1)}, bf16[1024,128]{1,0:T(8,128)(2,1)S(1)}, u32[]{:S(2)}, u32[]{:S(2)}) collective-permute-start(bf16[1024,128]{1,0:T(8,128)(2,1)} %copy-done.8), channel_id=1, source_target_pairs={{0,8},{4,12},{8,0},{12,4},{16,24},{20,28},{24,16},{28,20},{1,9},{5... | collective-permute-start | bytes 786440 | tf_op jit(solution)/shard_map/ppermute | solution.py:365
  31.6 0.9 %collective-permute-start.13 = (bf16[1024,128]{1,0:T(8,128)(2,1)}, bf16[1024,128]{1,0:T(8,128)(2,1)S(1)}, u32[]{:S(2)}, u32[]{:S(2)}) collective-permute-start(bf16[1024,128]{1,0:T(8,128)(2,1)} %copy-done.8), channel_id=1, source_target_pairs={{0,16},{4,20},{8,24},{12,28},{16,0},{20,4},{24,8},{28,12},{1,17},{... | collective-permute-start | bytes 786440 | tf_op jit(solution)/shard_map/ppermute | solution.py:365
  32.5 0.0 collective-permute-done.refs_1_
  32.5 1.1 %collective-permute-start.15 = (bf16[1024,128]{1,0:T(8,128)(2,1)}, bf16[1024,128]{1,0:T(8,128)(2,1)S(1)}, u32[]{:S(2)}, u32[]{:S(2)}) collective-permute-start(bf16[1024,128]{1,0:T(8,128)(2,1)} %copy-done.8), channel_id=1, source_target_pairs={{0,24},{4,28},{8,16},{12,20},{16,8},{20,12},{24,0},{28,4},{1,25},{... | collective-permute-start | bytes 786440 | tf_op jit(solution)/shard_map/ppermute | solution.py:365
  33.6 2.2 %copy-done.3 = bf16[2048,1024]{1,0:T(8,128)(2,1)S(1)} copy-done((bf16[2048,1024]{1,0:T(8,128)(2,1)S(1)}, bf16[2048,1024]{1,0:T(8,128)(2,1)}, u32[]{:S(2)}) %copy-start.3) | copy-done | bytes 4194328
  35.8 2.2 %copy-done.5 = bf16[2048,1024]{1,0:T(8,128)(2,1)S(1)} copy-done((bf16[2048,1024]{1,0:T(8,128)(2,1)S(1)}, bf16[2048,1024]{1,0:T(8,128)(2,1)}, u32[]{:S(2)}) %copy-start.5) | copy-done | bytes 4194328
  38.0 2.2 %copy-done.6 = bf16[2048,1024]{1,0:T(8,128)(2,1)S(1)} copy-done((bf16[2048,1024]{1,0:T(8,128)(2,1)S(1)}, bf16[2048,1024]{1,0:T(8,128)(2,1)}, u32[]{:S(2)}) %copy-start.6) | copy-done | bytes 4194328
  40.2 10.8 %inner.1.inner_ref = f32[2048,1024]{1,0:T(8,128)S(1)} custom-call(bf16[2048,1024]{1,0:T(8,128)(2,1)S(1)} %copy-done.6, bf16[2048,1024]{1,0:T(8,128)(2,1)S(1)} %copy-done.3, bf16[2048,1024]{1,0:T(8,128)(2,1)S(1)} %copy-done.5, f32[8,2048]{1,0:T(8,128)S(1)} %get-tuple-element.10.cum_ref), custom_call_target="tpu_custom_call" | custom-call | flops 4294967296 | bytes 20971520 | tf_op jit(solution)/shard_map/inner/pallas_call | solution.py:150
  51.0 3.3 %copy-done = f32[2048,1024]{1,0:T(8,128)} copy-done((f32[2048,1024]{1,0:T(8,128)}, f32[2048,1024]{1,0:T(8,128)S(1)}, u32[]{:S(2)}) %copy-start) | copy-done | bytes 8388632
  54.2 0.0 collective-permute-done.2.refs_3_
  54.2 0.0 collective-permute-done.11.refs_10_
  54.3 0.5 collective-permute-start.12
  54.8 0.0 collective-permute-done.13.refs_12_
  54.8 0.1 collective-permute-start.14
  54.8 0.4 collective-permute-start.16
  55.3 0.0 collective-permute-done.4.refs_5_
  55.3 9.0 %finish.1 = (f32[2048,1024]{1,0:T(8,128)}, f32[4,8,512]{2,1,0:T(8,128)S(1)}) custom-call(s32[1]{0:T(128)} %bitcast.index_ref, f32[2048,1024]{1,0:T(8,128)} %copy-done, bf16[2048,1024]{1,0:T(8,128)(2,1)S(1)} %copy-done.7, f32[8,2048]{1,0:T(8,128)S(1)} %get-tuple-element.10.cum_ref, ...), custom_call_target="tpu_custom_call", output_to_operand_aliasing={{0}: (1, {})} | custom-call | flops 1073741824 | bytes 20971520 | tf_op jit(solution)/shard_map/finish/pallas_call | solution.py:243
  64.3 1.6 %collective-permute-start.7 = (f32[4,8,512]{2,1,0:T(8,128)S(1)}, f32[4,8,512]{2,1,0:T(8,128)S(1)}, u32[]{:S(2)}, u32[]{:S(2)}) collective-permute-start(f32[4,8,512]{2,1,0:T(8,128)S(1)} %get-tuple-element.15.refs_0_), channel_id=1, source_target_pairs={{0,1},{1,0},{2,3},{3,2},{4,5},{5,4},{6,7},{7,6},{8,9},{9,8},{10,11... | collective-permute-start | bytes 196616 | tf_op jit(solution)/shard_map/ppermute | solution.py:365
  65.9 2.7 %collective-permute-done.7.refs_1_ = f32[4,8,512]{2,1,0:T(8,128)S(1)} collective-permute-done((f32[4,8,512]{2,1,0:T(8,128)S(1)}, f32[4,8,512]{2,1,0:T(8,128)S(1)}, u32[]{:S(2)}, u32[]{:S(2)}) %collective-permute-start.7) | collective-permute-done | bytes 65568 | tf_op jit(solution)/shard_map/ppermute | solution.py:365
  68.6 2.6 %collective-permute-start.8 = (f32[4,8,512]{2,1,0:T(8,128)S(1)}, f32[4,8,512]{2,1,0:T(8,128)S(1)}, u32[]{:S(2)}, u32[]{:S(2)}) collective-permute-start(f32[4,8,512]{2,1,0:T(8,128)S(1)} %get-tuple-element.15.refs_0_), channel_id=1, source_target_pairs={{0,2},{1,3},{2,0},{3,1},{4,6},{5,7},{6,4},{7,5},{8,10},{9,11},{10,... | collective-permute-start | bytes 196616 | tf_op jit(solution)/shard_map/ppermute | solution.py:365
  71.2 2.6 %collective-permute-done.8.refs_2_ = f32[4,8,512]{2,1,0:T(8,128)S(1)} collective-permute-done((f32[4,8,512]{2,1,0:T(8,128)S(1)}, f32[4,8,512]{2,1,0:T(8,128)S(1)}, u32[]{:S(2)}, u32[]{:S(2)}) %collective-permute-start.8) | collective-permute-done | bytes 65568 | tf_op jit(solution)/shard_map/ppermute | solution.py:365
  73.7 4.4 %collective-permute-start.9 = (f32[4,8,512]{2,1,0:T(8,128)S(1)}, f32[4,8,512]{2,1,0:T(8,128)S(1)}, u32[]{:S(2)}, u32[]{:S(2)}) collective-permute-start(f32[4,8,512]{2,1,0:T(8,128)S(1)} %get-tuple-element.15.refs_0_), channel_id=1, source_target_pairs={{0,3},{1,2},{2,1},{3,0},{4,7},{5,6},{6,5},{7,4},{8,11},{9,10},{10,... | collective-permute-start | bytes 196616 | tf_op jit(solution)/shard_map/ppermute | solution.py:365
  78.1 2.2 %collective-permute-done.9.refs_3_ = f32[4,8,512]{2,1,0:T(8,128)S(1)} collective-permute-done((f32[4,8,512]{2,1,0:T(8,128)S(1)}, f32[4,8,512]{2,1,0:T(8,128)S(1)}, u32[]{:S(2)}, u32[]{:S(2)}) %collective-permute-start.9) | collective-permute-done | bytes 65568 | tf_op jit(solution)/shard_map/ppermute | solution.py:365
  80.4 3.4 %copy-done.1 = f32[2048,1024]{1,0:T(8,128)S(1)} copy-done((f32[2048,1024]{1,0:T(8,128)S(1)}, f32[2048,1024]{1,0:T(8,128)}, u32[]{:S(2)}) %copy-start.1) | copy-done | bytes 8388632
  83.8 3.1 %scale.1 = bf16[2048,1024]{1,0:T(8,128)(2,1)} custom-call(f32[2048,1024]{1,0:T(8,128)S(1)} %copy-done.1, f32[1,1024]{1,0:T(1,128)S(1)} %bitcast.3, f32[4,8,512]{2,1,0:T(8,128)S(1)} %get-tuple-element.15.refs_0_, f32[4,8,512]{2,1,0:T(8,128)S(1)} %collective-permute-done.7.refs_1_, f32[4,8,512]{2,1,0:T(8,128)S(1)} %collective-permute-done.8.refs_2_, ...), custom_call_target="tpu_custom_call" | custom-call | flops 2097152 | bytes 12582912 | tf_op jit(solution)/shard_map/scale/pallas_call | solution.py:280
  86.8 0.0 collective-permute-done.10.refs_9_
  86.8 0.0 collective-permute-done.12.refs_11_
  86.8 0.0 collective-permute-done.14.refs_13_
  86.8 0.0 collective-permute-done.16.refs_15_
  86.8 3.0 %cache.1 = bf16[5,1024,128]{2,1,0:T(8,128)(2,1)} custom-call(s32[1]{0:T(128)} %bitcast.index_ref, s32[16]{0:T(128)S(1)} %copy-done.12, bf16[1072,128]{1,0:T(8,128)(2,1)S(1)} %get-tuple-element.13.refs_0_, bf16[1072,128]{1,0:T(8,128)(2,1)} %collective-permute-done.refs_1_, bf16[1072,128]{1,0:T(8,128)(2,1)S(1)} %collective-permute-done.1.refs_2_, ...), custom_call_target="tpu_custom_call" | custom-call | flops 2621440 | bytes 2621440 | tf_op jit(solution)/shard_map/cache/pallas_call | solution.py:347
  (17 shorter events, 0.0 us)
Async XLA Ops:
  0.6 2.2 %copy-start.2 = (bf16[2048,1024]{1,0:T(8,128)(2,1)S(1)}, bf16[2048,1024]{1,0:T(8,128)(2,1)}, u32[]{:S(2)}) copy-start(bf16[2048,1024]{1,0:T(8,128)(2,1)} %key_ref.3) | copy-start | bytes 12582916
  2.8 2.2 %copy-start.4 = (bf16[2048,1024]{1,0:T(8,128)(2,1)S(1)}, bf16[2048,1024]{1,0:T(8,128)(2,1)}, u32[]{:S(2)}) copy-start(bf16[2048,1024]{1,0:T(8,128)(2,1)} %value_ref.3) | copy-start | bytes 12582916
  5.0 0.8 copy-start.10
  12.3 0.7 copy-start.8
  13.0 11.3 %collective-permute-start.5 = (bf16[1072,128]{1,0:T(8,128)(2,1)S(1)}, bf16[1072,128]{1,0:T(8,128)(2,1)S(1)}, u32[]{:S(2)}, u32[]{:S(2)}) collective-permute-start(bf16[1072,128]{1,0:T(8,128)(2,1)S(1)} %get-tuple-element.13.refs_0_), channel_id=1, source_target_pairs={{0,24},{4,28},{8,16},{12,20},{16,8},{20,12},{24,0},{28,4},{1,25},{... | collective-permute-start | bytes 823304 | tf_op jit(solution)/shard_map/ppermute | solution.py:365
  16.9 12.7 %collective-permute-start.1 = (bf16[1072,128]{1,0:T(8,128)(2,1)S(1)}, bf16[1072,128]{1,0:T(8,128)(2,1)S(1)}, u32[]{:S(2)}, u32[]{:S(2)}) collective-permute-start(bf16[1072,128]{1,0:T(8,128)(2,1)S(1)} %get-tuple-element.13.refs_0_), channel_id=1, source_target_pairs={{0,8},{4,12},{8,0},{12,4},{16,24},{20,28},{24,16},{28,20},{1,9},{5... | collective-permute-start | bytes 823304 | tf_op jit(solution)/shard_map/ppermute | solution.py:365
  17.4 12.2 %collective-permute-start.3 = (bf16[1072,128]{1,0:T(8,128)(2,1)S(1)}, bf16[1072,128]{1,0:T(8,128)(2,1)S(1)}, u32[]{:S(2)}, u32[]{:S(2)}) collective-permute-start(bf16[1072,128]{1,0:T(8,128)(2,1)S(1)} %get-tuple-element.13.refs_0_), channel_id=1, source_target_pairs={{0,16},{4,20},{8,24},{12,28},{16,0},{20,4},{24,8},{28,12},{1,17},{... | collective-permute-start | bytes 823304 | tf_op jit(solution)/shard_map/ppermute | solution.py:365
  24.3 5.8 %collective-permute-start.6 = (bf16[1072,128]{1,0:T(8,128)(2,1)S(1)}, bf16[1072,128]{1,0:T(8,128)(2,1)S(1)}, u32[]{:S(2)}, u32[]{:S(2)}) collective-permute-start(bf16[1072,128]{1,0:T(8,128)(2,1)S(1)} %collective-permute-done.5.refs_6_), channel_id=1, source_target_pairs={{0,4},{4,0},{8,12},{12,8},{16,20},{20,16},{24,28},{28,24},{1,5},{5... | collective-permute-start | bytes 823304 | tf_op jit(solution)/shard_map/ppermute | solution.py:365
  24.3 8.2 %collective-permute-start = (bf16[1072,128]{1,0:T(8,128)(2,1)S(1)}, bf16[1072,128]{1,0:T(8,128)(2,1)}, u32[]{:S(2)}, u32[]{:S(2)}) collective-permute-start(bf16[1072,128]{1,0:T(8,128)(2,1)S(1)} %get-tuple-element.13.refs_0_), channel_id=1, source_target_pairs={{0,4},{4,0},{8,12},{12,8},{16,20},{20,16},{24,28},{28,24},{1,5},{5... | collective-permute-start | bytes 823304 | tf_op jit(solution)/shard_map/ppermute | solution.py:365
  29.6 24.6 %collective-permute-start.2 = (bf16[1072,128]{1,0:T(8,128)(2,1)S(1)}, bf16[1072,128]{1,0:T(8,128)(2,1)S(1)}, u32[]{:S(2)}, u32[]{:S(2)}) collective-permute-start(bf16[1072,128]{1,0:T(8,128)(2,1)S(1)} %collective-permute-done.1.refs_2_), channel_id=1, source_target_pairs={{0,4},{4,0},{8,12},{12,8},{16,20},{20,16},{24,28},{28,24},{1,5},{5... | collective-permute-start | bytes 823304 | tf_op jit(solution)/shard_map/ppermute | solution.py:365
  29.6 25.7 %collective-permute-start.4 = (bf16[1072,128]{1,0:T(8,128)(2,1)S(1)}, bf16[1072,128]{1,0:T(8,128)(2,1)S(1)}, u32[]{:S(2)}, u32[]{:S(2)}) collective-permute-start(bf16[1072,128]{1,0:T(8,128)(2,1)S(1)} %collective-permute-done.3.refs_4_), channel_id=1, source_target_pairs={{0,4},{4,0},{8,12},{12,8},{16,20},{20,16},{24,28},{28,24},{1,5},{5... | collective-permute-start | bytes 823304 | tf_op jit(solution)/shard_map/ppermute | solution.py:365
  30.1 24.1 %collective-permute-start.11 = (bf16[1024,128]{1,0:T(8,128)(2,1)}, bf16[1024,128]{1,0:T(8,128)(2,1)S(1)}, u32[]{:S(2)}, u32[]{:S(2)}) collective-permute-start(bf16[1024,128]{1,0:T(8,128)(2,1)} %copy-done.8), channel_id=1, source_target_pairs={{0,8},{4,12},{8,0},{12,4},{16,24},{20,28},{24,16},{28,20},{1,9},{5... | collective-permute-start | bytes 786440 | tf_op jit(solution)/shard_map/ppermute | solution.py:365
  31.6 23.2 %collective-permute-start.13 = (bf16[1024,128]{1,0:T(8,128)(2,1)}, bf16[1024,128]{1,0:T(8,128)(2,1)S(1)}, u32[]{:S(2)}, u32[]{:S(2)}) collective-permute-start(bf16[1024,128]{1,0:T(8,128)(2,1)} %copy-done.8), channel_id=1, source_target_pairs={{0,16},{4,20},{8,24},{12,28},{16,0},{20,4},{24,8},{28,12},{1,17},{... | collective-permute-start | bytes 786440 | tf_op jit(solution)/shard_map/ppermute | solution.py:365
  32.5 22.3 %collective-permute-start.15 = (bf16[1024,128]{1,0:T(8,128)(2,1)}, bf16[1024,128]{1,0:T(8,128)(2,1)S(1)}, u32[]{:S(2)}, u32[]{:S(2)}) collective-permute-start(bf16[1024,128]{1,0:T(8,128)(2,1)} %copy-done.8), channel_id=1, source_target_pairs={{0,24},{4,28},{8,16},{12,20},{16,8},{20,12},{24,0},{28,4},{1,25},{... | collective-permute-start | bytes 786440 | tf_op jit(solution)/shard_map/ppermute | solution.py:365
  33.6 2.2 %copy-start.3 = (bf16[2048,1024]{1,0:T(8,128)(2,1)S(1)}, bf16[2048,1024]{1,0:T(8,128)(2,1)}, u32[]{:S(2)}) copy-start(bf16[2048,1024]{1,0:T(8,128)(2,1)} %key_ref.3) | copy-start | bytes 12582916
  35.8 2.2 %copy-start.5 = (bf16[2048,1024]{1,0:T(8,128)(2,1)S(1)}, bf16[2048,1024]{1,0:T(8,128)(2,1)}, u32[]{:S(2)}) copy-start(bf16[2048,1024]{1,0:T(8,128)(2,1)} %value_ref.3) | copy-start | bytes 12582916
  38.0 2.2 %copy-start.6 = (bf16[2048,1024]{1,0:T(8,128)(2,1)S(1)}, bf16[2048,1024]{1,0:T(8,128)(2,1)}, u32[]{:S(2)}) copy-start(bf16[2048,1024]{1,0:T(8,128)(2,1)} %query_ref.3) | copy-start | bytes 12582916
  40.2 14.1 %copy-start.9 = (bf16[1024,128]{1,0:T(8,128)(2,1)S(1)}, bf16[1024,128]{1,0:T(8,128)(2,1)}, u32[]{:S(2)}) copy-start(bf16[1024,128]{1,0:T(8,128)(2,1)} %copy-done.8) | copy-start | bytes 786436
  40.2 15.1 %copy-start.7 = (bf16[2048,1024]{1,0:T(8,128)(2,1)S(1)}, bf16[2048,1024]{1,0:T(8,128)(2,1)}, u32[]{:S(2)}) copy-start(bf16[2048,1024]{1,0:T(8,128)(2,1)} %query_ref.3) | copy-start | bytes 12582916
  51.0 3.3 %copy-start = (f32[2048,1024]{1,0:T(8,128)}, f32[2048,1024]{1,0:T(8,128)S(1)}, u32[]{:S(2)}) copy-start(f32[2048,1024]{1,0:T(8,128)S(1)} %inner.1.inner_ref) | copy-start | bytes 25165828
  54.2 32.6 %collective-permute-start.10 = (bf16[1024,128]{1,0:T(8,128)(2,1)S(1)}, bf16[1024,128]{1,0:T(8,128)(2,1)S(1)}, u32[]{:S(2)}, u32[]{:S(2)}) collective-permute-start(bf16[1024,128]{1,0:T(8,128)(2,1)S(1)} %copy-done.9), channel_id=1, source_target_pairs={{0,4},{4,0},{8,12},{12,8},{16,20},{20,16},{24,28},{28,24},{1,5},{5... | collective-permute-start | bytes 786440 | tf_op jit(solution)/shard_map/ppermute | solution.py:365
  54.3 32.6 %collective-permute-start.12 = (bf16[1024,128]{1,0:T(8,128)(2,1)S(1)}, bf16[1024,128]{1,0:T(8,128)(2,1)S(1)}, u32[]{:S(2)}, u32[]{:S(2)}) collective-permute-start(bf16[1024,128]{1,0:T(8,128)(2,1)S(1)} %collective-permute-done.11.refs_10_), channel_id=1, source_target_pairs={{0,4},{4,0},{8,12},{12,8},{16,20},{20,16},{24,28},{28,24},{1,5},{5... | collective-permute-start | bytes 786440 | tf_op jit(solution)/shard_map/ppermute | solution.py:365
  54.8 32.1 %collective-permute-start.14 = (bf16[1024,128]{1,0:T(8,128)(2,1)S(1)}, bf16[1024,128]{1,0:T(8,128)(2,1)S(1)}, u32[]{:S(2)}, u32[]{:S(2)}) collective-permute-start(bf16[1024,128]{1,0:T(8,128)(2,1)S(1)} %collective-permute-done.13.refs_12_), channel_id=1, source_target_pairs={{0,4},{4,0},{8,12},{12,8},{16,20},{20,16},{24,28},{28,24},{1,5},{5... | collective-permute-start | bytes 786440 | tf_op jit(solution)/shard_map/ppermute | solution.py:365
  54.8 32.0 %collective-permute-start.16 = (bf16[1024,128]{1,0:T(8,128)(2,1)S(1)}, bf16[1024,128]{1,0:T(8,128)(2,1)S(1)}, u32[]{:S(2)}, u32[]{:S(2)}) collective-permute-start(bf16[1024,128]{1,0:T(8,128)(2,1)S(1)} %collective-permute-done.15.refs_14_), channel_id=1, source_target_pairs={{0,4},{4,0},{8,12},{12,8},{16,20},{20,16},{24,28},{28,24},{1,5},{5... | collective-permute-start | bytes 786440 | tf_op jit(solution)/shard_map/ppermute | solution.py:365
  55.3 25.1 %copy-start.11 = (f32[1024]{0:T(1024)S(1)}, f32[1024]{0:T(1024)}, u32[]{:S(2)}) copy-start(f32[1024]{0:T(1024)} %param.10) | copy-start | bytes 12292
  64.3 4.3 %collective-permute-start.7 = (f32[4,8,512]{2,1,0:T(8,128)S(1)}, f32[4,8,512]{2,1,0:T(8,128)S(1)}, u32[]{:S(2)}, u32[]{:S(2)}) collective-permute-start(f32[4,8,512]{2,1,0:T(8,128)S(1)} %get-tuple-element.15.refs_0_), channel_id=1, source_target_pairs={{0,1},{1,0},{2,3},{3,2},{4,5},{5,4},{6,7},{7,6},{8,9},{9,8},{10,11... | collective-permute-start | bytes 196616 | tf_op jit(solution)/shard_map/ppermute | solution.py:365
  68.6 5.2 %collective-permute-start.8 = (f32[4,8,512]{2,1,0:T(8,128)S(1)}, f32[4,8,512]{2,1,0:T(8,128)S(1)}, u32[]{:S(2)}, u32[]{:S(2)}) collective-permute-start(f32[4,8,512]{2,1,0:T(8,128)S(1)} %get-tuple-element.15.refs_0_), channel_id=1, source_target_pairs={{0,2},{1,3},{2,0},{3,1},{4,6},{5,7},{6,4},{7,5},{8,10},{9,11},{10,... | collective-permute-start | bytes 196616 | tf_op jit(solution)/shard_map/ppermute | solution.py:365
  73.7 6.6 %collective-permute-start.9 = (f32[4,8,512]{2,1,0:T(8,128)S(1)}, f32[4,8,512]{2,1,0:T(8,128)S(1)}, u32[]{:S(2)}, u32[]{:S(2)}) collective-permute-start(f32[4,8,512]{2,1,0:T(8,128)S(1)} %get-tuple-element.15.refs_0_), channel_id=1, source_target_pairs={{0,3},{1,2},{2,1},{3,0},{4,7},{5,6},{6,5},{7,4},{8,11},{9,10},{10,... | collective-permute-start | bytes 196616 | tf_op jit(solution)/shard_map/ppermute | solution.py:365
  80.4 3.4 %copy-start.1 = (f32[2048,1024]{1,0:T(8,128)S(1)}, f32[2048,1024]{1,0:T(8,128)}, u32[]{:S(2)}) copy-start(f32[2048,1024]{1,0:T(8,128)} %get-tuple-element.14.out_ref) | copy-start | bytes 25165828
  83.8 3.1 %copy-start.12 = (s32[16]{0:T(128)S(1)}, s32[16]{0:T(128)}, u32[]{:S(2)}) copy-start(s32[16]{0:T(128)} %owner_ref.1) | copy-start | bytes 196

commit v2 on v1

v2 whole, which is shorter than its diff:
```python
import functools
import math

import jax
import jax.numpy as jnp
from jax import lax
from jax.experimental import pallas as pl
from jax.experimental.pallas import tpu as pltpu
from jax.sharding import PartitionSpec as P

BLOCK = 512
PAGE = 1024
SLOTS = 5
TILE = 256
LOG2E = math.log2(math.e)
MIB = 1 << 20

NT = (((1,), (1,)), ((), ()))
TN = (((0,), (0,)), ((), ()))


def split3(x):
    high = x.astype(jnp.bfloat16)
    rest = x - high.astype(jnp.float32)
    middle = rest.astype(jnp.bfloat16)
    low = (rest - middle.astype(jnp.float32)).astype(jnp.bfloat16)
    return high, middle, low


def state_kernel(heads, key_ref, value_ref, decay_ref, cum_ref, states_ref, reached_ref, end_ref, mid_ref, reached, upper):
    blk = pl.program_id(0)
    count = pl.num_programs(0)
    length, width = key_ref.shape
    dim = width // heads
    size = heads * dim

    @pl.when(blk == 0)
    def _():
        reached[...] = jnp.zeros_like(reached)
        states_ref[count - 1] = jnp.zeros((size, dim), jnp.float32)
        rows = lax.broadcasted_iota(jnp.int32, (length, length), 0)
        cols = lax.broadcasted_iota(jnp.int32, (length, length), 1)
        upper[...] = jnp.where(rows <= cols, 1.0, 0.0).astype(jnp.bfloat16)

    parts = jnp.concatenate(split3(decay_ref[...] * LOG2E), axis=0)
    sums = jnp.dot(parts, upper[...], preferred_element_type=jnp.float32)
    cum = sums[:heads] + sums[heads : 2 * heads] + sums[2 * heads :]
    cum_ref[...] = cum
    last = cum[:, length - 1 :]
    to_last = jnp.exp2(last - cum)
    decay = jnp.exp2(jnp.broadcast_to(last, (heads, dim)))
    before = jnp.where(blk == 0, count, blk) - 1
    for pair in range(heads // 2):
        scaled = []
        for head in (2 * pair, 2 * pair + 1):
            keys = key_ref[:, head * dim : (head + 1) * dim].T.astype(jnp.float32)
            scaled.append((keys * to_last[head : head + 1]).astype(jnp.bfloat16))
        update = jnp.dot(
            jnp.concatenate(scaled, axis=0),
            value_ref[:, 2 * pair * dim : 2 * (pair + 1) * dim],
            preferred_element_type=jnp.float32,
        )
        for which, head in enumerate((2 * pair, 2 * pair + 1)):
            rows = slice(head * dim, (head + 1) * dim)
            cols = slice(which * dim, (which + 1) * dim)
            states_ref[blk, rows] = decay[head : head + 1] * states_ref[before, rows] + update[cols, cols]
    reached[...] += jnp.broadcast_to(last, (heads, dim))
    reached_ref[blk] = reached[...]

    @pl.when(blk == PAGE // BLOCK - 1)
    def _():
        mid_ref[...] = states_ref[blk].astype(jnp.bfloat16)
        end_ref[size + 3 * heads :] = jnp.concatenate(split3(reached[...]), axis=0)

    @pl.when(blk == count - 1)
    def _():
        end_ref[:size] = states_ref[blk].astype(jnp.bfloat16)
        end_ref[size : size + 3 * heads] = jnp.concatenate(split3(reached[...]), axis=0)


def in_hbm(value):
    return pltpu.with_memory_space_constraint(value, pltpu.HBM)


def run_states(key_rows, value_rows, decay_log):
    tokens, width = key_rows.shape
    heads = decay_log.shape[0]
    dim = width // heads
    blocks = tokens // BLOCK
    size = heads * dim
    whole = pl.BlockSpec(memory_space=pltpu.VMEM)
    return pl.pallas_call(
        functools.partial(state_kernel, heads),
        grid=(blocks,),
        in_specs=[
            pl.BlockSpec((BLOCK, width), lambda b: (b, 0)),
            pl.BlockSpec((BLOCK, width), lambda b: (b, 0)),
            pl.BlockSpec((heads, BLOCK), lambda b: (0, b)),
        ],
        out_specs=[pl.BlockSpec((heads, BLOCK), lambda b: (0, b)), whole, whole, whole, whole],
        out_shape=[
            jax.ShapeDtypeStruct((heads, tokens), jnp.float32),
            pltpu.VMEM((blocks, size, dim), jnp.float32),
            pltpu.VMEM((blocks, heads, dim), jnp.float32),
            pltpu.VMEM((size + 6 * heads, dim), jnp.bfloat16),
            pltpu.VMEM((size, dim), jnp.bfloat16),
        ],
        scratch_shapes=[
            pltpu.VMEM((heads, dim), jnp.float32),
            pltpu.VMEM((BLOCK, BLOCK), jnp.bfloat16),
        ],
        compiler_params=pltpu.CompilerParams(vmem_limit_bytes=12 * MIB),
        cost_estimate=pl.CostEstimate(flops=4 * tokens * width * dim, bytes_accessed=4 * tokens * width, transcendentals=0),
        name="states",
    )(in_hbm(key_rows), in_hbm(value_rows), decay_log)


def inner_kernel(heads, first, query_ref, key_ref, value_ref, cum_ref, *refs):
    out_ref, done_ref = refs[-2:]
    length, width = query_ref.shape
    dim = width // heads
    cum = cum_ref[...]
    cum_cols = cum.T
    causal = lax.broadcasted_iota(jnp.int32, (TILE, TILE), 0) >= lax.broadcasted_iota(jnp.int32, (TILE, TILE), 1)
    base = (pl.program_id(0) + first) * length
    for head in range(heads):
        lanes = slice(head * dim, (head + 1) * dim)
        for tile in range(length // TILE):
            start, stop = tile * TILE, (tile + 1) * TILE
            scores = lax.dot_general(
                query_ref[start:stop, lanes], key_ref[:stop, lanes], NT, preferred_element_type=jnp.float32
            )
            damping = jnp.exp2(cum_cols[start:stop, head : head + 1] - cum[head : head + 1, :stop])
            weights = scores * damping
            diagonal = jnp.where(causal, weights[:, start:], 0.0)
            if tile:
                weights = jnp.concatenate([weights[:, :start], diagonal], axis=1)
            else:
                weights = diagonal
            out_ref[pl.ds(pl.multiple_of(base + start, TILE), TILE), lanes] = jnp.dot(
                weights.astype(jnp.bfloat16), value_ref[:stop, lanes], preferred_element_type=jnp.float32
            )
    done_ref[...] = cum[:, :128]


def run_inner(queries, key_rows, value_rows, cumulative, first, count, earlier=None):
    tokens, width = queries.shape
    heads = cumulative.shape[0]
    rows = pl.BlockSpec((BLOCK, width), lambda b: (b + first, 0))
    whole = pl.BlockSpec(memory_space=pltpu.VMEM)
    share = tokens * count * BLOCK // tokens
    return pl.pallas_call(
        functools.partial(inner_kernel, heads, first),
        grid=(count,),
        in_specs=[rows, rows, rows, pl.BlockSpec((heads, BLOCK), lambda b: (0, b + first))]
        + ([] if earlier is None else [whole]),
        out_specs=[whole, pl.BlockSpec((heads, 128), lambda b: (0, 0))],
        out_shape=[pltpu.VMEM((tokens, width), jnp.float32), jax.ShapeDtypeStruct((heads, 128), jnp.float32)],
        input_output_aliases={} if earlier is None else {4: 0},
        compiler_params=pltpu.CompilerParams(vmem_limit_bytes=12 * MIB),
        cost_estimate=pl.CostEstimate(flops=4 * share * width * BLOCK, bytes_accessed=10 * share * width, transcendentals=0),
        name="inner",
    )(in_hbm(queries), in_hbm(key_rows), in_hbm(value_rows), cumulative, *([] if earlier is None else [earlier]))


def read_logs(ends, size, heads):
    whole, first = [], []
    for end in ends:
        parts = end[size:].astype(jnp.float32)
        whole.append(parts[:heads] + parts[heads : 2 * heads] + parts[2 * heads : 3 * heads])
        first.append(parts[3 * heads : 4 * heads] + parts[4 * heads : 5 * heads] + parts[5 * heads :])
    return whole, first


def gather_states(total, ends, places, logs, place, extra, heads, dim):
    factors = []
    for source in range(len(ends)):
        log = extra
        for other, other_log in enumerate(logs):
            between = (places[other] > places[source]) & (places[other] < place)
            log = log + jnp.where(between, other_log, 0.0)
        factors.append(jnp.where(places[source] < place, jnp.exp2(log), 0.0))
    for head in range(heads):
        rows = slice(head * dim, (head + 1) * dim)
        value = jnp.zeros((dim, dim), jnp.float32)
        for source, end in enumerate(ends):
            value += factors[source][head : head + 1] * end[rows].astype(jnp.float32)
        total[rows] = value


def finish_kernel(heads, inner_ref, query_ref, cum_ref, states_ref, reached_ref, *refs):
    *ends, out_ref, square_ref, entry = refs
    blk = pl.program_id(0)
    length, width = query_ref.shape
    dim = width // heads
    size = heads * dim

    @pl.when(blk == 0)
    def _():
        place = lax.axis_index("seq")
        logs, _unused = read_logs(ends, size, heads)
        places = [place ^ offset for offset in range(len(ends))]
        gather_states(entry, ends, places, logs, place, jnp.zeros((heads, dim), jnp.float32), heads, dim)

    started = blk > 0
    before = jnp.maximum(blk, 1) - 1
    factor = jnp.exp2(jnp.where(started, reached_ref[before], 0.0))
    growth = jnp.exp2(cum_ref[...]).T
    squares = jnp.zeros((length, dim), jnp.float32)
    zero = jnp.zeros((dim, dim), jnp.bfloat16)
    here = pl.ds(pl.multiple_of(blk * length, length), length)
    for pair in range(heads // 2):
        highs, lows = [], []
        for head in (2 * pair, 2 * pair + 1):
            rows = slice(head * dim, (head + 1) * dim)
            state = factor[head : head + 1] * entry[rows] + jnp.where(started, states_ref[before, rows], 0.0)
            high = state.astype(jnp.bfloat16)
            highs.append(high)
            lows.append((state - high.astype(jnp.float32)).astype(jnp.bfloat16))
        query = query_ref[:, 2 * pair * dim : 2 * (pair + 1) * dim]
        carried = 0.0
        for one, two in (highs, lows):
            both = jnp.concatenate(
                [jnp.concatenate([one, zero], axis=1), jnp.concatenate([zero, two], axis=1)], axis=0
            )
            carried = carried + jnp.dot(query, both, preferred_element_type=jnp.float32)
        for which, head in enumerate((2 * pair, 2 * pair + 1)):
            lanes = slice(head * dim, (head + 1) * dim)
            out = inner_ref[here, lanes] + carried[:, which * dim : (which + 1) * dim] * growth[:, head : head + 1]
            out_ref[here, lanes] = out
            squares += out * out
    high = squares.astype(jnp.bfloat16)
    low = (squares - high.astype(jnp.float32)).astype(jnp.bfloat16)
    ones = jnp.ones((8, dim), jnp.bfloat16)
    sums = lax.dot_general(ones, high, NT, preferred_element_type=jnp.float32)
    sums = sums + lax.dot_general(ones, low, NT, preferred_element_type=jnp.float32)
    for row in range(length // 128):
        square_ref[pl.ds(blk * (length // 128) + row, 1)] = sums[:1, row * 128 : (row + 1) * 128]


def run_finish(inner, queries, cumulative, states, reached, ends):
    tokens, width = queries.shape
    heads = cumulative.shape[0]
    dim = width // heads
    size = heads * dim
    blocks = tokens // BLOCK
    rows = pl.BlockSpec((BLOCK, width), lambda b: (b, 0))
    whole = pl.BlockSpec(memory_space=pltpu.VMEM)
    return pl.pallas_call(
        functools.partial(finish_kernel, heads),
        grid=(blocks,),
        in_specs=[
            whole,
            rows,
            pl.BlockSpec((heads, BLOCK), lambda b: (0, b)),
            whole,
            whole,
        ]
        + [whole] * len(ends),
        out_specs=[whole, whole],
        out_shape=[
            pltpu.VMEM((tokens, width), jnp.float32),
            pltpu.VMEM((tokens // 128, 128), jnp.float32),
        ],
        input_output_aliases={0: 0},
        scratch_shapes=[pltpu.VMEM((size, dim), jnp.float32)],
        compiler_params=pltpu.CompilerParams(vmem_limit_bytes=12 * MIB),
        cost_estimate=pl.CostEstimate(flops=4 * tokens * width * dim, bytes_accessed=10 * tokens * width, transcendentals=0),
        name="finish",
    )(inner, in_hbm(queries), cumulative, states, reached, *ends)


def scale_kernel(whole_width, out_ref, gain_ref, *refs):
    *squares, attended_ref = refs
    blk = pl.program_id(0)
    length, width = attended_ref.shape
    for part in range(length // 128):
        row = pl.ds(blk * (length // 128) + part, 1)
        total = squares[0][row]
        for square in squares[1:]:
            total = total + square[row]
        scale = lax.rsqrt(total * (1.0 / whole_width) + 1e-06)
        scale = jnp.broadcast_to(scale, (8, 128)).T[:, :1]
        here = pl.ds(pl.multiple_of(blk * length + part * 128, 128), 128)
        attended_ref[part * 128 : (part + 1) * 128] = (out_ref[here] * scale * gain_ref[...]).astype(jnp.bfloat16)


def run_scale(out, gain, squares, whole_width):
    tokens, width = out.shape
    whole = pl.BlockSpec(memory_space=pltpu.VMEM)
    return pl.pallas_call(
        functools.partial(scale_kernel, whole_width),
        grid=(tokens // BLOCK,),
        in_specs=[whole, whole] + [whole for _ in squares],
        out_specs=pl.BlockSpec((BLOCK, width), lambda b: (b, 0)),
        out_shape=jax.ShapeDtypeStruct((tokens, width), jnp.bfloat16),
        compiler_params=pltpu.CompilerParams(vmem_limit_bytes=12 * MIB),
        cost_estimate=pl.CostEstimate(flops=tokens * width, bytes_accessed=6 * tokens * width, transcendentals=0),
        name="scale",
    )(out, gain.reshape(1, width), *squares)


def cache_kernel(heads, count, owner_ref, *refs):
    ends, mids = refs[:count], refs[count : 2 * count]
    cache_ref, total, logs_ref, first_ref, page_of = refs[2 * count :]
    size, dim = mids[0].shape
    place = lax.axis_index("seq")
    places = [place ^ offset for offset in range(count)]
    whole, first = read_logs(ends, size, heads)
    for source in range(count):
        logs_ref[source] = whole[source]
        first_ref[source] = first[source]
    for slot in range(SLOTS):
        page_of[slot] = -1

    def look(page, found):
        mine = (owner_ref[page] == place) & (found < SLOTS)

        @pl.when(mine)
        def _():
            page_of[found] = page

        return found + mine.astype(jnp.int32)

    lax.fori_loop(0, owner_ref.shape[0], look, jnp.int32(0))

    def fill(slot, carry):
        page = page_of[slot]
        at_end = page % 2 == 1
        until = page // 2 + page % 2
        halfway = jnp.logical_not(at_end) & (page >= 0)

        @pl.when(page >= 0)
        def _():
            logs = [logs_ref[source] for source in range(count)]
            extra = jnp.zeros((heads, dim), jnp.float32)
            for source in range(count):
                extra = extra + jnp.where((places[source] == until) & halfway, first_ref[source], 0.0)
            gather_states(total, ends, places, logs, until, extra, heads, dim)

        @pl.when(page < 0)
        def _():
            total[...] = jnp.zeros_like(total)

        for source in range(count):

            @pl.when((places[source] == until) & halfway)
            def _():
                total[...] += mids[source][...].astype(jnp.float32)

        cache_ref[slot] = total[...].astype(jnp.bfloat16)
        return carry

    lax.fori_loop(0, SLOTS, fill, 0)


def run_cache(page_owner, ends, mids, heads):
    size, dim = mids[0].shape
    count = len(ends)
    vmem = pl.BlockSpec(memory_space=pltpu.VMEM)
    smem = pl.BlockSpec(memory_space=pltpu.SMEM)
    return pl.pallas_call(
        functools.partial(cache_kernel, heads, count),
        in_specs=[smem] + [vmem] * (2 * count),
        out_specs=vmem,
        out_shape=jax.ShapeDtypeStruct((SLOTS, size, dim), jnp.bfloat16),
        scratch_shapes=[
            pltpu.VMEM((size, dim), jnp.float32),
            pltpu.VMEM((count, heads, dim), jnp.float32),
            pltpu.VMEM((count, heads, dim), jnp.float32),
            pltpu.SMEM((SLOTS,), jnp.int32),
        ],
        compiler_params=pltpu.CompilerParams(vmem_limit_bytes=12 * MIB),
        cost_estimate=pl.CostEstimate(flops=20 * size * dim, bytes_accessed=20 * size * dim, transcendentals=0),
        name="cache",
    )(page_owner, *ends, *mids)


def swap(value, axis, offset):
    return lax.ppermute(value, axis, [(place, place ^ offset) for place in range(lax.axis_size(axis))])


def tie(value, *after):
    return lax.optimization_barrier((value, *after))[0]


def shards(queries, key_rows, value_rows, decay_log, norm_gain, page_owner):
    tokens, width = queries.shape
    heads = decay_log.shape[0]
    dim = width // heads
    count = lax.axis_size("seq")
    blocks = tokens // BLOCK
    cumulative, states, reached, end, mid = run_states(key_rows, value_rows, decay_log)
    ends, mids = {0: end}, {0: mid}
    for offset in range(2, count, 2):
        ends[offset] = swap(end, "seq", offset)
    ends[1] = swap(end, "seq", 1)
    inner, done = run_inner(queries, key_rows, value_rows, cumulative, 0, blocks // 2)
    mid = tie(mid, done)
    for offset in range(2, count, 2):
        mids[offset] = swap(mid, "seq", offset)
    inner, done = run_inner(queries, key_rows, value_rows, cumulative, blocks // 2, blocks - blocks // 2, inner)
    for offset in range(2, count, 2):
        ends[offset + 1] = swap(tie(ends[offset], done), "seq", 1)
    ends = [ends[offset] for offset in range(count)]
    out, square = run_finish(inner, queries, cumulative, states, reached, ends)
    squares = [square] + [swap(square, "head", offset) for offset in range(1, lax.axis_size("head"))]
    for offset in range(0, count, 2):
        mids[offset + 1] = swap(tie(mids[offset], square), "seq", 1)
    mids = [mids[offset] for offset in range(count)]
    attended = run_scale(out, norm_gain, squares, width * lax.axis_size("head"))
    page_cache = run_cache(page_owner, ends, mids, heads)
    return attended, page_cache.reshape(SLOTS, heads, dim, dim)


def solution(mesh):
    return jax.shard_map(
        shards,
        mesh=mesh,
        in_specs=(
            P("seq", "head"),
            P("seq", "head"),
            P("seq", "head"),
            P("head", "seq"),
            P("head"),
            P(),
        ),
        out_specs=(P("seq", "head"), P("seq", "head", None, None)),
        check_vma=False,
    )
```

time: 90.5 us -> 63.6 us (0.70)
  local copies, waits for them, and re-layouts: 19.1 us -> 0.84 us
  waiting for transfers between devices: 19.2 us -> 9.33 us
  Pallas kernels: 32.3 us -> 35.4 us
  starting transfers between devices: 18.5 us -> 17.5 us
    unnamed x26 -> x6, local copies, waits for them, and re-layouts: 19.1 us -> 0.84 us
    ppermute x17, waiting for transfers between devices: 19.2 us -> 9.33 us  [swap(): lax.ppermute(value, axis, [(place, place ^ offset) for place in range(lax...]
    pallas_call x1 -> x2, Pallas kernels: 10.8 us -> 15 us  [run_inner(): pl.pallas_call(functools.partial(inner_kernel, heads, first), grid=(count...]
    ppermute x17, starting transfers between devices: 18.5 us -> 17.5 us  [swap(): lax.ppermute(value, axis, [(place, place ^ offset) for place in range(lax...]
  transfers between devices with their start and end apart: 17 -> 17, of which waited for: 5 -> 4; matrix products, arithmetic and copies ran while one was open for 0% -> 0% of each run, Pallas kernels for 25% -> 41%
where the time goes in v2:
time: 63.6 us; the launch traced here: 63.8 us
  Pallas kernels  35.4 us (56%)
  starting transfers between devices  17.5 us (28%)
  waiting for transfers between devices  9.33 us (15%)
  local copies, waits for them, and re-layouts  0.84 us (1%)
  between operations  0.69 us (1%)
    ppermute x17, starting transfers between devices, swap(): lax.ppermute(value, axis, [(place, place ^ offset) for place in range(lax...  17.5 us
    pallas_call x2, Pallas kernels, run_inner(): pl.pallas_call(functools.partial(inner_kernel, heads, first), grid=(count...  15 us
    ppermute x17, waiting for transfers between devices, swap(): lax.ppermute(value, axis, [(place, place ^ offset) for place in range(lax...  9.33 us
    pallas_call x1, Pallas kernels, run_finish(): pl.pallas_call(functools.partial(finish_kernel, heads), grid=(blocks,), i...  8.44 us
    pallas_call x1, Pallas kernels, run_states(): pl.pallas_call(functools.partial(state_kernel, heads), grid=(blocks,), in...  5.54 us
    pallas_call x1, Pallas kernels, run_cache(): pl.pallas_call(functools.partial(cache_kernel, heads, count), in_specs=[s...  3.48 us
    pallas_call x1, Pallas kernels, run_scale(): pl.pallas_call(functools.partial(scale_kernel, whole_width), grid=(tokens...  3.04 us
  transfers between devices with their start and end apart: 17, of which 4 were waited for; matrix products, arithmetic and copies ran while one was open for 0% of the time, Pallas kernels for 41%

profile of v2, /device:TPU:0, one launch (start us, length us, event | category | flops | bytes accessed | tf_op | source)
XLA Modules:
  0.0 63.8 jit_solution(7053958842344173569)
XLA Ops:
  0.6 0.0 copy-start
  0.6 0.8 %copy-done = f32[8,2048]{1,0:T(8,128)S(1)} copy-done((f32[8,2048]{1,0:T(8,128)S(1)}, f32[8,2048]{1,0:T(8,128)}, u32[]{:S(2)}) %copy-start) | copy-done | bytes 65560
  1.5 5.5 %states.1 = (f32[8,2048]{1,0:T(8,128)S(1)}, f32[4,1024,128]{2,1,0:T(8,128)S(1)}, f32[4,8,128]{2,1,0:T(8,128)S(1)}, bf16[1072,128]{1,0:T(8,128)(2,1)S(1)}, bf16[1024,128]{1,0:T(8,128)(2,1)S(1)}) custom-call(bf16[2048,1024]{1,0:T(8,128)(2,1)} %key_ref.5, bf16[2048,1024]{1,0:T(8,128)(2,1)} %value_ref.5, f32[8,2048]{1,0:T(8,128)S(1)} %copy-done), custom_call_target="tpu_custom_call" | custom-call | flops 1073741824 | bytes 8388608 | tf_op jit(solution)/shard_map/states/pallas_call | solution.py:92
  7.0 4.0 %collective-permute-start.5 = (bf16[1072,128]{1,0:T(8,128)(2,1)S(1)}, bf16[1072,128]{1,0:T(8,128)(2,1)S(1)}, u32[]{:S(2)}, u32[]{:S(2)}) collective-permute-start(bf16[1072,128]{1,0:T(8,128)(2,1)S(1)} %get-tuple-element.24.refs_0_), channel_id=1, source_target_pairs={{0,24},{4,28},{8,16},{12,20},{16,8},{20,12},{24,0},{28,4},{1,25},{... | collective-permute-start | bytes 823304 | tf_op jit(solution)/shard_map/ppermute | solution.py:380
  11.0 0.5 collective-permute-start.3
  11.5 0.1 collective-permute-start.1
  11.6 0.0 collective-permute-start
  11.6 7.5 %inner.2 = (f32[2048,1024]{1,0:T(8,128)S(1)}, f32[8,128]{1,0:T(8,128)}) custom-call(bf16[2048,1024]{1,0:T(8,128)(2,1)} %query_ref.5, bf16[2048,1024]{1,0:T(8,128)(2,1)} %key_ref.5, bf16[2048,1024]{1,0:T(8,128)(2,1)} %value_ref.5, f32[8,2048]{1,0:T(8,128)S(1)} %get-tuple-element.19.cum_ref), custom_call_target="tpu_custom_call" | custom-call | flops 2147483648 | bytes 10485760 | tf_op jit(solution)/shard_map/inner/pallas_call | solution.py:152
  19.1 7.5 %inner.3 = (f32[2048,1024]{1,0:T(8,128)S(1)}, f32[8,128]{1,0:T(8,128)}) custom-call(bf16[2048,1024]{1,0:T(8,128)(2,1)} %query_ref.5, bf16[2048,1024]{1,0:T(8,128)(2,1)} %key_ref.5, bf16[2048,1024]{1,0:T(8,128)(2,1)} %value_ref.5, f32[8,2048]{1,0:T(8,128)S(1)} %get-tuple-element.19.cum_ref, ...), custom_call_target="tpu_custom_call", output_to_operand_aliasing={{0}: (4, {})} | custom-call | flops 2147483648 | bytes 10485760 | tf_op jit(solution)/shard_map/inner/pallas_call | solution.py:152
  26.6 0.0 collective-permute-done.5.refs_6_
  26.6 0.5 collective-permute-start.6
  27.1 0.0 collective-permute-done.3.refs_4_
  27.1 0.1 collective-permute-start.4
  27.2 0.0 collective-permute-done.1.refs_2_
  27.2 0.4 collective-permute-start.2
  27.6 1.9 %collective-permute-start.11 = (bf16[1024,128]{1,0:T(8,128)(2,1)S(1)}, bf16[1024,128]{1,0:T(8,128)(2,1)S(1)}, u32[]{:S(2)}, u32[]{:S(2)}) collective-permute-start(bf16[1024,128]{1,0:T(8,128)(2,1)S(1)} %get-tuple-element.32.refs_8_), channel_id=1, source_target_pairs={{0,8},{4,12},{8,0},{12,4},{16,24},{20,28},{24,16},{28,20},{1,9},{5... | collective-permute-start | bytes 786440 | tf_op jit(solution)/shard_map/ppermute | solution.py:380
  29.5 0.0 collective-permute-done.refs_1_
  29.5 1.5 %collective-permute-start.13 = (bf16[1024,128]{1,0:T(8,128)(2,1)S(1)}, bf16[1024,128]{1,0:T(8,128)(2,1)S(1)}, u32[]{:S(2)}, u32[]{:S(2)}) collective-permute-start(bf16[1024,128]{1,0:T(8,128)(2,1)S(1)} %get-tuple-element.32.refs_8_), channel_id=1, source_target_pairs={{0,16},{4,20},{8,24},{12,28},{16,0},{20,4},{24,8},{28,12},{1,17},{... | collective-permute-start | bytes 786440 | tf_op jit(solution)/shard_map/ppermute | solution.py:380
  31.0 0.0 collective-permute-done.6.refs_7_
  31.0 0.1 collective-permute-start.15
  31.1 0.0 collective-permute-done.4.refs_5_
  31.1 0.0 collective-permute-done.2.refs_3_
  31.1 0.0 copy-start.1
  31.1 8.4 %finish.1 = (f32[2048,1024]{1,0:T(8,128)S(1)}, f32[16,128]{1,0:T(8,128)S(1)}) custom-call(f32[2048,1024]{1,0:T(8,128)S(1)} %get-tuple-element.21.inner_ref, bf16[2048,1024]{1,0:T(8,128)(2,1)} %query_ref.5, f32[8,2048]{1,0:T(8,128)S(1)} %get-tuple-element.19.cum_ref, ...), custom_call_target="tpu_custom_call", output_to_operand_aliasing={{0}: (0, {})} | custom-call | flops 1073741824 | bytes 20971520 | tf_op jit(solution)/shard_map/finish/pallas_call | solution.py:249
  39.6 0.0 collective-permute-done.11.refs_10_
  39.6 0.1 collective-permute-start.12
  39.7 3.4 %collective-permute-done.13.refs_12_ = bf16[1024,128]{1,0:T(8,128)(2,1)S(1)} collective-permute-done((bf16[1024,128]{1,0:T(8,128)(2,1)S(1)}, bf16[1024,128]{1,0:T(8,128)(2,1)S(1)}, u32[]{:S(2)}, u32[]{:S(2)}) %collective-permute-start.13) | collective-permute-done | bytes 262176 | tf_op jit(solution)/shard_map/ppermute | solution.py:380
  43.1 0.0 collective-permute-start.14
  43.1 0.0 collective-permute-done.15.refs_14_
  43.1 0.5 collective-permute-start.16
  43.6 0.0 collective-permute-start.10
  43.6 1.6 %collective-permute-start.7 = (f32[16,128]{1,0:T(8,128)S(1)}, f32[16,128]{1,0:T(8,128)S(1)}, u32[]{:S(2)}, u32[]{:S(2)}) collective-permute-start(f32[16,128]{1,0:T(8,128)S(1)} %get-tuple-element.30.refs_0_), channel_id=1, source_target_pairs={{0,1},{1,0},{2,3},{3,2},{4,5},{5,4},{6,7},{7,6},{8,9},{9,8},{10,11... | collective-permute-start | bytes 24584 | tf_op jit(solution)/shard_map/ppermute | solution.py:380
  45.2 2.1 %collective-permute-done.7.refs_1_ = f32[16,128]{1,0:T(8,128)S(1)} collective-permute-done((f32[16,128]{1,0:T(8,128)S(1)}, f32[16,128]{1,0:T(8,128)S(1)}, u32[]{:S(2)}, u32[]{:S(2)}) %collective-permute-start.7) | collective-permute-done | bytes 8224 | tf_op jit(solution)/shard_map/ppermute | solution.py:380
  47.3 2.6 %collective-permute-start.8 = (f32[16,128]{1,0:T(8,128)S(1)}, f32[16,128]{1,0:T(8,128)S(1)}, u32[]{:S(2)}, u32[]{:S(2)}) collective-permute-start(f32[16,128]{1,0:T(8,128)S(1)} %get-tuple-element.30.refs_0_), channel_id=1, source_target_pairs={{0,2},{1,3},{2,0},{3,1},{4,6},{5,7},{6,4},{7,5},{8,10},{9,11},{10,... | collective-permute-start | bytes 24584 | tf_op jit(solution)/shard_map/ppermute | solution.py:380
  49.9 2.0 %collective-permute-done.8.refs_2_ = f32[16,128]{1,0:T(8,128)S(1)} collective-permute-done((f32[16,128]{1,0:T(8,128)S(1)}, f32[16,128]{1,0:T(8,128)S(1)}, u32[]{:S(2)}, u32[]{:S(2)}) %collective-permute-start.8) | collective-permute-done | bytes 8224 | tf_op jit(solution)/shard_map/ppermute | solution.py:380
  51.8 3.6 %collective-permute-start.9 = (f32[16,128]{1,0:T(8,128)S(1)}, f32[16,128]{1,0:T(8,128)S(1)}, u32[]{:S(2)}, u32[]{:S(2)}) collective-permute-start(f32[16,128]{1,0:T(8,128)S(1)} %get-tuple-element.30.refs_0_), channel_id=1, source_target_pairs={{0,3},{1,2},{2,1},{3,0},{4,7},{5,6},{6,5},{7,4},{8,11},{9,10},{10,... | collective-permute-start | bytes 24584 | tf_op jit(solution)/shard_map/ppermute | solution.py:380
  55.4 1.8 %collective-permute-done.9.refs_3_ = f32[16,128]{1,0:T(8,128)S(1)} collective-permute-done((f32[16,128]{1,0:T(8,128)S(1)}, f32[16,128]{1,0:T(8,128)S(1)}, u32[]{:S(2)}, u32[]{:S(2)}) %collective-permute-start.9) | collective-permute-done | bytes 8224 | tf_op jit(solution)/shard_map/ppermute | solution.py:380
  57.3 0.0 copy-done.1
  57.3 0.0 copy-start.2
  57.3 3.0 %scale.1 = bf16[2048,1024]{1,0:T(8,128)(2,1)} custom-call(f32[2048,1024]{1,0:T(8,128)S(1)} %get-tuple-element.29.out_ref, f32[1,1024]{1,0:T(1,128)S(1)} %bitcast.2, f32[16,128]{1,0:T(8,128)S(1)} %get-tuple-element.30.refs_0_, f32[16,128]{1,0:T(8,128)S(1)} %collective-permute-done.7.refs_1_, f32[16,128]{1,0:T(8,128)S(1)} %collective-permute-done.8.refs_2_, ...), custom_call_target="tpu_custom_call" | custom-call | flops 2097152 | bytes 12582912 | tf_op jit(solution)/shard_map/scale/pallas_call | solution.py:291
  60.3 0.0 collective-permute-done.12.refs_11_
  60.3 0.0 collective-permute-done.14.refs_13_
  60.3 0.0 collective-permute-done.16.refs_15_
  60.3 0.0 collective-permute-done.10.refs_9_
  60.4 0.0 copy-done.2
  60.4 3.5 %cache.1 = bf16[5,1024,128]{2,1,0:T(8,128)(2,1)} custom-call(s32[16]{0:T(128)S(1)} %copy-done.2, bf16[1072,128]{1,0:T(8,128)(2,1)S(1)} %get-tuple-element.24.refs_0_, bf16[1072,128]{1,0:T(8,128)(2,1)S(1)} %collective-permute-done.refs_1_, bf16[1072,128]{1,0:T(8,128)(2,1)S(1)} %collective-permute-done.1.refs_2_, ...), custom_call_target="tpu_custom_call" | custom-call | flops 2621440 | bytes 2621440 | tf_op jit(solution)/shard_map/cache/pallas_call | solution.py:362
Async XLA Ops:
  0.6 0.8 %copy-start = (f32[8,2048]{1,0:T(8,128)S(1)}, f32[8,2048]{1,0:T(8,128)}, u32[]{:S(2)}) copy-start(f32[8,2048]{1,0:T(8,128)} %decay_ref.1) | copy-start | bytes 196612
  7.0 19.6 %collective-permute-start.5 = (bf16[1072,128]{1,0:T(8,128)(2,1)S(1)}, bf16[1072,128]{1,0:T(8,128)(2,1)S(1)}, u32[]{:S(2)}, u32[]{:S(2)}) collective-permute-start(bf16[1072,128]{1,0:T(8,128)(2,1)S(1)} %get-tuple-element.24.refs_0_), channel_id=1, source_target_pairs={{0,24},{4,28},{8,16},{12,20},{16,8},{20,12},{24,0},{28,4},{1,25},{... | collective-permute-start | bytes 823304 | tf_op jit(solution)/shard_map/ppermute | solution.py:380
  11.0 16.1 %collective-permute-start.3 = (bf16[1072,128]{1,0:T(8,128)(2,1)S(1)}, bf16[1072,128]{1,0:T(8,128)(2,1)S(1)}, u32[]{:S(2)}, u32[]{:S(2)}) collective-permute-start(bf16[1072,128]{1,0:T(8,128)(2,1)S(1)} %get-tuple-element.24.refs_0_), channel_id=1, source_target_pairs={{0,16},{4,20},{8,24},{12,28},{16,0},{20,4},{24,8},{28,12},{1,17},{... | collective-permute-start | bytes 823304 | tf_op jit(solution)/shard_map/ppermute | solution.py:380
  11.5 15.7 %collective-permute-start.1 = (bf16[1072,128]{1,0:T(8,128)(2,1)S(1)}, bf16[1072,128]{1,0:T(8,128)(2,1)S(1)}, u32[]{:S(2)}, u32[]{:S(2)}) collective-permute-start(bf16[1072,128]{1,0:T(8,128)(2,1)S(1)} %get-tuple-element.24.refs_0_), channel_id=1, source_target_pairs={{0,8},{4,12},{8,0},{12,4},{16,24},{20,28},{24,16},{28,20},{1,9},{5... | collective-permute-start | bytes 823304 | tf_op jit(solution)/shard_map/ppermute | solution.py:380
  11.6 17.9 %collective-permute-start = (bf16[1072,128]{1,0:T(8,128)(2,1)S(1)}, bf16[1072,128]{1,0:T(8,128)(2,1)S(1)}, u32[]{:S(2)}, u32[]{:S(2)}) collective-permute-start(bf16[1072,128]{1,0:T(8,128)(2,1)S(1)} %get-tuple-element.24.refs_0_), channel_id=1, source_target_pairs={{0,4},{4,0},{8,12},{12,8},{16,20},{20,16},{24,28},{28,24},{1,5},{5... | collective-permute-start | bytes 823304 | tf_op jit(solution)/shard_map/ppermute | solution.py:380
  26.6 4.4 %collective-permute-start.6 = (bf16[1072,128]{1,0:T(8,128)(2,1)S(1)}, bf16[1072,128]{1,0:T(8,128)(2,1)S(1)}, u32[]{:S(2)}, u32[]{:S(2)}) collective-permute-start(bf16[1072,128]{1,0:T(8,128)(2,1)S(1)} %collective-permute-done.5.refs_6_), channel_id=1, source_target_pairs={{0,4},{4,0},{8,12},{12,8},{16,20},{20,16},{24,28},{28,24},{1,5},{5... | collective-permute-start | bytes 823304 | tf_op jit(solution)/shard_map/ppermute | solution.py:380
  27.1 4.0 %collective-permute-start.4 = (bf16[1072,128]{1,0:T(8,128)(2,1)S(1)}, bf16[1072,128]{1,0:T(8,128)(2,1)S(1)}, u32[]{:S(2)}, u32[]{:S(2)}) collective-permute-start(bf16[1072,128]{1,0:T(8,128)(2,1)S(1)} %collective-permute-done.3.refs_4_), channel_id=1, source_target_pairs={{0,4},{4,0},{8,12},{12,8},{16,20},{20,16},{24,28},{28,24},{1,5},{5... | collective-permute-start | bytes 823304 | tf_op jit(solution)/shard_map/ppermute | solution.py:380
  27.2 4.0 %collective-permute-start.2 = (bf16[1072,128]{1,0:T(8,128)(2,1)S(1)}, bf16[1072,128]{1,0:T(8,128)(2,1)S(1)}, u32[]{:S(2)}, u32[]{:S(2)}) collective-permute-start(bf16[1072,128]{1,0:T(8,128)(2,1)S(1)} %collective-permute-done.1.refs_2_), channel_id=1, source_target_pairs={{0,4},{4,0},{8,12},{12,8},{16,20},{20,16},{24,28},{28,24},{1,5},{5... | collective-permute-start | bytes 823304 | tf_op jit(solution)/shard_map/ppermute | solution.py:380
  27.6 12.0 %collective-permute-start.11 = (bf16[1024,128]{1,0:T(8,128)(2,1)S(1)}, bf16[1024,128]{1,0:T(8,128)(2,1)S(1)}, u32[]{:S(2)}, u32[]{:S(2)}) collective-permute-start(bf16[1024,128]{1,0:T(8,128)(2,1)S(1)} %get-tuple-element.32.refs_8_), channel_id=1, source_target_pairs={{0,8},{4,12},{8,0},{12,4},{16,24},{20,28},{24,16},{28,20},{1,9},{5... | collective-permute-start | bytes 786440 | tf_op jit(solution)/shard_map/ppermute | solution.py:380
  29.5 13.6 %collective-permute-start.13 = (bf16[1024,128]{1,0:T(8,128)(2,1)S(1)}, bf16[1024,128]{1,0:T(8,128)(2,1)S(1)}, u32[]{:S(2)}, u32[]{:S(2)}) collective-permute-start(bf16[1024,128]{1,0:T(8,128)(2,1)S(1)} %get-tuple-element.32.refs_8_), channel_id=1, source_target_pairs={{0,16},{4,20},{8,24},{12,28},{16,0},{20,4},{24,8},{28,12},{1,17},{... | collective-permute-start | bytes 786440 | tf_op jit(solution)/shard_map/ppermute | solution.py:380
  31.0 12.1 %collective-permute-start.15 = (bf16[1024,128]{1,0:T(8,128)(2,1)S(1)}, bf16[1024,128]{1,0:T(8,128)(2,1)S(1)}, u32[]{:S(2)}, u32[]{:S(2)}) collective-permute-start(bf16[1024,128]{1,0:T(8,128)(2,1)S(1)} %get-tuple-element.32.refs_8_), channel_id=1, source_target_pairs={{0,24},{4,28},{8,16},{12,20},{16,8},{20,12},{24,0},{28,4},{1,25},{... | collective-permute-start | bytes 786440 | tf_op jit(solution)/shard_map/ppermute | solution.py:380
  31.1 26.2 %copy-start.1 = (f32[1024]{0:T(1024)S(1)}, f32[1024]{0:T(1024)}, u32[]{:S(2)}) copy-start(f32[1024]{0:T(1024)} %param.10) | copy-start | bytes 12292
  39.6 20.8 %collective-permute-start.12 = (bf16[1024,128]{1,0:T(8,128)(2,1)S(1)}, bf16[1024,128]{1,0:T(8,128)(2,1)S(1)}, u32[]{:S(2)}, u32[]{:S(2)}) collective-permute-start(bf16[1024,128]{1,0:T(8,128)(2,1)S(1)} %collective-permute-done.11.refs_10_), channel_id=1, source_target_pairs={{0,4},{4,0},{8,12},{12,8},{16,20},{20,16},{24,28},{28,24},{1,5},{5... | collective-permute-start | bytes 786440 | tf_op jit(solution)/shard_map/ppermute | solution.py:380
  43.1 17.2 %collective-permute-start.14 = (bf16[1024,128]{1,0:T(8,128)(2,1)S(1)}, bf16[1024,128]{1,0:T(8,128)(2,1)S(1)}, u32[]{:S(2)}, u32[]{:S(2)}) collective-permute-start(bf16[1024,128]{1,0:T(8,128)(2,1)S(1)} %collective-permute-done.13.refs_12_), channel_id=1, source_target_pairs={{0,4},{4,0},{8,12},{12,8},{16,20},{20,16},{24,28},{28,24},{1,5},{5... | collective-permute-start | bytes 786440 | tf_op jit(solution)/shard_map/ppermute | solution.py:380
  43.1 17.2 %collective-permute-start.16 = (bf16[1024,128]{1,0:T(8,128)(2,1)S(1)}, bf16[1024,128]{1,0:T(8,128)(2,1)S(1)}, u32[]{:S(2)}, u32[]{:S(2)}) collective-permute-start(bf16[1024,128]{1,0:T(8,128)(2,1)S(1)} %collective-permute-done.15.refs_14_), channel_id=1, source_target_pairs={{0,4},{4,0},{8,12},{12,8},{16,20},{20,16},{24,28},{28,24},{1,5},{5... | collective-permute-start | bytes 786440 | tf_op jit(solution)/shard_map/ppermute | solution.py:380
  43.6 16.7 %collective-permute-start.10 = (bf16[1024,128]{1,0:T(8,128)(2,1)S(1)}, bf16[1024,128]{1,0:T(8,128)(2,1)S(1)}, u32[]{:S(2)}, u32[]{:S(2)}) collective-permute-start(bf16[1024,128]{1,0:T(8,128)(2,1)S(1)} %get-tuple-element.32.refs_8_), channel_id=1, source_target_pairs={{0,4},{4,0},{8,12},{12,8},{16,20},{20,16},{24,28},{28,24},{1,5},{5... | collective-permute-start | bytes 786440 | tf_op jit(solution)/shard_map/ppermute | solution.py:380
  43.6 3.7 %collective-permute-start.7 = (f32[16,128]{1,0:T(8,128)S(1)}, f32[16,128]{1,0:T(8,128)S(1)}, u32[]{:S(2)}, u32[]{:S(2)}) collective-permute-start(f32[16,128]{1,0:T(8,128)S(1)} %get-tuple-element.30.refs_0_), channel_id=1, source_target_pairs={{0,1},{1,0},{2,3},{3,2},{4,5},{5,4},{6,7},{7,6},{8,9},{9,8},{10,11... | collective-permute-start | bytes 24584 | tf_op jit(solution)/shard_map/ppermute | solution.py:380
  47.3 4.5 %collective-permute-start.8 = (f32[16,128]{1,0:T(8,128)S(1)}, f32[16,128]{1,0:T(8,128)S(1)}, u32[]{:S(2)}, u32[]{:S(2)}) collective-permute-start(f32[16,128]{1,0:T(8,128)S(1)} %get-tuple-element.30.refs_0_), channel_id=1, source_target_pairs={{0,2},{1,3},{2,0},{3,1},{4,6},{5,7},{6,4},{7,5},{8,10},{9,11},{10,... | collective-permute-start | bytes 24584 | tf_op jit(solution)/shard_map/ppermute | solution.py:380
  51.8 5.4 %collective-permute-start.9 = (f32[16,128]{1,0:T(8,128)S(1)}, f32[16,128]{1,0:T(8,128)S(1)}, u32[]{:S(2)}, u32[]{:S(2)}) collective-permute-start(f32[16,128]{1,0:T(8,128)S(1)} %get-tuple-element.30.refs_0_), channel_id=1, source_target_pairs={{0,3},{1,2},{2,1},{3,0},{4,7},{5,6},{6,5},{7,4},{8,11},{9,10},{10,... | collective-permute-start | bytes 24584 | tf_op jit(solution)/shard_map/ppermute | solution.py:380
  57.3 3.1 %copy-start.2 = (s32[16]{0:T(128)S(1)}, s32[16]{0:T(128)}, u32[]{:S(2)}) copy-start(s32[16]{0:T(128)} %owner_ref.1) | copy-start | bytes 196

commit v3 on v2

v3 whole, which is shorter than its diff:
```python
import functools
import math

import jax
import jax.numpy as jnp
from jax import lax
from jax.experimental import pallas as pl
from jax.experimental.pallas import tpu as pltpu
from jax.sharding import PartitionSpec as P

BLOCK = 512
PAGE = 1024
SLOTS = 5
TILE = 256
LOG2E = math.log2(math.e)
MIB = 1 << 20
SMALL = pl.CostEstimate(flops=1, bytes_accessed=1, transcendentals=0)

NT = (((1,), (1,)), ((), ()))
TN = (((0,), (0,)), ((), ()))


def split3(x):
    high = x.astype(jnp.bfloat16)
    rest = x - high.astype(jnp.float32)
    middle = rest.astype(jnp.bfloat16)
    low = (rest - middle.astype(jnp.float32)).astype(jnp.bfloat16)
    return high, middle, low


def state_kernel(heads, key_hbm, value_hbm, decay_hbm, cum_ref, states_ref, reached_ref, end_ref, mid_ref, keys, values, decays, sems):
    tokens, width = keys.shape
    dim = width // heads
    size = heads * dim
    blocks = tokens // BLOCK
    decay_copy = pltpu.make_async_copy(decay_hbm, decays, sems.at[2 * blocks])
    decay_copy.start()
    copies = []
    for blk in range(blocks):
        rows = pl.ds(blk * BLOCK, BLOCK)
        copies.append(
            (
                pltpu.make_async_copy(key_hbm.at[rows], keys.at[rows], sems.at[2 * blk]),
                pltpu.make_async_copy(value_hbm.at[rows], values.at[rows], sems.at[2 * blk + 1]),
            )
        )
        copies[-1][0].start()
        copies[-1][1].start()
    upper = jnp.where(
        lax.broadcasted_iota(jnp.int32, (BLOCK, BLOCK), 0) <= lax.broadcasted_iota(jnp.int32, (BLOCK, BLOCK), 1), 1.0, 0.0
    ).astype(jnp.bfloat16)
    decay_copy.wait()
    parts = [
        part for blk in range(blocks) for part in split3(decays[:, blk * BLOCK : (blk + 1) * BLOCK] * LOG2E)
    ]
    sums = jnp.dot(jnp.concatenate(parts, axis=0), upper, preferred_element_type=jnp.float32)
    to_last, decay = [], []
    reached = jnp.zeros((heads, dim), jnp.float32)
    for blk in range(blocks):
        base = 3 * heads * blk
        cum = sums[base : base + heads] + sums[base + heads : base + 2 * heads] + sums[base + 2 * heads : base + 3 * heads]
        cum_ref[:, blk * BLOCK : (blk + 1) * BLOCK] = cum
        last = cum[:, BLOCK - 1 :]
        to_last.append(jnp.exp2(last - cum))
        wide = jnp.broadcast_to(last, (heads, dim))
        decay.append(jnp.exp2(wide))
        reached = reached + wide
        reached_ref[blk] = reached
        if blk == PAGE // BLOCK - 1:
            end_ref[size + 3 * heads :] = jnp.concatenate(split3(reached), axis=0)
    end_ref[size : size + 3 * heads] = jnp.concatenate(split3(reached), axis=0)
    for blk in range(blocks):
        copies[blk][0].wait()
        copies[blk][1].wait()
        here = slice(blk * BLOCK, (blk + 1) * BLOCK)
        for pair in range(heads // 2):
            scaled = []
            for head in (2 * pair, 2 * pair + 1):
                turned = keys[here, head * dim : (head + 1) * dim].T.astype(jnp.float32)
                scaled.append((turned * to_last[blk][head : head + 1]).astype(jnp.bfloat16))
            update = jnp.dot(
                jnp.concatenate(scaled, axis=0),
                values[here, 2 * pair * dim : 2 * (pair + 1) * dim],
                preferred_element_type=jnp.float32,
            )
            for which, head in enumerate((2 * pair, 2 * pair + 1)):
                rows = slice(head * dim, (head + 1) * dim)
                cols = slice(which * dim, (which + 1) * dim)
                state = update[cols, cols]
                if blk:
                    state = state + decay[blk][head : head + 1] * states_ref[blk - 1, rows]
                states_ref[blk, rows] = state
                if blk == PAGE // BLOCK - 1:
                    mid_ref[rows] = state.astype(jnp.bfloat16)
                if blk == blocks - 1:
                    end_ref[rows] = state.astype(jnp.bfloat16)


def in_hbm(value):
    return pltpu.with_memory_space_constraint(value, pltpu.HBM)


HBM = pl.BlockSpec(memory_space=pltpu.HBM)
VMEM = pl.BlockSpec(memory_space=pltpu.VMEM)
SMEM = pl.BlockSpec(memory_space=pltpu.SMEM)


def run_states(key_rows, value_rows, decay_log):
    tokens, width = key_rows.shape
    heads = decay_log.shape[0]
    dim = width // heads
    blocks = tokens // BLOCK
    size = heads * dim
    return pl.pallas_call(
        functools.partial(state_kernel, heads),
        in_specs=[HBM] * 3,
        out_specs=[VMEM] * 7,
        out_shape=[
            pltpu.VMEM((heads, tokens), jnp.float32),
            pltpu.VMEM((blocks, size, dim), jnp.float32),
            pltpu.VMEM((blocks, heads, dim), jnp.float32),
            pltpu.VMEM((size + 6 * heads, dim), jnp.bfloat16),
            pltpu.VMEM((size, dim), jnp.bfloat16),
            pltpu.VMEM((tokens, width), jnp.bfloat16),
            pltpu.VMEM((tokens, width), jnp.bfloat16),
        ],
        scratch_shapes=[pltpu.VMEM((heads, tokens), jnp.float32), pltpu.SemaphoreType.DMA((2 * blocks + 1,))],
        compiler_params=pltpu.CompilerParams(vmem_limit_bytes=8 * MIB),
        cost_estimate=SMALL,
        name="states",
    )(in_hbm(key_rows), in_hbm(value_rows), in_hbm(decay_log))


def pair_of(one, two):
    zero = jnp.zeros_like(one)
    return jnp.concatenate([jnp.concatenate([one, zero], axis=1), jnp.concatenate([zero, two], axis=1)], axis=0)


def inner_kernel(heads, first, keys, values, cum_ref, states_ref, reached_ref, *refs):
    blk = pl.program_id(0) + first
    if first:
        queries, _, _, out_ref, growth_ref, done_ref = refs
    else:
        query_hbm, out_ref, growth_ref, done_ref, queries, sems = refs
        blocks = queries.shape[0] // BLOCK

        def copy_of(part):
            rows = pl.ds(part * BLOCK, BLOCK)
            return pltpu.make_async_copy(query_hbm.at[rows], queries.at[rows], sems.at[part])

        @pl.when(blk == 0)
        def _():
            for part in range(blocks):
                copy_of(part).start()
            copy_of(0).wait()

        @pl.when(blk == 1)
        def _():
            for part in range(1, blocks):
                copy_of(part).wait()

    tokens, width = queries.shape
    dim = width // heads
    base = pl.multiple_of(blk * BLOCK, BLOCK)
    cum = cum_ref[:, pl.ds(base, BLOCK)]
    cum_cols = cum.T
    before = jnp.maximum(blk, 1) - 1
    reached = jnp.where(blk > 0, reached_ref[before], 0.0)
    causal = lax.broadcasted_iota(jnp.int32, (TILE, TILE), 0) >= lax.broadcasted_iota(jnp.int32, (TILE, TILE), 1)
    items = [(head, tile) for head in range(heads) for tile in range(BLOCK // TILE)]

    def rows_of(start, count):
        return pl.ds(pl.multiple_of(base + start, TILE), count)

    def scores_of(head, tile):
        lanes = slice(head * dim, (head + 1) * dim)
        return lax.dot_general(
            queries[rows_of(tile * TILE, TILE), lanes],
            keys[rows_of(0, (tile + 1) * TILE), lanes],
            NT,
            preferred_element_type=jnp.float32,
        )

    def carried_of(pair, tile):
        states = []
        for head in (2 * pair, 2 * pair + 1):
            state = states_ref[before, head * dim : (head + 1) * dim]
            states.append(jnp.where(blk > 0, state, 0.0).astype(jnp.bfloat16))
        query = queries[rows_of(tile * TILE, TILE), 2 * pair * dim : 2 * (pair + 1) * dim]
        return jnp.dot(query, pair_of(*states), preferred_element_type=jnp.float32)

    scores = scores_of(*items[0])
    carried = {}
    for number, (head, tile) in enumerate(items):
        ahead = scores_of(*items[number + 1]) if number + 1 < len(items) else None
        if head % 2 == 0:
            carried[tile] = carried_of(head // 2, tile)
        lanes = slice(head * dim, (head + 1) * dim)
        start, stop = tile * TILE, (tile + 1) * TILE
        column = jnp.broadcast_to(cum_cols[start:stop, head : head + 1], (TILE, dim))
        columns = jnp.concatenate([column] * (stop // dim), axis=1)
        weights = scores * jnp.exp2(columns - cum[head : head + 1, :stop])
        diagonal = jnp.where(causal, weights[:, start:], 0.0)
        weights = jnp.concatenate([weights[:, :start], diagonal], axis=1) if tile else diagonal
        local = jnp.dot(
            weights.astype(jnp.bfloat16), values[rows_of(0, stop), lanes], preferred_element_type=jnp.float32
        )
        which = head % 2
        local = local + carried[tile][:, which * dim : (which + 1) * dim] * jnp.exp2(column)
        out_ref[rows_of(start, TILE), lanes] = local
        growth_ref[rows_of(start, TILE), lanes] = jnp.exp2(column + reached[head : head + 1])
        scores = ahead
    done_ref[...] = cum[:, :128]


def run_inner(keys, values, cumulative, states, reached, first, count, queries, earlier=()):
    tokens, width = keys.shape
    heads = cumulative.shape[0]
    share = count * BLOCK
    made = pltpu.VMEM((tokens, width), jnp.float32)
    out_shape = [made, made, pltpu.VMEM((heads, 128), jnp.float32)]
    if not first:
        out_shape.append(pltpu.VMEM((tokens, width), jnp.bfloat16))
        queries = in_hbm(queries)
    return pl.pallas_call(
        functools.partial(inner_kernel, heads, first),
        grid=(count,),
        in_specs=[VMEM] * 5 + [VMEM if first else HBM] + [VMEM] * len(earlier),
        out_specs=[VMEM] * len(out_shape),
        out_shape=out_shape,
        scratch_shapes=[] if first else [pltpu.SemaphoreType.DMA((tokens // BLOCK,))],
        input_output_aliases={6: 0, 7: 1} if first else {},
        compiler_params=pltpu.CompilerParams(vmem_limit_bytes=8 * MIB),
        cost_estimate=SMALL,
        name="inner",
    )(keys, values, cumulative, states, reached, queries, *earlier)


def read_logs(ends, size, heads):
    whole, first = [], []
    for end in ends:
        parts = end[size:].astype(jnp.float32)
        whole.append(parts[:heads] + parts[heads : 2 * heads] + parts[2 * heads : 3 * heads])
        first.append(parts[3 * heads : 4 * heads] + parts[4 * heads : 5 * heads] + parts[5 * heads :])
    return whole, first


def gather_states(total, ends, places, logs, place, extra, heads, dim):
    factors = []
    for source in range(len(ends)):
        log = extra
        for other, other_log in enumerate(logs):
            between = (places[other] > places[source]) & (places[other] < place)
            log = log + jnp.where(between, other_log, 0.0)
        factors.append(jnp.where(places[source] < place, jnp.exp2(log), 0.0))
    for head in range(heads):
        rows = slice(head * dim, (head + 1) * dim)
        value = jnp.zeros((dim, dim), jnp.float32)
        for source, end in enumerate(ends):
            value += factors[source][head : head + 1] * end[rows].astype(jnp.float32)
        total[rows] = value


def with_entry(heads, here, inner_ref, growth_ref, queries, entry, use):
    dim = entry.shape[1]
    for pair in range(heads // 2):
        rows = [slice(head * dim, (head + 1) * dim) for head in (2 * pair, 2 * pair + 1)]
        carried = jnp.dot(
            queries[here, 2 * pair * dim : 2 * (pair + 1) * dim],
            pair_of(entry[rows[0]], entry[rows[1]]),
            preferred_element_type=jnp.float32,
        )
        for which, lanes in enumerate(rows):
            part = carried[:, which * dim : (which + 1) * dim]
            use(2 * pair + which, inner_ref[here, lanes] + part * growth_ref[here, lanes])


def finish_kernel(heads, inner_ref, growth_ref, queries, *refs):
    *ends, square_ref, entry_ref, entry = refs
    blk = pl.program_id(0)
    tokens, width = queries.shape
    dim = width // heads
    size = heads * dim

    @pl.when(blk == 0)
    def _():
        place = lax.axis_index("seq")
        logs, _unused = read_logs(ends, size, heads)
        places = [place ^ offset for offset in range(len(ends))]
        gather_states(entry, ends, places, logs, place, jnp.zeros((heads, dim), jnp.float32), heads, dim)
        entry_ref[...] = entry[...].astype(jnp.bfloat16)

    total = [jnp.zeros((BLOCK, dim), jnp.float32)]

    def use(head, out):
        total[0] = total[0] + out * out

    here = pl.ds(pl.multiple_of(blk * BLOCK, BLOCK), BLOCK)
    with_entry(heads, here, inner_ref, growth_ref, queries, entry_ref, use)
    high = total[0].astype(jnp.bfloat16)
    low = (total[0] - high.astype(jnp.float32)).astype(jnp.bfloat16)
    ones = jnp.ones((8, dim), jnp.bfloat16)
    sums = lax.dot_general(ones, high, NT, preferred_element_type=jnp.float32)
    sums = sums + lax.dot_general(ones, low, NT, preferred_element_type=jnp.float32)
    for row in range(BLOCK // 128):
        square_ref[pl.ds(blk * (BLOCK // 128) + row, 1)] = sums[:1, row * 128 : (row + 1) * 128]


def run_finish(inner, growth, queries, ends, heads):
    tokens, width = queries.shape
    dim = width // heads
    size = heads * dim
    return pl.pallas_call(
        functools.partial(finish_kernel, heads),
        grid=(tokens // BLOCK,),
        in_specs=[VMEM] * (3 + len(ends)),
        out_specs=[VMEM, VMEM],
        out_shape=[pltpu.VMEM((tokens // 128, 128), jnp.float32), pltpu.VMEM((size, dim), jnp.bfloat16)],
        scratch_shapes=[pltpu.VMEM((size, dim), jnp.float32)],
        compiler_params=pltpu.CompilerParams(vmem_limit_bytes=8 * MIB),
        cost_estimate=SMALL,
        name="finish",
    )(inner, growth, queries, *ends)


def scale_kernel(heads, whole_width, inner_ref, growth_ref, queries, entry, gain_ref, *refs):
    *squares, attended_ref = refs
    blk = pl.program_id(0)
    length, width = attended_ref.shape
    dim = width // heads
    scales = []
    for part in range(length // 128):
        row = pl.ds(blk * (length // 128) + part, 1)
        total = squares[0][row]
        for square in squares[1:]:
            total = total + square[row]
        scale = lax.rsqrt(total * (1.0 / whole_width) + 1e-06)
        scales.append(jnp.broadcast_to(jnp.broadcast_to(scale, (8, 128)).T[:, :1], (128, dim)))
    scale = jnp.concatenate(scales, axis=0)

    def use(head, out):
        lanes = slice(head * dim, (head + 1) * dim)
        attended_ref[:, lanes] = (out * scale * gain_ref[:, lanes]).astype(jnp.bfloat16)

    here = pl.ds(pl.multiple_of(blk * length, length), length)
    with_entry(heads, here, inner_ref, growth_ref, queries, entry, use)


def run_scale(inner, growth, queries, entry, gain, squares, whole_width, heads):
    tokens, width = inner.shape
    return pl.pallas_call(
        functools.partial(scale_kernel, heads, whole_width),
        grid=(tokens // BLOCK,),
        in_specs=[VMEM] * (5 + len(squares)),
        out_specs=pl.BlockSpec((BLOCK, width), lambda b: (b, 0)),
        out_shape=jax.ShapeDtypeStruct((tokens, width), jnp.bfloat16),
        compiler_params=pltpu.CompilerParams(vmem_limit_bytes=8 * MIB),
        cost_estimate=SMALL,
        name="scale",
    )(inner, growth, queries, entry, gain.reshape(1, width), *squares)


def cache_kernel(heads, count, owner_ref, *refs):
    ends, mids = refs[:count], refs[count : 2 * count]
    cache_ref, total, logs_ref, first_ref, page_of = refs[2 * count :]
    size, dim = mids[0].shape
    place = lax.axis_index("seq")
    places = [place ^ offset for offset in range(count)]
    whole, first = read_logs(ends, size, heads)
    for source in range(count):
        logs_ref[source] = whole[source]
        first_ref[source] = first[source]
    for slot in range(SLOTS):
        page_of[slot] = -1

    def look(page, found):
        mine = (owner_ref[page] == place) & (found < SLOTS)

        @pl.when(mine)
        def _():
            page_of[found] = page

        return found + mine.astype(jnp.int32)

    lax.fori_loop(0, owner_ref.shape[0], look, jnp.int32(0))

    def fill(slot, carry):
        page = page_of[slot]
        at_end = page % 2 == 1
        until = page // 2 + page % 2
        halfway = jnp.logical_not(at_end) & (page >= 0)

        @pl.when(page >= 0)
        def _():
            logs = [logs_ref[source] for source in range(count)]
            extra = jnp.zeros((heads, dim), jnp.float32)
            for source in range(count):
                extra = extra + jnp.where((places[source] == until) & halfway, first_ref[source], 0.0)
            gather_states(total, ends, places, logs, until, extra, heads, dim)

        @pl.when(page < 0)
        def _():
            total[...] = jnp.zeros_like(total)

        for source in range(count):

            @pl.when((places[source] == until) & halfway)
            def _():
                total[...] += mids[source][...].astype(jnp.float32)

        cache_ref[slot] = total[...].astype(jnp.bfloat16)
        return carry

    lax.fori_loop(0, SLOTS, fill, 0)


def run_cache(page_owner, ends, mids, heads):
    size, dim = mids[0].shape
    count = len(ends)
    return pl.pallas_call(
        functools.partial(cache_kernel, heads, count),
        in_specs=[SMEM] + [VMEM] * (2 * count),
        out_specs=VMEM,
        out_shape=jax.ShapeDtypeStruct((SLOTS, size, dim), jnp.bfloat16),
        scratch_shapes=[
            pltpu.VMEM((size, dim), jnp.float32),
            pltpu.VMEM((count, heads, dim), jnp.float32),
            pltpu.VMEM((count, heads, dim), jnp.float32),
            pltpu.SMEM((SLOTS,), jnp.int32),
        ],
        compiler_params=pltpu.CompilerParams(vmem_limit_bytes=12 * MIB),
        cost_estimate=SMALL,
        name="cache",
    )(page_owner, *ends, *mids)


def swap(value, axis, offset):
    return lax.ppermute(value, axis, [(place, place ^ offset) for place in range(lax.axis_size(axis))])


def tie(value, *after):
    return lax.optimization_barrier((value, *after))[0]


def add_kernel(one_ref, two_ref, sum_ref):
    sum_ref[...] = one_ref[...] + two_ref[...]


def add(one, two):
    return pl.pallas_call(
        add_kernel,
        in_specs=[VMEM, VMEM],
        out_specs=VMEM,
        out_shape=pltpu.VMEM(one.shape, one.dtype),
        compiler_params=pltpu.CompilerParams(vmem_limit_bytes=4 * MIB),
        cost_estimate=SMALL,
        name="add",
    )(one, two)


def shards(queries, key_rows, value_rows, decay_log, norm_gain, page_owner):
    tokens, width = queries.shape
    heads = decay_log.shape[0]
    dim = width // heads
    count = lax.axis_size("seq")
    half = tokens // BLOCK // 2
    cumulative, states, reached, end, mid, keys, values = run_states(key_rows, value_rows, decay_log)
    local = (keys, values, cumulative, states, reached)
    ends, mids = {0: end}, {0: mid}
    for offset in range(2, count, 2):
        ends[offset] = swap(end, "seq", offset)
    ends[1] = swap(end, "seq", 1)
    mids[1] = swap(mid, "seq", 1)
    inner, growth, done, held = run_inner(*local, 0, half, queries)
    mid = tie(mid, done, ends[1], mids[1])
    for offset in range(2, count, 2):
        mids[offset] = swap(mid, "seq", offset)
    inner, growth, done = run_inner(*local, half, half, held, (inner, growth))
    for offset in range(2, count, 2):
        ends[offset + 1] = swap(tie(ends[offset], done), "seq", 1)
    ends = [ends[offset] for offset in range(count)]
    square, entry = run_finish(inner, growth, held, ends, heads)
    offset = 1
    while offset < lax.axis_size("head"):
        square = add(square, swap(square, "head", offset))
        offset *= 2
    for offset in range(2, count, 2):
        mids[offset + 1] = swap(tie(mids[offset], square), "seq", 1)
    mids = [mids[offset] for offset in range(count)]
    attended = run_scale(inner, growth, held, entry, norm_gain, [square], width * lax.axis_size("head"), heads)
    page_cache = run_cache(page_owner, ends, mids, heads)
    return attended, page_cache.reshape(SLOTS, heads, dim, dim)


def solution(mesh):
    return jax.shard_map(
        shards,
        mesh=mesh,
        in_specs=(
            P("seq", "head"),
            P("seq", "head"),
            P("seq", "head"),
            P("head", "seq"),
            P("head"),
            P(),
        ),
        out_specs=(P("seq", "head"), P("seq", "head", None, None)),
        check_vma=False,
    )
```

time: 63.6 us -> 49.2 us (0.77)
  Pallas kernels: 35.4 us -> 29.5 us
  waiting for transfers between devices: 9.33 us -> 4.6 us
  starting transfers between devices: 17.5 us -> 14.7 us
  local copies, waits for them, and re-layouts: 0.84 us -> 0.01 us
    ppermute x17 -> x16, waiting for transfers between devices: 9.33 us -> 4.6 us  [swap(): lax.ppermute(value, axis, [(place, place ^ offset) for place in range(lax...]
    pallas_call x4 -> x6, Pallas kernels: 20.5 us -> 16.3 us  [the longest x1 4.82 us: run_cache(): pl.pallas_call(functools.partial(cache_kernel, heads, count), in_specs=[S...]
    ppermute x17 -> x16, starting transfers between devices: 17.5 us -> 14.7 us  [swap(): lax.ppermute(value, axis, [(place, place ^ offset) for place in range(lax...]
    pallas_call x2, Pallas kernels: 15 us -> 13.2 us  [run_inner(): pl.pallas_call(functools.partial(inner_kernel, heads, first), grid=(count...]
    unnamed x6 -> x4, local copies, waits for them, and re-layouts: 0.84 us -> 0.01 us
  transfers between devices with their start and end apart: 17 -> 16, of which waited for: 4 -> 4; matrix products, arithmetic and copies ran while one was open for 0% -> 0% of each run, Pallas kernels for 41% -> 41%
where the time goes in v3:
time: 49.2 us; the launch traced here: 49.5 us
  Pallas kernels  29.5 us (60%)
  starting transfers between devices  14.7 us (30%)
  waiting for transfers between devices  4.6 us (9%)
  between operations  0.69 us (1%)
    ppermute x16, starting transfers between devices, swap(): lax.ppermute(value, axis, [(place, place ^ offset) for place in range(lax...  14.7 us
    pallas_call x2, Pallas kernels, run_inner(): pl.pallas_call(functools.partial(inner_kernel, heads, first), grid=(count...  13.2 us
    pallas_call x1, Pallas kernels, run_cache(): pl.pallas_call(functools.partial(cache_kernel, heads, count), in_specs=[S...  4.82 us
    ppermute x16, waiting for transfers between devices, swap(): lax.ppermute(value, axis, [(place, place ^ offset) for place in range(lax...  4.6 us
    pallas_call x1, Pallas kernels, run_states(): pl.pallas_call(functools.partial(state_kernel, heads), in_specs=[HBM] * 3...  4.23 us
    pallas_call x1, Pallas kernels, run_scale(): pl.pallas_call(functools.partial(scale_kernel, heads, whole_width), grid=...  4.02 us
    pallas_call x1, Pallas kernels, run_finish(): pl.pallas_call(functools.partial(finish_kernel, heads), grid=(tokens // B...  3.21 us
  transfers between devices with their start and end apart: 16, of which 4 were waited for; matrix products, arithmetic and copies ran while one was open for 0% of the time, Pallas kernels for 41%

profile of v3, /device:TPU:0, one launch (start us, length us, event | category | flops | bytes accessed | tf_op | source)
XLA Modules:
  0.0 49.5 jit_solution(8707914160232053712)
XLA Ops:
  0.6 4.2 %states.1 = (f32[8,2048]{1,0:T(8,128)S(1)}, f32[4,1024,128]{2,1,0:T(8,128)S(1)}, f32[4,8,128]{2,1,0:T(8,128)S(1)}, bf16[1072,128]{1,0:T(8,128)(2,1)S(1)}, bf16[1...) custom-call(bf16[2048,1024]{1,0:T(8,128)(2,1)} %key_hbm.1, ...), custom_call_target="tpu_custom_call" | custom-call | flops 1 | bytes 1 | tf_op jit(solution)/shard_map/states/pallas_call | solution.py:114
  4.9 4.0 %collective-permute-start.5 = (bf16[1072,128]{1,0:T(8,128)(2,1)S(1)}, bf16[1072,128]{1,0:T(8,128)(2,1)S(1)}, u32[]{:S(2)}, u32[]{:S(2)}) collective-permute-start(bf16[1072,128]{1,0:T(8,128)(2,1)S(1)} %get-tuple-element.34.refs_0_), channel_id=1, source_target_pairs={{0,24},{4,28},{8,16},{12,20},{16,8},{20,12},{24,0},{28,4},{1,25},{... | collective-permute-start | bytes 823304 | tf_op jit(solution)/shard_map/ppermute | solution.py:438
  8.8 0.5 %collective-permute-start.3 = (bf16[1072,128]{1,0:T(8,128)(2,1)S(1)}, bf16[1072,128]{1,0:T(8,128)(2,1)S(1)}, u32[]{:S(2)}, u32[]{:S(2)}) collective-permute-start(bf16[1072,128]{1,0:T(8,128)(2,1)S(1)} %get-tuple-element.34.refs_0_), channel_id=1, source_target_pairs={{0,16},{4,20},{8,24},{12,28},{16,0},{20,4},{24,8},{28,12},{1,17},{... | collective-permute-start | bytes 823304 | tf_op jit(solution)/shard_map/ppermute | solution.py:438
  9.3 0.1 collective-permute-start.1
  9.5 0.0 collective-permute-start
  9.5 7.2 %inner.2 = (f32[2048,1024]{1,0:T(8,128)S(1)}, f32[2048,1024]{1,0:T(8,128)S(1)}, f32[8,128]{1,0:T(8,128)}, bf16[2048,1024]{1,0:T(8,128)(2,1)S(1)}) custom-call(bf16[2048,1024]{1,0:T(8,128)(2,1)S(1)} %get-tuple-element.24.keys, bf16[2048,1024]{1,0:T(8,128)(2,1)S(1)} %get-tuple-element.25.values, f32[8,2048]{1,0:T(8,128)S(1)} %get-tuple-element.26.cum_ref, ...), custom_call_target="tpu_custom_call" | custom-call | flops 1 | bytes 1 | tf_op jit(solution)/shard_map/inner/pallas_call | solution.py:225
  16.7 6.0 %inner.3 = (f32[2048,1024]{1,0:T(8,128)S(1)}, f32[2048,1024]{1,0:T(8,128)S(1)}, f32[8,128]{1,0:T(8,128)}) custom-call(bf16[2048,1024]{1,0:T(8,128)(2,1)S(1)} %get-tuple-element.24.keys, bf16[2048,1024]{1,0:T(8,128)(2,1)S(1)} %get-tuple-element.25.values, f32[8,2048]{1,0:T(8,128)S(1)} %get-tuple-element.26.cum_ref, ...), custom_call_target="tpu_custom_call", output_to_operand_aliasing={{0}: (6, {}), {1}: (7, {})} | custom-call | flops 1 | bytes 1 | tf_op jit(solution)/shard_map/inner/pallas_call | solution.py:225
  22.7 0.0 collective-permute-done.5.refs_6_
  22.7 0.5 %collective-permute-start.6 = (bf16[1072,128]{1,0:T(8,128)(2,1)S(1)}, bf16[1072,128]{1,0:T(8,128)(2,1)S(1)}, u32[]{:S(2)}, u32[]{:S(2)}) collective-permute-start(bf16[1072,128]{1,0:T(8,128)(2,1)S(1)} %collective-permute-done.5.refs_6_), channel_id=1, source_target_pairs={{0,4},{4,0},{8,12},{12,8},{16,20},{20,16},{24,28},{28,24},{1,5},{5... | collective-permute-start | bytes 823304 | tf_op jit(solution)/shard_map/ppermute | solution.py:438
  23.2 0.0 collective-permute-start.9
  23.2 0.0 collective-permute-done.3.refs_4_
  23.2 0.5 %collective-permute-start.4 = (bf16[1072,128]{1,0:T(8,128)(2,1)S(1)}, bf16[1072,128]{1,0:T(8,128)(2,1)S(1)}, u32[]{:S(2)}, u32[]{:S(2)}) collective-permute-start(bf16[1072,128]{1,0:T(8,128)(2,1)S(1)} %collective-permute-done.3.refs_4_), channel_id=1, source_target_pairs={{0,4},{4,0},{8,12},{12,8},{16,20},{20,16},{24,28},{28,24},{1,5},{5... | collective-permute-start | bytes 823304 | tf_op jit(solution)/shard_map/ppermute | solution.py:438
  23.7 0.0 collective-permute-done.1.refs_2_
  23.7 0.1 collective-permute-start.2
  23.8 1.0 %collective-permute-done.9.refs_9_ = bf16[1024,128]{1,0:T(8,128)(2,1)S(1)} collective-permute-done((bf16[1024,128]{1,0:T(8,128)(2,1)S(1)}, bf16[1024,128]{1,0:T(8,128)(2,1)S(1)}, u32[]{:S(2)}, u32[]{:S(2)}) %collective-permute-start.9) | collective-permute-done | bytes 262176 | tf_op jit(solution)/shard_map/ppermute | solution.py:438
  24.8 0.0 collective-permute-done.refs_1_
  24.8 2.8 %collective-permute-start.14 = (bf16[1024,128]{1,0:T(8,128)(2,1)S(1)}, bf16[1024,128]{1,0:T(8,128)(2,1)S(1)}, u32[]{:S(2)}, u32[]{:S(2)}) collective-permute-start(bf16[1024,128]{1,0:T(8,128)(2,1)S(1)} %get-tuple-element.42.refs_8_), channel_id=1, source_target_pairs={{0,24},{4,28},{8,16},{12,20},{16,8},{20,12},{24,0},{28,4},{1,25},{... | collective-permute-start | bytes 786440 | tf_op jit(solution)/shard_map/ppermute | solution.py:438
  27.6 0.5 %collective-permute-start.12 = (bf16[1024,128]{1,0:T(8,128)(2,1)S(1)}, bf16[1024,128]{1,0:T(8,128)(2,1)S(1)}, u32[]{:S(2)}, u32[]{:S(2)}) collective-permute-start(bf16[1024,128]{1,0:T(8,128)(2,1)S(1)} %get-tuple-element.42.refs_8_), channel_id=1, source_target_pairs={{0,16},{4,20},{8,24},{12,28},{16,0},{20,4},{24,8},{28,12},{1,17},{... | collective-permute-start | bytes 786440 | tf_op jit(solution)/shard_map/ppermute | solution.py:438
  28.1 0.0 collective-permute-done.6.refs_7_
  28.1 0.2 collective-permute-start.10
  28.3 0.0 collective-permute-done.4.refs_5_
  28.3 0.0 collective-permute-done.2.refs_3_
  28.3 0.0 copy-start
  28.3 3.2 %finish.1 = (f32[16,128]{1,0:T(8,128)S(1)}, bf16[1024,128]{1,0:T(8,128)(2,1)S(1)}) custom-call(f32[2048,1024]{1,0:T(8,128)S(1)} %get-tuple-element.32.inner_ref, f32[2048,1024]{1,0:T(8,128)S(1)} %get-tuple-element.33.growth_ref, bf16[2048,1024]{1,0:T(8,128)(2,1)S(1)} %get-tuple-element.29.refs_0_.queries, bf16[1072,128]{1,0:T(8,128)(2,1)S(1)} %get-tuple-element.34.refs_0_, ...), custom_call_target="tpu_custom_call" | custom-call | flops 1 | bytes 1 | tf_op jit(solution)/shard_map/finish/pallas_call | solution.py:313
  31.5 2.0 %collective-permute-start.7 = (f32[16,128]{1,0:T(8,128)S(1)}, f32[16,128]{1,0:T(8,128)S(1)}, u32[]{:S(2)}, u32[]{:S(2)}) collective-permute-start(f32[16,128]{1,0:T(8,128)S(1)} %get-tuple-element.40.one_ref), channel_id=1, source_target_pairs={{0,1},{1,0},{2,3},{3,2},{4,5},{5,4},{6,7},{7,6},{8,9},{9,8},{10,11... | collective-permute-start | bytes 24584 | tf_op jit(solution)/shard_map/ppermute | solution.py:438
  33.5 1.7 %collective-permute-done.7.two_ref = f32[16,128]{1,0:T(8,128)S(1)} collective-permute-done((f32[16,128]{1,0:T(8,128)S(1)}, f32[16,128]{1,0:T(8,128)S(1)}, u32[]{:S(2)}, u32[]{:S(2)}) %collective-permute-start.7) | collective-permute-done | bytes 8224 | tf_op jit(solution)/shard_map/ppermute | solution.py:438
  35.2 3.0 %collective-permute-start.8 = (f32[16,128]{1,0:T(8,128)S(1)}, f32[16,128]{1,0:T(8,128)S(1)}, u32[]{:S(2)}, u32[]{:S(2)}) collective-permute-start(f32[16,128]{1,0:T(8,128)S(1)} %add.2.one_ref), channel_id=1, source_target_pairs={{0,2},{1,3},{2,0},{3,1},{4,6},{5,7},{6,4},{7,5},{8,10},{9,11},{10,... | collective-permute-start | bytes 24584 | tf_op jit(solution)/shard_map/ppermute | solution.py:438
  38.2 1.6 %collective-permute-done.8.two_ref = f32[16,128]{1,0:T(8,128)S(1)} collective-permute-done((f32[16,128]{1,0:T(8,128)S(1)}, f32[16,128]{1,0:T(8,128)S(1)}, u32[]{:S(2)}, u32[]{:S(2)}) %collective-permute-start.8) | collective-permute-done | bytes 8224 | tf_op jit(solution)/shard_map/ppermute | solution.py:438
  39.8 0.0 collective-permute-done.14.refs_14_
  39.8 0.0 collective-permute-start.15
  39.8 0.2 collective-permute-done.12.refs_12_
  40.1 0.3 collective-permute-start.13
  40.3 0.0 collective-permute-done.10.refs_10_
  40.4 0.2 collective-permute-start.11
  40.6 0.0 copy-done
  40.6 0.0 copy-start.1
  40.6 4.0 %scale.1 = bf16[2048,1024]{1,0:T(8,128)(2,1)} custom-call(f32[2048,1024]{1,0:T(8,128)S(1)} %get-tuple-element.32.inner_ref, f32[2048,1024]{1,0:T(8,128)S(1)} %get-tuple-element.33.growth_ref, bf16[2048,1024]{1,0:T(8,128)(2,1)S(1)} %get-tuple-element.29.refs_0_.queries, bf16[1024,128]{1,0:T(8,128)(2,1)S(1)} %get-tuple-element.39.entry, ...), custom_call_target="tpu_custom_call" | custom-call | flops 1 | bytes 1 | tf_op jit(solution)/shard_map/scale/pallas_call | solution.py:351
  44.6 0.0 collective-permute-done.15.refs_15_
  44.6 0.0 collective-permute-done.13.refs_13_
  44.6 0.0 collective-permute-done.11.refs_11_
  44.6 0.0 copy-done.1
  44.6 4.8 %cache.1 = bf16[5,1024,128]{2,1,0:T(8,128)(2,1)} custom-call(s32[16]{0:T(128)S(1)} %copy-done.1, bf16[1072,128]{1,0:T(8,128)(2,1)S(1)} %get-tuple-element.34.refs_0_, bf16[1072,128]{1,0:T(8,128)(2,1)S(1)} %collective-permute-done.refs_1_, bf16[1072,128]{1,0:T(8,128)(2,1)S(1)} %collective-permute-done.1.refs_2_, ...), custom_call_target="tpu_custom_call" | custom-call | flops 1 | bytes 1 | tf_op jit(solution)/shard_map/cache/pallas_call | solution.py:420
  (2 shorter events, 0.0 us)
Async XLA Ops:
  4.9 17.8 %collective-permute-start.5 = (bf16[1072,128]{1,0:T(8,128)(2,1)S(1)}, bf16[1072,128]{1,0:T(8,128)(2,1)S(1)}, u32[]{:S(2)}, u32[]{:S(2)}) collective-permute-start(bf16[1072,128]{1,0:T(8,128)(2,1)S(1)} %get-tuple-element.34.refs_0_), channel_id=1, source_target_pairs={{0,24},{4,28},{8,16},{12,20},{16,8},{20,12},{24,0},{28,4},{1,25},{... | collective-permute-start | bytes 823304 | tf_op jit(solution)/shard_map/ppermute | solution.py:438
  8.8 14.4 %collective-permute-start.3 = (bf16[1072,128]{1,0:T(8,128)(2,1)S(1)}, bf16[1072,128]{1,0:T(8,128)(2,1)S(1)}, u32[]{:S(2)}, u32[]{:S(2)}) collective-permute-start(bf16[1072,128]{1,0:T(8,128)(2,1)S(1)} %get-tuple-element.34.refs_0_), channel_id=1, source_target_pairs={{0,16},{4,20},{8,24},{12,28},{16,0},{20,4},{24,8},{28,12},{1,17},{... | collective-permute-start | bytes 823304 | tf_op jit(solution)/shard_map/ppermute | solution.py:438
  9.3 14.4 %collective-permute-start.1 = (bf16[1072,128]{1,0:T(8,128)(2,1)S(1)}, bf16[1072,128]{1,0:T(8,128)(2,1)S(1)}, u32[]{:S(2)}, u32[]{:S(2)}) collective-permute-start(bf16[1072,128]{1,0:T(8,128)(2,1)S(1)} %get-tuple-element.34.refs_0_), channel_id=1, source_target_pairs={{0,8},{4,12},{8,0},{12,4},{16,24},{20,28},{24,16},{28,20},{1,9},{5... | collective-permute-start | bytes 823304 | tf_op jit(solution)/shard_map/ppermute | solution.py:438
  9.5 15.3 %collective-permute-start = (bf16[1072,128]{1,0:T(8,128)(2,1)S(1)}, bf16[1072,128]{1,0:T(8,128)(2,1)S(1)}, u32[]{:S(2)}, u32[]{:S(2)}) collective-permute-start(bf16[1072,128]{1,0:T(8,128)(2,1)S(1)} %get-tuple-element.34.refs_0_), channel_id=1, source_target_pairs={{0,4},{4,0},{8,12},{12,8},{16,20},{20,16},{24,28},{28,24},{1,5},{5... | collective-permute-start | bytes 823304 | tf_op jit(solution)/shard_map/ppermute | solution.py:438
  22.7 5.4 %collective-permute-start.6 = (bf16[1072,128]{1,0:T(8,128)(2,1)S(1)}, bf16[1072,128]{1,0:T(8,128)(2,1)S(1)}, u32[]{:S(2)}, u32[]{:S(2)}) collective-permute-start(bf16[1072,128]{1,0:T(8,128)(2,1)S(1)} %collective-permute-done.5.refs_6_), channel_id=1, source_target_pairs={{0,4},{4,0},{8,12},{12,8},{16,20},{20,16},{24,28},{28,24},{1,5},{5... | collective-permute-start | bytes 823304 | tf_op jit(solution)/shard_map/ppermute | solution.py:438
  23.2 1.6 %collective-permute-start.9 = (bf16[1024,128]{1,0:T(8,128)(2,1)S(1)}, bf16[1024,128]{1,0:T(8,128)(2,1)S(1)}, u32[]{:S(2)}, u32[]{:S(2)}) collective-permute-start(bf16[1024,128]{1,0:T(8,128)(2,1)S(1)} %get-tuple-element.42.refs_8_), channel_id=1, source_target_pairs={{0,4},{4,0},{8,12},{12,8},{16,20},{20,16},{24,28},{28,24},{1,5},{5... | collective-permute-start | bytes 786440 | tf_op jit(solution)/shard_map/ppermute | solution.py:438
  23.2 5.1 %collective-permute-start.4 = (bf16[1072,128]{1,0:T(8,128)(2,1)S(1)}, bf16[1072,128]{1,0:T(8,128)(2,1)S(1)}, u32[]{:S(2)}, u32[]{:S(2)}) collective-permute-start(bf16[1072,128]{1,0:T(8,128)(2,1)S(1)} %collective-permute-done.3.refs_4_), channel_id=1, source_target_pairs={{0,4},{4,0},{8,12},{12,8},{16,20},{20,16},{24,28},{28,24},{1,5},{5... | collective-permute-start | bytes 823304 | tf_op jit(solution)/shard_map/ppermute | solution.py:438
  23.7 4.6 %collective-permute-start.2 = (bf16[1072,128]{1,0:T(8,128)(2,1)S(1)}, bf16[1072,128]{1,0:T(8,128)(2,1)S(1)}, u32[]{:S(2)}, u32[]{:S(2)}) collective-permute-start(bf16[1072,128]{1,0:T(8,128)(2,1)S(1)} %collective-permute-done.1.refs_2_), channel_id=1, source_target_pairs={{0,4},{4,0},{8,12},{12,8},{16,20},{20,16},{24,28},{28,24},{1,5},{5... | collective-permute-start | bytes 823304 | tf_op jit(solution)/shard_map/ppermute | solution.py:438
  24.8 15.0 %collective-permute-start.14 = (bf16[1024,128]{1,0:T(8,128)(2,1)S(1)}, bf16[1024,128]{1,0:T(8,128)(2,1)S(1)}, u32[]{:S(2)}, u32[]{:S(2)}) collective-permute-start(bf16[1024,128]{1,0:T(8,128)(2,1)S(1)} %get-tuple-element.42.refs_8_), channel_id=1, source_target_pairs={{0,24},{4,28},{8,16},{12,20},{16,8},{20,12},{24,0},{28,4},{1,25},{... | collective-permute-start | bytes 786440 | tf_op jit(solution)/shard_map/ppermute | solution.py:438
  27.6 12.4 %collective-permute-start.12 = (bf16[1024,128]{1,0:T(8,128)(2,1)S(1)}, bf16[1024,128]{1,0:T(8,128)(2,1)S(1)}, u32[]{:S(2)}, u32[]{:S(2)}) collective-permute-start(bf16[1024,128]{1,0:T(8,128)(2,1)S(1)} %get-tuple-element.42.refs_8_), channel_id=1, source_target_pairs={{0,16},{4,20},{8,24},{12,28},{16,0},{20,4},{24,8},{28,12},{1,17},{... | collective-permute-start | bytes 786440 | tf_op jit(solution)/shard_map/ppermute | solution.py:438
  28.1 12.2 %collective-permute-start.10 = (bf16[1024,128]{1,0:T(8,128)(2,1)S(1)}, bf16[1024,128]{1,0:T(8,128)(2,1)S(1)}, u32[]{:S(2)}, u32[]{:S(2)}) collective-permute-start(bf16[1024,128]{1,0:T(8,128)(2,1)S(1)} %get-tuple-element.42.refs_8_), channel_id=1, source_target_pairs={{0,8},{4,12},{8,0},{12,4},{16,24},{20,28},{24,16},{28,20},{1,9},{5... | collective-permute-start | bytes 786440 | tf_op jit(solution)/shard_map/ppermute | solution.py:438
  28.3 12.3 %copy-start = (f32[1024]{0:T(1024)S(1)}, f32[1024]{0:T(1024)}, u32[]{:S(2)}) copy-start(f32[1024]{0:T(1024)} %param.10) | copy-start | bytes 12292
  31.5 3.7 %collective-permute-start.7 = (f32[16,128]{1,0:T(8,128)S(1)}, f32[16,128]{1,0:T(8,128)S(1)}, u32[]{:S(2)}, u32[]{:S(2)}) collective-permute-start(f32[16,128]{1,0:T(8,128)S(1)} %get-tuple-element.40.one_ref), channel_id=1, source_target_pairs={{0,1},{1,0},{2,3},{3,2},{4,5},{5,4},{6,7},{7,6},{8,9},{9,8},{10,11... | collective-permute-start | bytes 24584 | tf_op jit(solution)/shard_map/ppermute | solution.py:438
  35.2 4.6 %collective-permute-start.8 = (f32[16,128]{1,0:T(8,128)S(1)}, f32[16,128]{1,0:T(8,128)S(1)}, u32[]{:S(2)}, u32[]{:S(2)}) collective-permute-start(f32[16,128]{1,0:T(8,128)S(1)} %add.2.one_ref), channel_id=1, source_target_pairs={{0,2},{1,3},{2,0},{3,1},{4,6},{5,7},{6,4},{7,5},{8,10},{9,11},{10,... | collective-permute-start | bytes 24584 | tf_op jit(solution)/shard_map/ppermute | solution.py:438
  39.8 4.8 %collective-permute-start.15 = (bf16[1024,128]{1,0:T(8,128)(2,1)S(1)}, bf16[1024,128]{1,0:T(8,128)(2,1)S(1)}, u32[]{:S(2)}, u32[]{:S(2)}) collective-permute-start(bf16[1024,128]{1,0:T(8,128)(2,1)S(1)} %collective-permute-done.14.refs_14_), channel_id=1, source_target_pairs={{0,4},{4,0},{8,12},{12,8},{16,20},{20,16},{24,28},{28,24},{1,5},{5... | collective-permute-start | bytes 786440 | tf_op jit(solution)/shard_map/ppermute | solution.py:438
  40.1 4.5 %collective-permute-start.13 = (bf16[1024,128]{1,0:T(8,128)(2,1)S(1)}, bf16[1024,128]{1,0:T(8,128)(2,1)S(1)}, u32[]{:S(2)}, u32[]{:S(2)}) collective-permute-start(bf16[1024,128]{1,0:T(8,128)(2,1)S(1)} %collective-permute-done.12.refs_12_), channel_id=1, source_target_pairs={{0,4},{4,0},{8,12},{12,8},{16,20},{20,16},{24,28},{28,24},{1,5},{5... | collective-permute-start | bytes 786440 | tf_op jit(solution)/shard_map/ppermute | solution.py:438
  40.4 4.2 %collective-permute-start.11 = (bf16[1024,128]{1,0:T(8,128)(2,1)S(1)}, bf16[1024,128]{1,0:T(8,128)(2,1)S(1)}, u32[]{:S(2)}, u32[]{:S(2)}) collective-permute-start(bf16[1024,128]{1,0:T(8,128)(2,1)S(1)} %collective-permute-done.10.refs_10_), channel_id=1, source_target_pairs={{0,4},{4,0},{8,12},{12,8},{16,20},{20,16},{24,28},{28,24},{1,5},{5... | collective-permute-start | bytes 786440 | tf_op jit(solution)/shard_map/ppermute | solution.py:438
  40.6 4.0 %copy-start.1 = (s32[16]{0:T(128)S(1)}, s32[16]{0:T(128)}, u32[]{:S(2)}) copy-start(s32[16]{0:T(128)} %owner_ref.1) | copy-start | bytes 196

commit v4 on v3

v4 whole, which is shorter than its diff:
```python
import functools
import math

import jax
import jax.numpy as jnp
from jax import lax
from jax.experimental import pallas as pl
from jax.experimental.pallas import tpu as pltpu
from jax.sharding import PartitionSpec as P

BLOCK = 256
ROWS = 512
PAGE = 1024
SLOTS = 5
LOG2E = math.log2(math.e)
MIB = 1 << 20
SMALL = pl.CostEstimate(flops=1, bytes_accessed=1, transcendentals=0)

NT = (((1,), (1,)), ((), ()))
TN = (((0,), (0,)), ((), ()))


def split3(x):
    high = x.astype(jnp.bfloat16)
    rest = x - high.astype(jnp.float32)
    middle = rest.astype(jnp.bfloat16)
    low = (rest - middle.astype(jnp.float32)).astype(jnp.bfloat16)
    return high, middle, low


def state_kernel(heads, key_hbm, value_hbm, decay_hbm, cum_ref, states_ref, reached_ref, end_ref, mid_ref, keys, values, decays, running, sems):
    tokens, width = keys.shape
    dim = width // heads
    size = heads * dim
    blocks = tokens // BLOCK
    decay_copy = pltpu.make_async_copy(decay_hbm, decays, sems.at[2 * blocks])
    decay_copy.start()
    copies = []
    for blk in range(blocks):
        rows = pl.ds(blk * BLOCK, BLOCK)
        copies.append(
            (
                pltpu.make_async_copy(key_hbm.at[rows], keys.at[rows], sems.at[2 * blk]),
                pltpu.make_async_copy(value_hbm.at[rows], values.at[rows], sems.at[2 * blk + 1]),
            )
        )
        copies[-1][0].start()
        copies[-1][1].start()
    upper = jnp.where(
        lax.broadcasted_iota(jnp.int32, (BLOCK, BLOCK), 0) <= lax.broadcasted_iota(jnp.int32, (BLOCK, BLOCK), 1), 1.0, 0.0
    ).astype(jnp.bfloat16)
    decay_copy.wait()
    parts = [
        part for blk in range(blocks) for part in split3(decays[:, blk * BLOCK : (blk + 1) * BLOCK] * LOG2E)
    ]
    sums = jnp.dot(jnp.concatenate(parts, axis=0), upper, preferred_element_type=jnp.float32)
    to_last, decay = [], []
    reached = jnp.zeros((heads, dim), jnp.float32)
    for blk in range(blocks):
        base = 3 * heads * blk
        cum = sums[base : base + heads] + sums[base + heads : base + 2 * heads] + sums[base + 2 * heads : base + 3 * heads]
        cum_ref[:, blk * BLOCK : (blk + 1) * BLOCK] = cum
        last = cum[:, BLOCK - 1 :]
        to_last.append(jnp.exp2(last - cum))
        wide = jnp.broadcast_to(last, (heads, dim))
        decay.append(jnp.exp2(wide))
        reached = reached + wide
        reached_ref[blk] = reached
        if blk == PAGE // BLOCK - 1:
            end_ref[size + 3 * heads :] = jnp.concatenate(split3(reached), axis=0)
    end_ref[size : size + 3 * heads] = jnp.concatenate(split3(reached), axis=0)
    for blk in range(blocks):
        copies[blk][0].wait()
        copies[blk][1].wait()
        here = slice(blk * BLOCK, (blk + 1) * BLOCK)
        for pair in range(heads // 2):
            scaled = []
            for head in (2 * pair, 2 * pair + 1):
                turned = keys[here, head * dim : (head + 1) * dim].T.astype(jnp.float32)
                scaled.append((turned * to_last[blk][head : head + 1]).astype(jnp.bfloat16))
            update = jnp.dot(
                jnp.concatenate(scaled, axis=0),
                values[here, 2 * pair * dim : 2 * (pair + 1) * dim],
                preferred_element_type=jnp.float32,
            )
            for which, head in enumerate((2 * pair, 2 * pair + 1)):
                rows = slice(head * dim, (head + 1) * dim)
                cols = slice(which * dim, (which + 1) * dim)
                state = update[cols, cols]
                if blk:
                    state = state + decay[blk][head : head + 1] * running[rows]
                running[rows] = state
                states_ref[blk, rows] = state.astype(jnp.bfloat16)
                if blk == PAGE // BLOCK - 1:
                    mid_ref[rows] = state.astype(jnp.bfloat16)
                if blk == blocks - 1:
                    end_ref[rows] = state.astype(jnp.bfloat16)


def in_hbm(value):
    return pltpu.with_memory_space_constraint(value, pltpu.HBM)


HBM = pl.BlockSpec(memory_space=pltpu.HBM)
VMEM = pl.BlockSpec(memory_space=pltpu.VMEM)
SMEM = pl.BlockSpec(memory_space=pltpu.SMEM)


def run_states(key_rows, value_rows, decay_log):
    tokens, width = key_rows.shape
    heads = decay_log.shape[0]
    dim = width // heads
    blocks = tokens // BLOCK
    size = heads * dim
    return pl.pallas_call(
        functools.partial(state_kernel, heads),
        in_specs=[HBM] * 3,
        out_specs=[VMEM] * 7,
        out_shape=[
            pltpu.VMEM((heads, tokens), jnp.float32),
            pltpu.VMEM((blocks, size, dim), jnp.bfloat16),
            pltpu.VMEM((blocks, heads, dim), jnp.float32),
            pltpu.VMEM((size + 6 * heads, dim), jnp.bfloat16),
            pltpu.VMEM((size, dim), jnp.bfloat16),
            pltpu.VMEM((tokens, width), jnp.bfloat16),
            pltpu.VMEM((tokens, width), jnp.bfloat16),
        ],
        scratch_shapes=[
            pltpu.VMEM((heads, tokens), jnp.float32),
            pltpu.VMEM((size, dim), jnp.float32),
            pltpu.SemaphoreType.DMA((2 * blocks + 1,)),
        ],
        compiler_params=pltpu.CompilerParams(vmem_limit_bytes=8 * MIB),
        cost_estimate=SMALL,
        name="states",
    )(in_hbm(key_rows), in_hbm(value_rows), in_hbm(decay_log))


def pair_of(one, two):
    zero = jnp.zeros_like(one)
    return jnp.concatenate([jnp.concatenate([one, zero], axis=1), jnp.concatenate([zero, two], axis=1)], axis=0)


def inner_kernel(heads, keys, values, queries, cum_ref, states_ref, reached_ref, out_ref, growth_ref, done_ref):
    step = pl.program_id(0)
    width = queries.shape[1]
    dim = width // heads
    causal = lax.broadcasted_iota(jnp.int32, (BLOCK, BLOCK), 0) >= lax.broadcasted_iota(jnp.int32, (BLOCK, BLOCK), 1)
    blks = [step * (ROWS // BLOCK) + part for part in range(ROWS // BLOCK)]
    here = [pl.ds(pl.multiple_of(blk * BLOCK, BLOCK), BLOCK) for blk in blks]
    before = [jnp.maximum(blk, 1) - 1 for blk in blks]
    cums = [cum_ref[:, rows] for rows in here]
    cum_cols = [cum.T for cum in cums]
    reached = [jnp.where(blk > 0, reached_ref[last], 0.0) for blk, last in zip(blks, before)]
    items = [(head, part) for head in range(heads) for part in range(len(blks))]

    def scores_of(head, part):
        lanes = slice(head * dim, (head + 1) * dim)
        return lax.dot_general(queries[here[part], lanes], keys[here[part], lanes], NT, preferred_element_type=jnp.float32)

    def carried_of(pair, part):
        states = []
        for head in (2 * pair, 2 * pair + 1):
            state = states_ref[before[part], head * dim : (head + 1) * dim]
            states.append(jnp.where(blks[part] > 0, state, jnp.zeros_like(state)))
        query = queries[here[part], 2 * pair * dim : 2 * (pair + 1) * dim]
        return jnp.dot(query, pair_of(*states), preferred_element_type=jnp.float32)

    scores = scores_of(*items[0])
    carried = {}
    for number, (head, part) in enumerate(items):
        ahead = scores_of(*items[number + 1]) if number + 1 < len(items) else None
        if head % 2 == 0:
            carried[part] = carried_of(head // 2, part)
        lanes = slice(head * dim, (head + 1) * dim)
        column = jnp.broadcast_to(cum_cols[part][:, head : head + 1], (BLOCK, dim))
        columns = jnp.concatenate([column] * (BLOCK // dim), axis=1)
        weights = jnp.where(causal, scores * jnp.exp2(columns - cums[part][head : head + 1]), 0.0)
        local = jnp.dot(weights.astype(jnp.bfloat16), values[here[part], lanes], preferred_element_type=jnp.float32)
        which = head % 2
        local = local + carried[part][:, which * dim : (which + 1) * dim] * jnp.exp2(column)
        out_ref[here[part], lanes] = local
        growth_ref[here[part], lanes] = jnp.exp2(column + reached[part][head : head + 1])
        scores = ahead
    done_ref[...] = cums[0][:, :128]


def run_inner(keys, values, queries, cumulative, states, reached):
    tokens, width = keys.shape
    heads = cumulative.shape[0]
    made = pltpu.VMEM((tokens, width), jnp.float32)
    return pl.pallas_call(
        functools.partial(inner_kernel, heads),
        grid=(tokens // ROWS,),
        in_specs=[VMEM] * 6,
        out_specs=[VMEM] * 3,
        out_shape=[made, made, pltpu.VMEM((heads, 128), jnp.float32)],
        compiler_params=pltpu.CompilerParams(vmem_limit_bytes=8 * MIB),
        cost_estimate=SMALL,
        name="inner",
    )(keys, values, queries, cumulative, states, reached)


def read_logs(ends, size, heads):
    whole, first = [], []
    for end in ends:
        parts = end[size:].astype(jnp.float32)
        whole.append(parts[:heads] + parts[heads : 2 * heads] + parts[2 * heads : 3 * heads])
        first.append(parts[3 * heads : 4 * heads] + parts[4 * heads : 5 * heads] + parts[5 * heads :])
    return whole, first


def gather_states(total, ends, places, logs, place, extra, heads, dim):
    factors = []
    for source in range(len(ends)):
        log = extra
        for other, other_log in enumerate(logs):
            between = (places[other] > places[source]) & (places[other] < place)
            log = log + jnp.where(between, other_log, 0.0)
        factors.append(jnp.where(places[source] < place, jnp.exp2(log), 0.0))
    for head in range(heads):
        rows = slice(head * dim, (head + 1) * dim)
        value = jnp.zeros((dim, dim), jnp.float32)
        for source, end in enumerate(ends):
            value += factors[source][head : head + 1] * end[rows].astype(jnp.float32)
        total[rows] = value


def with_entry(heads, here, inner_ref, growth_ref, queries, entry, use):
    dim = entry.shape[1]
    for pair in range(heads // 2):
        rows = [slice(head * dim, (head + 1) * dim) for head in (2 * pair, 2 * pair + 1)]
        carried = jnp.dot(
            queries[here, 2 * pair * dim : 2 * (pair + 1) * dim],
            pair_of(entry[rows[0]], entry[rows[1]]),
            preferred_element_type=jnp.float32,
        )
        for which, lanes in enumerate(rows):
            part = carried[:, which * dim : (which + 1) * dim]
            use(2 * pair + which, inner_ref[here, lanes] + part * growth_ref[here, lanes])


def finish_kernel(heads, inner_ref, growth_ref, queries, *refs):
    *ends, square_ref, entry_ref, entry = refs
    blk = pl.program_id(0)
    tokens, width = queries.shape
    dim = width // heads
    size = heads * dim

    @pl.when(blk == 0)
    def _():
        place = lax.axis_index("seq")
        logs, _unused = read_logs(ends, size, heads)
        places = [place ^ offset for offset in range(len(ends))]
        gather_states(entry, ends, places, logs, place, jnp.zeros((heads, dim), jnp.float32), heads, dim)
        entry_ref[...] = entry[...].astype(jnp.bfloat16)

    total = [jnp.zeros((ROWS, dim), jnp.float32)]

    def use(head, out):
        total[0] = total[0] + out * out

    here = pl.ds(pl.multiple_of(blk * ROWS, ROWS), ROWS)
    with_entry(heads, here, inner_ref, growth_ref, queries, entry_ref, use)
    high = total[0].astype(jnp.bfloat16)
    low = (total[0] - high.astype(jnp.float32)).astype(jnp.bfloat16)
    ones = jnp.ones((8, dim), jnp.bfloat16)
    sums = lax.dot_general(ones, high, NT, preferred_element_type=jnp.float32)
    sums = sums + lax.dot_general(ones, low, NT, preferred_element_type=jnp.float32)
    for row in range(ROWS // 128):
        square_ref[pl.ds(blk * (ROWS // 128) + row, 1)] = sums[:1, row * 128 : (row + 1) * 128]


def run_finish(inner, growth, queries, ends, heads):
    tokens, width = queries.shape
    dim = width // heads
    size = heads * dim
    return pl.pallas_call(
        functools.partial(finish_kernel, heads),
        grid=(tokens // ROWS,),
        in_specs=[VMEM] * (3 + len(ends)),
        out_specs=[VMEM, VMEM],
        out_shape=[pltpu.VMEM((tokens // 128, 128), jnp.float32), pltpu.VMEM((size, dim), jnp.bfloat16)],
        scratch_shapes=[pltpu.VMEM((size, dim), jnp.float32)],
        compiler_params=pltpu.CompilerParams(vmem_limit_bytes=8 * MIB),
        cost_estimate=SMALL,
        name="finish",
    )(inner, growth, queries, *ends)


def scale_kernel(heads, whole_width, inner_ref, growth_ref, queries, entry, gain_ref, square, attended_hbm, made, sems):
    blk = pl.program_id(0)
    tokens, width = made.shape
    dim = width // heads

    def copy_of(part):
        rows = pl.ds(part * ROWS, ROWS)
        return pltpu.make_async_copy(made.at[rows], attended_hbm.at[rows], sems.at[part])

    scales = []
    for part in range(ROWS // 128):
        total = square[pl.ds(blk * (ROWS // 128) + part, 1)]
        scale = lax.rsqrt(total * (1.0 / whole_width) + 1e-06)
        scales.append(jnp.broadcast_to(jnp.broadcast_to(scale, (8, 128)).T[:, :1], (128, dim)))
    scale = jnp.concatenate(scales, axis=0)
    here = pl.ds(pl.multiple_of(blk * ROWS, ROWS), ROWS)

    def use(head, out):
        lanes = slice(head * dim, (head + 1) * dim)
        made[here, lanes] = (out * scale * gain_ref[:, lanes]).astype(jnp.bfloat16)

    with_entry(heads, here, inner_ref, growth_ref, queries, entry, use)
    for part in range(tokens // ROWS):

        @pl.when(blk == part)
        def _():
            copy_of(part).start()

    @pl.when(blk == pl.num_programs(0) - 1)
    def _():
        for part in range(tokens // ROWS):
            copy_of(part).wait()


def run_scale(inner, growth, queries, entry, gain, square, whole_width, heads):
    tokens, width = inner.shape
    return pl.pallas_call(
        functools.partial(scale_kernel, heads, whole_width),
        grid=(tokens // ROWS,),
        in_specs=[VMEM] * 6,
        out_specs=HBM,
        out_shape=jax.ShapeDtypeStruct((tokens, width), jnp.bfloat16),
        scratch_shapes=[pltpu.VMEM((tokens, width), jnp.bfloat16), pltpu.SemaphoreType.DMA((tokens // ROWS,))],
        compiler_params=pltpu.CompilerParams(vmem_limit_bytes=12 * MIB),
        cost_estimate=SMALL,
        name="scale",
    )(inner, growth, queries, entry, gain.reshape(1, width), square)


def own_pages(owner_ref, place, page_of):
    for slot in range(SLOTS):
        page_of[slot] = -1

    def look(page, found):
        mine = (owner_ref[page] == place) & (found < SLOTS)

        @pl.when(mine)
        def _():
            page_of[found] = page

        return found + mine.astype(jnp.int32)

    lax.fori_loop(0, owner_ref.shape[0], look, jnp.int32(0))


def reach_kernel(heads, first, owner_ref, *refs):
    *ends, total, logs_ref, first_ref, page_of = refs
    count = len(ends)
    size, dim = total.shape[1:]
    place = lax.axis_index("seq")
    places = [place ^ offset for offset in range(count)]
    whole, half = read_logs(ends, size, heads)
    for source in range(count):
        logs_ref[source] = whole[source]
        first_ref[source] = half[source]
    own_pages(owner_ref, place, page_of)

    def fill(slot, carry):
        page = page_of[slot + first]

        @pl.when(page >= 0)
        def _():
            until = page // 2 + page % 2
            logs = [logs_ref[source] for source in range(count)]
            extra = jnp.zeros((heads, dim), jnp.float32)
            for source in range(count):
                extra = extra + jnp.where((places[source] == until) & (page % 2 == 0), first_ref[source], 0.0)
            gather_states(total.at[slot], ends, places, logs, until, extra, heads, dim)

        @pl.when(page < 0)
        def _():
            total[slot] = jnp.zeros((size, dim), jnp.float32)

        return carry

    lax.fori_loop(0, total.shape[0], fill, 0)


def run_reach(page_owner, ends, heads, first, slots):
    count = len(ends)
    rows, dim = ends[0].shape
    size = rows - 6 * heads
    return pl.pallas_call(
        functools.partial(reach_kernel, heads, first),
        in_specs=[SMEM] + [VMEM] * count,
        out_specs=VMEM,
        out_shape=pltpu.VMEM((slots, size, dim), jnp.float32),
        scratch_shapes=[
            pltpu.VMEM((count, heads, dim), jnp.float32),
            pltpu.VMEM((count, heads, dim), jnp.float32),
            pltpu.SMEM((SLOTS,), jnp.int32),
        ],
        compiler_params=pltpu.CompilerParams(vmem_limit_bytes=8 * MIB),
        cost_estimate=SMALL,
        name="reach",
    )(page_owner, *ends)


def cache_kernel(count, owner_ref, *refs):
    mids, totals = refs[:count], refs[count:-4]
    cache_hbm, made, page_of, sems = refs[-4:]
    place = lax.axis_index("seq")
    places = [place ^ offset for offset in range(count)]
    own_pages(owner_ref, place, page_of)
    parts = [(total, slot) for total in totals for slot in range(total.shape[0])]
    copies = []
    for slot, (total, row) in enumerate(parts):
        page = page_of[slot]
        halfway = (page >= 0) & (page % 2 == 0)

        @pl.when(jnp.logical_not(halfway))
        def _():
            made[slot] = total[row].astype(jnp.bfloat16)

        for source in range(count):

            @pl.when(halfway & (places[source] == page // 2))
            def _():
                made[slot] = (total[row] + mids[source][...].astype(jnp.float32)).astype(jnp.bfloat16)

        copies.append(pltpu.make_async_copy(made.at[slot], cache_hbm.at[slot], sems.at[slot]))
        copies[-1].start()
    for copy in copies:
        copy.wait()


def run_cache(page_owner, mids, totals):
    size, dim = mids[0].shape
    count = len(mids)
    return pl.pallas_call(
        functools.partial(cache_kernel, count),
        in_specs=[SMEM] + [VMEM] * (count + len(totals)),
        out_specs=HBM,
        out_shape=jax.ShapeDtypeStruct((SLOTS, size, dim), jnp.bfloat16),
        scratch_shapes=[
            pltpu.VMEM((SLOTS, size, dim), jnp.bfloat16),
            pltpu.SMEM((SLOTS,), jnp.int32),
            pltpu.SemaphoreType.DMA((SLOTS,)),
        ],
        compiler_params=pltpu.CompilerParams(vmem_limit_bytes=8 * MIB),
        cost_estimate=SMALL,
        name="cache",
    )(page_owner, *mids, *totals)


def swap(value, axis, offset):
    return lax.ppermute(value, axis, [(place, place ^ offset) for place in range(lax.axis_size(axis))])


def tie(value, *after):
    return lax.optimization_barrier((value, *after))[0]


def add_kernel(one_ref, two_ref, sum_ref):
    sum_ref[...] = one_ref[...] + two_ref[...]


def add(one, two):
    return pl.pallas_call(
        add_kernel,
        in_specs=[VMEM, VMEM],
        out_specs=VMEM,
        out_shape=pltpu.VMEM(one.shape, one.dtype),
        compiler_params=pltpu.CompilerParams(vmem_limit_bytes=4 * MIB),
        cost_estimate=SMALL,
        name="add",
    )(one, two)


def shards(queries, key_rows, value_rows, decay_log, norm_gain, page_owner):
    tokens, width = queries.shape
    heads = decay_log.shape[0]
    dim = width // heads
    count = lax.axis_size("seq")
    cumulative, states, reached, end, mid, keys, values = run_states(key_rows, value_rows, decay_log)
    held = pltpu.with_memory_space_constraint(tie(queries, cumulative), pltpu.VMEM)
    ends, mids = {0: end}, {0: mid}
    for offset in range(2, count, 2):
        ends[offset] = swap(end, "seq", offset)
    ends[1] = swap(end, "seq", 1)
    mids[1] = swap(mid, "seq", 1)
    inner, growth, done = run_inner(keys, values, held, cumulative, states, reached)
    mid = tie(mid, done, ends[1], mids[1])
    for offset in range(2, count, 2):
        mids[offset] = swap(mid, "seq", offset)
    for offset in range(2, count, 2):
        ends[offset + 1] = swap(tie(ends[offset], done), "seq", 1)
    ends = [ends[offset] for offset in range(count)]
    square, entry = run_finish(inner, growth, held, ends, heads)
    totals = []
    shares = [(0, 3), (3, SLOTS - 3)]
    offset = 1
    while offset < lax.axis_size("head"):
        other = swap(square, "head", offset)
        if shares:
            totals.append(run_reach(tie(page_owner, square), ends, heads, *shares.pop(0)))
            other = tie(other, totals[-1])
        square = add(square, other)
        offset *= 2
    for first, slots in shares:
        totals.append(run_reach(tie(page_owner, square), ends, heads, first, slots))
    for offset in range(2, count, 2):
        mids[offset + 1] = swap(tie(mids[offset], square), "seq", 1)
    mids = [mids[offset] for offset in range(count)]
    attended = run_scale(inner, growth, held, entry, norm_gain, square, width * lax.axis_size("head"), heads)
    page_cache = run_cache(page_owner, mids, totals)
    return attended, page_cache.reshape(SLOTS, heads, dim, dim)


def solution(mesh):
    return jax.shard_map(
        shards,
        mesh=mesh,
        in_specs=(
            P("seq", "head"),
            P("seq", "head"),
            P("seq", "head"),
            P("head", "seq"),
            P("head"),
            P(),
        ),
        out_specs=(P("seq", "head"), P("seq", "head", None, None)),
        check_vma=False,
    )
```

time: 49.2 us -> 43.7 us (0.89)
  Pallas kernels: 29.5 us -> 26.9 us
  waiting for transfers between devices: 4.6 us -> 2.28 us
  starting transfers between devices: 14.7 us -> 13.9 us
    pallas_call x4 -> x5, Pallas kernels: 21.2 us -> 18.6 us  [the longest x1 9.56 us: run_inner(): pl.pallas_call(functools.partial(inner_kernel, heads), grid=(tokens // RO...]
    ppermute x16, waiting for transfers between devices: 4.6 us -> 2.28 us  [swap(): lax.ppermute(value, axis, [(place, place ^ offset) for place in range(lax...]
    ppermute x16, starting transfers between devices: 14.7 us -> 13.9 us  [swap(): lax.ppermute(value, axis, [(place, place ^ offset) for place in range(lax...]
  transfers between devices with their start and end apart: 16 -> 16, of which waited for: 4 -> 3; matrix products, arithmetic and copies ran while one was open for 0% -> 0% of each run, Pallas kernels for 41% -> 47%
where the time goes in v4:
time: 43.7 us; the launch traced here: 43.8 us
  Pallas kernels  26.9 us (62%)
  starting transfers between devices  13.9 us (32%)
  waiting for transfers between devices  2.28 us (5%)
  between operations  0.74 us (2%)
    ppermute x16, starting transfers between devices, swap(): lax.ppermute(value, axis, [(place, place ^ offset) for place in range(lax...  13.9 us
    pallas_call x1, Pallas kernels, run_inner(): pl.pallas_call(functools.partial(inner_kernel, heads), grid=(tokens // RO...  9.56 us
    pallas_call x1, Pallas kernels, run_states(): pl.pallas_call(functools.partial(state_kernel, heads), in_specs=[HBM] * 3...  4.47 us
    pallas_call x2, Pallas kernels, run_reach(): pl.pallas_call(functools.partial(reach_kernel, heads, first), in_specs=[S...  3.91 us
    pallas_call x1, Pallas kernels, run_scale(): pl.pallas_call(functools.partial(scale_kernel, heads, whole_width), grid=...  3.77 us
    pallas_call x1, Pallas kernels, run_finish(): pl.pallas_call(functools.partial(finish_kernel, heads), grid=(tokens // R...  3.14 us
    ppermute x16, waiting for transfers between devices, swap(): lax.ppermute(value, axis, [(place, place ^ offset) for place in range(lax...  2.28 us
    pallas_call x1, Pallas kernels, run_cache(): pl.pallas_call(functools.partial(cache_kernel, count), in_specs=[SMEM] +...  2.03 us
  transfers between devices with their start and end apart: 16, of which 3 were waited for; matrix products, arithmetic and copies ran while one was open for 0% of the time, Pallas kernels for 47%

profile of v4, /device:TPU:0, one launch (start us, length us, event | category | flops | bytes accessed | tf_op | source)
XLA Modules:
  0.0 43.8 jit_solution(9069007307664981495)
XLA Ops:
  0.6 0.0 copy-start
  0.6 4.5 %states.1 = (f32[8,2048]{1,0:T(8,128)S(1)}, bf16[8,1024,128]{2,1,0:T(8,128)(2,1)S(1)}, f32[8,8,128]{2,1,0:T(8,128)S(1)}, bf16[1072,128]{1,0:T(8,128)(2,1)S(1)}, ...) custom-call(bf16[2048,1024]{1,0:T(8,128)(2,1)} %key_hbm.1, ...), custom_call_target="tpu_custom_call" | custom-call | flops 1 | bytes 1 | tf_op jit(solution)/shard_map/states/pallas_call | solution.py:115
  5.1 4.0 %collective-permute-start.5 = (bf16[1072,128]{1,0:T(8,128)(2,1)S(1)}, bf16[1072,128]{1,0:T(8,128)(2,1)S(1)}, u32[]{:S(2)}, u32[]{:S(2)}) collective-permute-start(bf16[1072,128]{1,0:T(8,128)(2,1)S(1)} %get-tuple-element.34.refs_0_), channel_id=1, source_target_pairs={{0,24},{4,28},{8,16},{12,20},{16,8},{20,12},{24,0},{28,4},{1,25},{... | collective-permute-start | bytes 823304 | tf_op jit(solution)/shard_map/ppermute | solution.py:457
  9.1 0.5 %collective-permute-start.3 = (bf16[1072,128]{1,0:T(8,128)(2,1)S(1)}, bf16[1072,128]{1,0:T(8,128)(2,1)S(1)}, u32[]{:S(2)}, u32[]{:S(2)}) collective-permute-start(bf16[1072,128]{1,0:T(8,128)(2,1)S(1)} %get-tuple-element.34.refs_0_), channel_id=1, source_target_pairs={{0,16},{4,20},{8,24},{12,28},{16,0},{20,4},{24,8},{28,12},{1,17},{... | collective-permute-start | bytes 823304 | tf_op jit(solution)/shard_map/ppermute | solution.py:457
  9.6 0.1 collective-permute-start.1
  9.7 0.0 collective-permute-start
  9.7 0.0 copy-done
  9.7 9.6 %inner.1 = (f32[2048,1024]{1,0:T(8,128)S(1)}, f32[2048,1024]{1,0:T(8,128)S(1)}, f32[8,128]{1,0:T(8,128)}) custom-call(bf16[2048,1024]{1,0:T(8,128)(2,1)S(1)} %get-tuple-element.26.keys, bf16[2048,1024]{1,0:T(8,128)(2,1)S(1)} %get-tuple-element.27.values, bf16[2048,1024]{1,0:T(8,128)(2,1)S(1)} %copy-done, f32[8,2048]{1,0:T(8,128)S(1)} %get-tuple-element.28.cum_ref, ...), custom_call_target="tpu_custom_call" | custom-call | flops 1 | bytes 1 | tf_op jit(solution)/shard_map/inner/pallas_call | solution.py:192
  19.3 0.0 collective-permute-done.5.refs_6_
  19.3 0.5 %collective-permute-start.6 = (bf16[1072,128]{1,0:T(8,128)(2,1)S(1)}, bf16[1072,128]{1,0:T(8,128)(2,1)S(1)}, u32[]{:S(2)}, u32[]{:S(2)}) collective-permute-start(bf16[1072,128]{1,0:T(8,128)(2,1)S(1)} %collective-permute-done.5.refs_6_), channel_id=1, source_target_pairs={{0,4},{4,0},{8,12},{12,8},{16,20},{20,16},{24,28},{28,24},{1,5},{5... | collective-permute-start | bytes 823304 | tf_op jit(solution)/shard_map/ppermute | solution.py:457
  19.8 0.0 collective-permute-start.9
  19.8 1.7 %collective-permute-done.3.refs_4_ = bf16[1072,128]{1,0:T(8,128)(2,1)S(1)} collective-permute-done((bf16[1072,128]{1,0:T(8,128)(2,1)S(1)}, bf16[1072,128]{1,0:T(8,128)(2,1)S(1)}, u32[]{:S(2)}, u32[]{:S(2)}) %collective-permute-start.3) | collective-permute-done | bytes 274464 | tf_op jit(solution)/shard_map/ppermute | solution.py:457
  21.5 0.0 collective-permute-start.4
  21.5 0.3 collective-permute-done.1.refs_2_
  21.8 0.2 collective-permute-start.2
  22.0 0.0 collective-permute-done.9.refs_1_
  22.0 0.0 collective-permute-done.refs_1_
  22.1 2.2 %collective-permute-start.14 = (bf16[1024,128]{1,0:T(8,128)(2,1)S(1)}, bf16[1024,128]{1,0:T(8,128)(2,1)S(1)}, u32[]{:S(2)}, u32[]{:S(2)}) collective-permute-start(bf16[1024,128]{1,0:T(8,128)(2,1)S(1)} %get-tuple-element.46.refs_0_), channel_id=1, source_target_pairs={{0,24},{4,28},{8,16},{12,20},{16,8},{20,12},{24,0},{28,4},{1,25},{... | collective-permute-start | bytes 786440 | tf_op jit(solution)/shard_map/ppermute | solution.py:457
  24.2 1.0 %collective-permute-start.12 = (bf16[1024,128]{1,0:T(8,128)(2,1)S(1)}, bf16[1024,128]{1,0:T(8,128)(2,1)S(1)}, u32[]{:S(2)}, u32[]{:S(2)}) collective-permute-start(bf16[1024,128]{1,0:T(8,128)(2,1)S(1)} %get-tuple-element.46.refs_0_), channel_id=1, source_target_pairs={{0,16},{4,20},{8,24},{12,28},{16,0},{20,4},{24,8},{28,12},{1,17},{... | collective-permute-start | bytes 786440 | tf_op jit(solution)/shard_map/ppermute | solution.py:457
  25.2 0.0 collective-permute-done.6.refs_7_
  25.2 0.4 collective-permute-start.10
  25.5 0.0 collective-permute-done.4.refs_5_
  25.6 0.0 collective-permute-done.2.refs_3_
  25.6 0.0 copy-start.1
  25.6 3.1 %finish.1 = (f32[16,128]{1,0:T(8,128)S(1)}, bf16[1024,128]{1,0:T(8,128)(2,1)S(1)}) custom-call(f32[2048,1024]{1,0:T(8,128)S(1)} %get-tuple-element.32.inner_ref, f32[2048,1024]{1,0:T(8,128)S(1)} %get-tuple-element.33.growth_ref, bf16[2048,1024]{1,0:T(8,128)(2,1)S(1)} %copy-done, bf16[1072,128]{1,0:T(8,128)(2,1)S(1)} %get-tuple-element.34.refs_0_, ...), custom_call_target="tpu_custom_call" | custom-call | flops 1 | bytes 1 | tf_op jit(solution)/shard_map/finish/pallas_call | solution.py:278
  28.7 0.0 copy-start.2
  28.7 1.8 %collective-permute-start.7 = (f32[16,128]{1,0:T(8,128)S(1)}, f32[16,128]{1,0:T(8,128)S(1)}, u32[]{:S(2)}, u32[]{:S(2)}) collective-permute-start(f32[16,128]{1,0:T(8,128)S(1)} %get-tuple-element.40.one_ref), channel_id=1, source_target_pairs={{0,1},{1,0},{2,3},{3,2},{4,5},{5,4},{6,7},{7,6},{8,9},{9,8},{10,11... | collective-permute-start | bytes 24584 | tf_op jit(solution)/shard_map/ppermute | solution.py:457
  30.5 0.0 copy-done.1
  30.5 2.2 %reach.2.refs_8_ = f32[3,1024,128]{2,1,0:T(8,128)S(1)} custom-call(s32[16]{0:T(128)S(1)} %copy-done.1, bf16[1072,128]{1,0:T(8,128)(2,1)S(1)} %get-tuple-element.34.refs_0_, bf16[1072,128]{1,0:T(8,128)(2,1)S(1)} %collective-permute-done.refs_1_, bf16[1072,128]{1,0:T(8,128)(2,1)S(1)} %collective-permute-done.1.refs_2_, ...), custom_call_target="tpu_custom_call" | custom-call | flops 1 | bytes 1 | tf_op jit(solution)/shard_map/reach/pallas_call | solution.py:393
  32.7 0.0 collective-permute-done.7.two_ref
  32.7 2.7 %collective-permute-start.8 = (f32[16,128]{1,0:T(8,128)S(1)}, f32[16,128]{1,0:T(8,128)S(1)}, u32[]{:S(2)}, u32[]{:S(2)}) collective-permute-start(f32[16,128]{1,0:T(8,128)S(1)} %add.2.one_ref), channel_id=1, source_target_pairs={{0,2},{1,3},{2,0},{3,1},{4,6},{5,7},{6,4},{7,5},{8,10},{9,11},{10,... | collective-permute-start | bytes 24584 | tf_op jit(solution)/shard_map/ppermute | solution.py:457
  35.4 1.7 %reach.3.refs_9_ = f32[2,1024,128]{2,1,0:T(8,128)S(1)} custom-call(s32[16]{0:T(128)S(1)} %copy-done.1, bf16[1072,128]{1,0:T(8,128)(2,1)S(1)} %get-tuple-element.34.refs_0_, bf16[1072,128]{1,0:T(8,128)(2,1)S(1)} %collective-permute-done.refs_1_, bf16[1072,128]{1,0:T(8,128)(2,1)S(1)} %collective-permute-done.1.refs_2_, ...), custom_call_target="tpu_custom_call" | custom-call | flops 1 | bytes 1 | tf_op jit(solution)/shard_map/reach/pallas_call | solution.py:393
  37.1 0.2 collective-permute-done.8.two_ref
  37.3 0.0 collective-permute-done.14.refs_6_
  37.4 0.0 collective-permute-start.15
  37.4 0.0 collective-permute-done.12.refs_4_
  37.4 0.5 %collective-permute-start.13 = (bf16[1024,128]{1,0:T(8,128)(2,1)S(1)}, bf16[1024,128]{1,0:T(8,128)(2,1)S(1)}, u32[]{:S(2)}, u32[]{:S(2)}) collective-permute-start(bf16[1024,128]{1,0:T(8,128)(2,1)S(1)} %collective-permute-done.12.refs_4_), channel_id=1, source_target_pairs={{0,4},{4,0},{8,12},{12,8},{16,20},{20,16},{24,28},{28,24},{1,5},{5... | collective-permute-start | bytes 786440 | tf_op jit(solution)/shard_map/ppermute | solution.py:457
  37.9 0.0 collective-permute-done.10.refs_2_
  37.9 0.1 collective-permute-start.11
  38.0 0.0 copy-done.2
  38.0 3.8 %scale.1 = bf16[2048,1024]{1,0:T(8,128)(2,1)} custom-call(f32[2048,1024]{1,0:T(8,128)S(1)} %get-tuple-element.32.inner_ref, f32[2048,1024]{1,0:T(8,128)S(1)} %get-tuple-element.33.growth_ref, bf16[2048,1024]{1,0:T(8,128)(2,1)S(1)} %copy-done, bf16[1024,128]{1,0:T(8,128)(2,1)S(1)} %get-tuple-element.39.entry, f32[1,1024]{1,0:T(1,128)S(1)} %bitcast.2, ...), custom_call_target="tpu_custom_call" | custom-call | flops 1 | bytes 1 | tf_op jit(solution)/shard_map/scale/pallas_call | solution.py:327
  41.7 0.0 collective-permute-done.15.refs_7_
  41.7 0.0 collective-permute-done.13.refs_5_
  41.7 0.0 collective-permute-done.11.refs_3_
  41.8 2.0 %cache.1 = bf16[5,1024,128]{2,1,0:T(8,128)(2,1)} custom-call(s32[16]{0:T(128)S(1)} %copy-done.1, bf16[1024,128]{1,0:T(8,128)(2,1)S(1)} %get-tuple-element.46.refs_0_, bf16[1024,128]{1,0:T(8,128)(2,1)S(1)} %collective-permute-done.9.refs_1_, bf16[1024,128]{1,0:T(8,128)(2,1)S(1)} %collective-permute-done.10.refs_2_, ...), custom_call_target="tpu_custom_call" | custom-call | flops 1 | bytes 1 | tf_op jit(solution)/shard_map/cache/pallas_call | solution.py:440
  (2 shorter events, 0.0 us)
Async XLA Ops:
  0.6 9.1 %copy-start = (bf16[2048,1024]{1,0:T(8,128)(2,1)S(1)}, bf16[2048,1024]{1,0:T(8,128)(2,1)}, u32[]{:S(2)}) copy-start(bf16[2048,1024]{1,0:T(8,128)(2,1)} %queries.2) | copy-start | bytes 12582916
  5.1 14.2 %collective-permute-start.5 = (bf16[1072,128]{1,0:T(8,128)(2,1)S(1)}, bf16[1072,128]{1,0:T(8,128)(2,1)S(1)}, u32[]{:S(2)}, u32[]{:S(2)}) collective-permute-start(bf16[1072,128]{1,0:T(8,128)(2,1)S(1)} %get-tuple-element.34.refs_0_), channel_id=1, source_target_pairs={{0,24},{4,28},{8,16},{12,20},{16,8},{20,12},{24,0},{28,4},{1,25},{... | collective-permute-start | bytes 823304 | tf_op jit(solution)/shard_map/ppermute | solution.py:457
  9.1 12.5 %collective-permute-start.3 = (bf16[1072,128]{1,0:T(8,128)(2,1)S(1)}, bf16[1072,128]{1,0:T(8,128)(2,1)S(1)}, u32[]{:S(2)}, u32[]{:S(2)}) collective-permute-start(bf16[1072,128]{1,0:T(8,128)(2,1)S(1)} %get-tuple-element.34.refs_0_), channel_id=1, source_target_pairs={{0,16},{4,20},{8,24},{12,28},{16,0},{20,4},{24,8},{28,12},{1,17},{... | collective-permute-start | bytes 823304 | tf_op jit(solution)/shard_map/ppermute | solution.py:457
  9.6 12.2 %collective-permute-start.1 = (bf16[1072,128]{1,0:T(8,128)(2,1)S(1)}, bf16[1072,128]{1,0:T(8,128)(2,1)S(1)}, u32[]{:S(2)}, u32[]{:S(2)}) collective-permute-start(bf16[1072,128]{1,0:T(8,128)(2,1)S(1)} %get-tuple-element.34.refs_0_), channel_id=1, source_target_pairs={{0,8},{4,12},{8,0},{12,4},{16,24},{20,28},{24,16},{28,20},{1,9},{5... | collective-permute-start | bytes 823304 | tf_op jit(solution)/shard_map/ppermute | solution.py:457
  9.7 12.3 %collective-permute-start = (bf16[1072,128]{1,0:T(8,128)(2,1)S(1)}, bf16[1072,128]{1,0:T(8,128)(2,1)S(1)}, u32[]{:S(2)}, u32[]{:S(2)}) collective-permute-start(bf16[1072,128]{1,0:T(8,128)(2,1)S(1)} %get-tuple-element.34.refs_0_), channel_id=1, source_target_pairs={{0,4},{4,0},{8,12},{12,8},{16,20},{20,16},{24,28},{28,24},{1,5},{5... | collective-permute-start | bytes 823304 | tf_op jit(solution)/shard_map/ppermute | solution.py:457
  19.3 5.9 %collective-permute-start.6 = (bf16[1072,128]{1,0:T(8,128)(2,1)S(1)}, bf16[1072,128]{1,0:T(8,128)(2,1)S(1)}, u32[]{:S(2)}, u32[]{:S(2)}) collective-permute-start(bf16[1072,128]{1,0:T(8,128)(2,1)S(1)} %collective-permute-done.5.refs_6_), channel_id=1, source_target_pairs={{0,4},{4,0},{8,12},{12,8},{16,20},{20,16},{24,28},{28,24},{1,5},{5... | collective-permute-start | bytes 823304 | tf_op jit(solution)/shard_map/ppermute | solution.py:457
  19.8 2.2 %collective-permute-start.9 = (bf16[1024,128]{1,0:T(8,128)(2,1)S(1)}, bf16[1024,128]{1,0:T(8,128)(2,1)S(1)}, u32[]{:S(2)}, u32[]{:S(2)}) collective-permute-start(bf16[1024,128]{1,0:T(8,128)(2,1)S(1)} %get-tuple-element.46.refs_0_), channel_id=1, source_target_pairs={{0,4},{4,0},{8,12},{12,8},{16,20},{20,16},{24,28},{28,24},{1,5},{5... | collective-permute-start | bytes 786440 | tf_op jit(solution)/shard_map/ppermute | solution.py:457
  21.5 4.0 %collective-permute-start.4 = (bf16[1072,128]{1,0:T(8,128)(2,1)S(1)}, bf16[1072,128]{1,0:T(8,128)(2,1)S(1)}, u32[]{:S(2)}, u32[]{:S(2)}) collective-permute-start(bf16[1072,128]{1,0:T(8,128)(2,1)S(1)} %collective-permute-done.3.refs_4_), channel_id=1, source_target_pairs={{0,4},{4,0},{8,12},{12,8},{16,20},{20,16},{24,28},{28,24},{1,5},{5... | collective-permute-start | bytes 823304 | tf_op jit(solution)/shard_map/ppermute | solution.py:457
  21.8 3.7 %collective-permute-start.2 = (bf16[1072,128]{1,0:T(8,128)(2,1)S(1)}, bf16[1072,128]{1,0:T(8,128)(2,1)S(1)}, u32[]{:S(2)}, u32[]{:S(2)}) collective-permute-start(bf16[1072,128]{1,0:T(8,128)(2,1)S(1)} %collective-permute-done.1.refs_2_), channel_id=1, source_target_pairs={{0,4},{4,0},{8,12},{12,8},{16,20},{20,16},{24,28},{28,24},{1,5},{5... | collective-permute-start | bytes 823304 | tf_op jit(solution)/shard_map/ppermute | solution.py:457
  22.1 15.3 %collective-permute-start.14 = (bf16[1024,128]{1,0:T(8,128)(2,1)S(1)}, bf16[1024,128]{1,0:T(8,128)(2,1)S(1)}, u32[]{:S(2)}, u32[]{:S(2)}) collective-permute-start(bf16[1024,128]{1,0:T(8,128)(2,1)S(1)} %get-tuple-element.46.refs_0_), channel_id=1, source_target_pairs={{0,24},{4,28},{8,16},{12,20},{16,8},{20,12},{24,0},{28,4},{1,25},{... | collective-permute-start | bytes 786440 | tf_op jit(solution)/shard_map/ppermute | solution.py:457
  24.2 13.1 %collective-permute-start.12 = (bf16[1024,128]{1,0:T(8,128)(2,1)S(1)}, bf16[1024,128]{1,0:T(8,128)(2,1)S(1)}, u32[]{:S(2)}, u32[]{:S(2)}) collective-permute-start(bf16[1024,128]{1,0:T(8,128)(2,1)S(1)} %get-tuple-element.46.refs_0_), channel_id=1, source_target_pairs={{0,16},{4,20},{8,24},{12,28},{16,0},{20,4},{24,8},{28,12},{1,17},{... | collective-permute-start | bytes 786440 | tf_op jit(solution)/shard_map/ppermute | solution.py:457
  25.2 12.7 %collective-permute-start.10 = (bf16[1024,128]{1,0:T(8,128)(2,1)S(1)}, bf16[1024,128]{1,0:T(8,128)(2,1)S(1)}, u32[]{:S(2)}, u32[]{:S(2)}) collective-permute-start(bf16[1024,128]{1,0:T(8,128)(2,1)S(1)} %get-tuple-element.46.refs_0_), channel_id=1, source_target_pairs={{0,8},{4,12},{8,0},{12,4},{16,24},{20,28},{24,16},{28,20},{1,9},{5... | collective-permute-start | bytes 786440 | tf_op jit(solution)/shard_map/ppermute | solution.py:457
  25.6 4.9 %copy-start.1 = (s32[16]{0:T(128)S(1)}, s32[16]{0:T(128)}, u32[]{:S(2)}) copy-start(s32[16]{0:T(128)} %owner_ref.3) | copy-start | bytes 196
  28.7 9.3 %copy-start.2 = (f32[1024]{0:T(1024)S(1)}, f32[1024]{0:T(1024)}, u32[]{:S(2)}) copy-start(f32[1024]{0:T(1024)} %param.10) | copy-start | bytes 12292
  28.7 4.0 %collective-permute-start.7 = (f32[16,128]{1,0:T(8,128)S(1)}, f32[16,128]{1,0:T(8,128)S(1)}, u32[]{:S(2)}, u32[]{:S(2)}) collective-permute-start(f32[16,128]{1,0:T(8,128)S(1)} %get-tuple-element.40.one_ref), channel_id=1, source_target_pairs={{0,1},{1,0},{2,3},{3,2},{4,5},{5,4},{6,7},{7,6},{8,9},{9,8},{10,11... | collective-permute-start | bytes 24584 | tf_op jit(solution)/shard_map/ppermute | solution.py:457
  32.7 4.6 %collective-permute-start.8 = (f32[16,128]{1,0:T(8,128)S(1)}, f32[16,128]{1,0:T(8,128)S(1)}, u32[]{:S(2)}, u32[]{:S(2)}) collective-permute-start(f32[16,128]{1,0:T(8,128)S(1)} %add.2.one_ref), channel_id=1, source_target_pairs={{0,2},{1,3},{2,0},{3,1},{4,6},{5,7},{6,4},{7,5},{8,10},{9,11},{10,... | collective-permute-start | bytes 24584 | tf_op jit(solution)/shard_map/ppermute | solution.py:457
  37.4 4.4 %collective-permute-start.15 = (bf16[1024,128]{1,0:T(8,128)(2,1)S(1)}, bf16[1024,128]{1,0:T(8,128)(2,1)S(1)}, u32[]{:S(2)}, u32[]{:S(2)}) collective-permute-start(bf16[1024,128]{1,0:T(8,128)(2,1)S(1)} %collective-permute-done.14.refs_6_), channel_id=1, source_target_pairs={{0,4},{4,0},{8,12},{12,8},{16,20},{20,16},{24,28},{28,24},{1,5},{5... | collective-permute-start | bytes 786440 | tf_op jit(solution)/shard_map/ppermute | solution.py:457
  37.4 4.4 %collective-permute-start.13 = (bf16[1024,128]{1,0:T(8,128)(2,1)S(1)}, bf16[1024,128]{1,0:T(8,128)(2,1)S(1)}, u32[]{:S(2)}, u32[]{:S(2)}) collective-permute-start(bf16[1024,128]{1,0:T(8,128)(2,1)S(1)} %collective-permute-done.12.refs_4_), channel_id=1, source_target_pairs={{0,4},{4,0},{8,12},{12,8},{16,20},{20,16},{24,28},{28,24},{1,5},{5... | collective-permute-start | bytes 786440 | tf_op jit(solution)/shard_map/ppermute | solution.py:457
  37.9 3.9 %collective-permute-start.11 = (bf16[1024,128]{1,0:T(8,128)(2,1)S(1)}, bf16[1024,128]{1,0:T(8,128)(2,1)S(1)}, u32[]{:S(2)}, u32[]{:S(2)}) collective-permute-start(bf16[1024,128]{1,0:T(8,128)(2,1)S(1)} %collective-permute-done.10.refs_2_), channel_id=1, source_target_pairs={{0,4},{4,0},{8,12},{12,8},{16,20},{20,16},{24,28},{28,24},{1,5},{5... | collective-permute-start | bytes 786440 | tf_op jit(solution)/shard_map/ppermute | solution.py:457

commit v5 on v4

--- a/solution.py
+++ b/solution.py
@@ -141,7 +141,7 @@
     return jnp.concatenate([jnp.concatenate([one, zero], axis=1), jnp.concatenate([zero, two], axis=1)], axis=0)
 
 
-def inner_kernel(heads, keys, values, queries, cum_ref, states_ref, reached_ref, out_ref, growth_ref, done_ref):
+def inner_kernel(heads, keys, values, queries, cum_ref, states_ref, reached_ref, out_ref, grown_ref, done_ref):
     step = pl.program_id(0)
     width = queries.shape[1]
     dim = width // heads
@@ -180,7 +180,8 @@
         which = head % 2
         local = local + carried[part][:, which * dim : (which + 1) * dim] * jnp.exp2(column)
         out_ref[here[part], lanes] = local
-        growth_ref[here[part], lanes] = jnp.exp2(column + reached[part][head : head + 1])
+        growth = jnp.exp2(column + reached[part][head : head + 1])
+        grown_ref[here[part], lanes] = (queries[here[part], lanes].astype(jnp.float32) * growth).astype(jnp.bfloat16)
         scores = ahead
     done_ref[...] = cums[0][:, :128]
 
@@ -194,7 +195,7 @@
         grid=(tokens // ROWS,),
         in_specs=[VMEM] * 6,
         out_specs=[VMEM] * 3,
-        out_shape=[made, made, pltpu.VMEM((heads, 128), jnp.float32)],
+        out_shape=[made, pltpu.VMEM((tokens, width), jnp.bfloat16), pltpu.VMEM((heads, 128), jnp.float32)],
         compiler_params=pltpu.CompilerParams(vmem_limit_bytes=8 * MIB),
         cost_estimate=SMALL,
         name="inner",
@@ -226,24 +227,10 @@
         total[rows] = value
 
 
-def with_entry(heads, here, inner_ref, growth_ref, queries, entry, use):
-    dim = entry.shape[1]
-    for pair in range(heads // 2):
-        rows = [slice(head * dim, (head + 1) * dim) for head in (2 * pair, 2 * pair + 1)]
-        carried = jnp.dot(
-            queries[here, 2 * pair * dim : 2 * (pair + 1) * dim],
-            pair_of(entry[rows[0]], entry[rows[1]]),
-            preferred_element_type=jnp.float32,
-        )
-        for which, lanes in enumerate(rows):
-            part = carried[:, which * dim : (which + 1) * dim]
-            use(2 * pair + which, inner_ref[here, lanes] + part * growth_ref[here, lanes])
-
-
-def finish_kernel(heads, inner_ref, growth_ref, queries, *refs):
-    *ends, square_ref, entry_ref, entry = refs
+def finish_kernel(heads, inner_ref, grown, gain_ref, *refs):
+    *ends, out_ref, square_ref, entry, entry_low = refs
     blk = pl.program_id(0)
-    tokens, width = queries.shape
+    width = grown.shape[1]
     dim = width // heads
     size = heads * dim
 
@@ -253,17 +240,28 @@
         logs, _unused = read_logs(ends, size, heads)
         places = [place ^ offset for offset in range(len(ends))]
         gather_states(entry, ends, places, logs, place, jnp.zeros((heads, dim), jnp.float32), heads, dim)
-        entry_ref[...] = entry[...].astype(jnp.bfloat16)
-
-    total = [jnp.zeros((ROWS, dim), jnp.float32)]
-
-    def use(head, out):
-        total[0] = total[0] + out * out
+        entry_low[...] = entry[...].astype(jnp.bfloat16)
 
     here = pl.ds(pl.multiple_of(blk * ROWS, ROWS), ROWS)
-    with_entry(heads, here, inner_ref, growth_ref, queries, entry_ref, use)
-    high = total[0].astype(jnp.bfloat16)
-    low = (total[0] - high.astype(jnp.float32)).astype(jnp.bfloat16)
+
+    def carried_of(pair):
+        rows = [slice(head * dim, (head + 1) * dim) for head in (2 * pair, 2 * pair + 1)]
+        query = grown[here, 2 * pair * dim : 2 * (pair + 1) * dim]
+        return jnp.dot(query, pair_of(entry_low[rows[0]], entry_low[rows[1]]), preferred_element_type=jnp.float32)
+
+    total = jnp.zeros((ROWS, dim), jnp.float32)
+    ahead = carried_of(0)
+    for pair in range(heads // 2):
+        carried = ahead
+        if pair + 1 < heads // 2:
+            ahead = carried_of(pair + 1)
+        for which in range(2):
+            lanes = slice((2 * pair + which) * dim, (2 * pair + which + 1) * dim)
+            out = inner_ref[here, lanes] + carried[:, which * dim : (which + 1) * dim]
+            total += out * out
+            out_ref[here, lanes] = out * gain_ref[:, lanes]
+    high = total.astype(jnp.bfloat16)
+    low = (total - high.astype(jnp.float32)).astype(jnp.bfloat16)
     ones = jnp.ones((8, dim), jnp.bfloat16)
     sums = lax.dot_general(ones, high, NT, preferred_element_type=jnp.float32)
     sums = sums + lax.dot_general(ones, low, NT, preferred_element_type=jnp.float32)
@@ -271,8 +269,8 @@
         square_ref[pl.ds(blk * (ROWS // 128) + row, 1)] = sums[:1, row * 128 : (row + 1) * 128]
 
 
-def run_finish(inner, growth, queries, ends, heads):
-    tokens, width = queries.shape
+def run_finish(inner, grown, gain, ends, heads):
+    tokens, width = grown.shape
     dim = width // heads
     size = heads * dim
     return pl.pallas_call(
@@ -280,61 +278,58 @@
         grid=(tokens // ROWS,),
         in_specs=[VMEM] * (3 + len(ends)),
         out_specs=[VMEM, VMEM],
-        out_shape=[pltpu.VMEM((tokens // 128, 128), jnp.float32), pltpu.VMEM((size, dim), jnp.bfloat16)],
-        scratch_shapes=[pltpu.VMEM((size, dim), jnp.float32)],
+        out_shape=[pltpu.VMEM((tokens, width), jnp.float32), pltpu.VMEM((tokens // 128, 128), jnp.float32)],
+        scratch_shapes=[pltpu.VMEM((size, dim), jnp.float32), pltpu.VMEM((size, dim), jnp.bfloat16)],
         compiler_params=pltpu.CompilerParams(vmem_limit_bytes=8 * MIB),
         cost_estimate=SMALL,
         name="finish",
-    )(inner, growth, queries, *ends)
-
-
-def scale_kernel(heads, whole_width, inner_ref, growth_ref, queries, entry, gain_ref, square, attended_hbm, made, sems):
+    )(inner, grown, gain.reshape(1, width), *ends)
+
+
+def scale_kernel(whole_width, out_ref, square, attended_hbm, made, sems):
     blk = pl.program_id(0)
     tokens, width = made.shape
-    dim = width // heads
 
     def copy_of(part):
-        rows = pl.ds(part * ROWS, ROWS)
+        rows = pl.ds(part * BLOCK, BLOCK)
         return pltpu.make_async_copy(made.at[rows], attended_hbm.at[rows], sems.at[part])
 
-    scales = []
-    for part in range(ROWS // 128):
-        total = square[pl.ds(blk * (ROWS // 128) + part, 1)]
-        scale = lax.rsqrt(total * (1.0 / whole_width) + 1e-06)
-        scales.append(jnp.broadcast_to(jnp.broadcast_to(scale, (8, 128)).T[:, :1], (128, dim)))
-    scale = jnp.concatenate(scales, axis=0)
-    here = pl.ds(pl.multiple_of(blk * ROWS, ROWS), ROWS)
-
-    def use(head, out):
-        lanes = slice(head * dim, (head + 1) * dim)
-        made[here, lanes] = (out * scale * gain_ref[:, lanes]).astype(jnp.bfloat16)
-
-    with_entry(heads, here, inner_ref, growth_ref, queries, entry, use)
-    for part in range(tokens // ROWS):
-
-        @pl.when(blk == part)
-        def _():
-            copy_of(part).start()
+    for sub in range(ROWS // BLOCK):
+        base = blk * ROWS + sub * BLOCK
+        scales = []
+        for part in range(BLOCK // 128):
+            total = square[pl.ds(blk * (ROWS // 128) + sub * (BLOCK // 128) + part, 1)]
+            scale = lax.rsqrt(total * (1.0 / whole_width) + 1e-06)
+            scales.append(jnp.broadcast_to(jnp.broadcast_to(scale, (8, 128)).T[:, :1], (128, 128)))
+        scale = jnp.concatenate(scales, axis=0)
+        here = pl.ds(pl.multiple_of(base, BLOCK), BLOCK)
+        for col in range(0, width, 128):
+            made[here, col : col + 128] = (out_ref[here, col : col + 128] * scale).astype(jnp.bfloat16)
+        for step in range(tokens // ROWS):
+
+            @pl.when(blk == step)
+            def _():
+                copy_of(step * (ROWS // BLOCK) + sub).start()
 
     @pl.when(blk == pl.num_programs(0) - 1)
     def _():
-        for part in range(tokens // ROWS):
+        for part in range(tokens // BLOCK):
             copy_of(part).wait()
 
 
-def run_scale(inner, growth, queries, entry, gain, square, whole_width, heads):
-    tokens, width = inner.shape
-    return pl.pallas_call(
-        functools.partial(scale_kernel, heads, whole_width),
+def run_scale(out, square, whole_width):
+    tokens, width = out.shape
+    return pl.pallas_call(
+        functools.partial(scale_kernel, whole_width),
         grid=(tokens // ROWS,),
-        in_specs=[VMEM] * 6,
+        in_specs=[VMEM] * 2,
         out_specs=HBM,
         out_shape=jax.ShapeDtypeStruct((tokens, width), jnp.bfloat16),
-        scratch_shapes=[pltpu.VMEM((tokens, width), jnp.bfloat16), pltpu.SemaphoreType.DMA((tokens // ROWS,))],
+        scratch_shapes=[pltpu.VMEM((tokens, width), jnp.bfloat16), pltpu.SemaphoreType.DMA((tokens // BLOCK,))],
         compiler_params=pltpu.CompilerParams(vmem_limit_bytes=12 * MIB),
         cost_estimate=SMALL,
         name="scale",
-    )(inner, growth, queries, entry, gain.reshape(1, width), square)
+    )(out, square)
 
 
 def own_pages(owner_ref, place, page_of):
@@ -489,14 +484,14 @@
         ends[offset] = swap(end, "seq", offset)
     ends[1] = swap(end, "seq", 1)
     mids[1] = swap(mid, "seq", 1)
-    inner, growth, done = run_inner(keys, values, held, cumulative, states, reached)
+    inner, grown, done = run_inner(keys, values, held, cumulative, states, reached)
     mid = tie(mid, done, ends[1], mids[1])
     for offset in range(2, count, 2):
         mids[offset] = swap(mid, "seq", offset)
     for offset in range(2, count, 2):
         ends[offset + 1] = swap(tie(ends[offset], done), "seq", 1)
     ends = [ends[offset] for offset in range(count)]
-    square, entry = run_finish(inner, growth, held, ends, heads)
+    out, square = run_finish(inner, grown, norm_gain, ends, heads)
     totals = []
     shares = [(0, 3), (3, SLOTS - 3)]
     offset = 1
@@ -506,13 +501,16 @@
             totals.append(run_reach(tie(page_owner, square), ends, heads, *shares.pop(0)))
             other = tie(other, totals[-1])
         square = add(square, other)
+        if offset == 1:
+            for part in range(2, count, 2):
+                if part != count - 2:
+                    mids[part + 1] = swap(tie(mids[part], square), "seq", 1)
         offset *= 2
     for first, slots in shares:
         totals.append(run_reach(tie(page_owner, square), ends, heads, first, slots))
-    for offset in range(2, count, 2):
-        mids[offset + 1] = swap(tie(mids[offset], square), "seq", 1)
+    mids[count - 1] = swap(tie(mids[count - 2], square), "seq", 1)
     mids = [mids[offset] for offset in range(count)]
-    attended = run_scale(inner, growth, held, entry, norm_gain, square, width * lax.axis_size("head"), heads)
+    attended = run_scale(out, square, width * lax.axis_size("head"))
     page_cache = run_cache(page_owner, mids, totals)
     return attended, page_cache.reshape(SLOTS, heads, dim, dim)
 

time: 43.7 us -> 42.3 us (0.968)
  Pallas kernels: 26.9 us -> 24.5 us
  starting transfers between devices: 13.9 us -> 14.4 us
    pallas_call x2, Pallas kernels: 3.91 us -> 2.18 us  [run_reach(): pl.pallas_call(functools.partial(reach_kernel, heads, first), in_specs=[S...]
    pallas_call x1, Pallas kernels: 3.77 us -> 2.38 us  [run_scale(): pl.pallas_call(functools.partial(scale_kernel, whole_width), grid=(tokens...]
    pallas_call x1, Pallas kernels: 9.56 us -> 10.3 us  [run_inner(): pl.pallas_call(functools.partial(inner_kernel, heads), grid=(tokens // RO...]
    ppermute x16, starting transfers between devices: 13.9 us -> 14.4 us  [swap(): lax.ppermute(value, axis, [(place, place ^ offset) for place in range(lax...]
  transfers between devices with their start and end apart: 16 -> 16, of which waited for: 3 -> 5; matrix products, arithmetic and copies ran while one was open for 0% -> 0% of each run, Pallas kernels for 47% -> 43%
where the time goes in v5:
time: 42.3 us; the launch traced here: 42 us
  Pallas kernels  24.5 us (58%)
  starting transfers between devices  14.4 us (34%)
  waiting for transfers between devices  2.41 us (6%)
  between operations  0.73 us (2%)
    ppermute x16, starting transfers between devices, swap(): lax.ppermute(value, axis, [(place, place ^ offset) for place in range(lax...  14.4 us
    pallas_call x1, Pallas kernels, run_inner(): pl.pallas_call(functools.partial(inner_kernel, heads), grid=(tokens // RO...  10.3 us
    pallas_call x1, Pallas kernels, run_states(): pl.pallas_call(functools.partial(state_kernel, heads), in_specs=[HBM] * 3...  4.47 us
    pallas_call x1, Pallas kernels, run_finish(): pl.pallas_call(functools.partial(finish_kernel, heads), grid=(tokens // R...  3.21 us
    ppermute x16, waiting for transfers between devices, swap(): lax.ppermute(value, axis, [(place, place ^ offset) for place in range(lax...  2.41 us
    pallas_call x1, Pallas kernels, run_scale(): pl.pallas_call(functools.partial(scale_kernel, whole_width), grid=(tokens...  2.38 us
    pallas_call x2, Pallas kernels, run_reach(): pl.pallas_call(functools.partial(reach_kernel, heads, first), in_specs=[S...  2.18 us
    pallas_call x1, Pallas kernels, run_cache(): pl.pallas_call(functools.partial(cache_kernel, count), in_specs=[SMEM] +...  1.96 us
  transfers between devices with their start and end apart: 16, of which 5 were waited for; matrix products, arithmetic and copies ran while one was open for 0% of the time, Pallas kernels for 43%

profile of v5, /device:TPU:0, one launch (start us, length us, event | category | flops | bytes accessed | tf_op | source)
XLA Modules:
  0.0 42.0 jit_solution(5378574021218454326)
XLA Ops:
  0.6 0.0 copy-start
  0.6 4.5 %states.1 = (f32[8,2048]{1,0:T(8,128)S(1)}, bf16[8,1024,128]{2,1,0:T(8,128)(2,1)S(1)}, f32[8,8,128]{2,1,0:T(8,128)S(1)}, bf16[1072,128]{1,0:T(8,128)(2,1)S(1)}, ...) custom-call(bf16[2048,1024]{1,0:T(8,128)(2,1)} %key_hbm.1, ...), custom_call_target="tpu_custom_call" | custom-call | flops 1 | bytes 1 | tf_op jit(solution)/shard_map/states/pallas_call | solution.py:115
  5.1 4.0 %collective-permute-start.5 = (bf16[1072,128]{1,0:T(8,128)(2,1)S(1)}, bf16[1072,128]{1,0:T(8,128)(2,1)S(1)}, u32[]{:S(2)}, u32[]{:S(2)}) collective-permute-start(bf16[1072,128]{1,0:T(8,128)(2,1)S(1)} %get-tuple-element.34.refs_0_), channel_id=1, source_target_pairs={{0,24},{4,28},{8,16},{12,20},{16,8},{20,12},{24,0},{28,4},{1,25},{... | collective-permute-start | bytes 823304 | tf_op jit(solution)/shard_map/ppermute | solution.py:452
  9.1 0.5 %collective-permute-start.3 = (bf16[1072,128]{1,0:T(8,128)(2,1)S(1)}, bf16[1072,128]{1,0:T(8,128)(2,1)S(1)}, u32[]{:S(2)}, u32[]{:S(2)}) collective-permute-start(bf16[1072,128]{1,0:T(8,128)(2,1)S(1)} %get-tuple-element.34.refs_0_), channel_id=1, source_target_pairs={{0,16},{4,20},{8,24},{12,28},{16,0},{20,4},{24,8},{28,12},{1,17},{... | collective-permute-start | bytes 823304 | tf_op jit(solution)/shard_map/ppermute | solution.py:452
  9.6 0.1 collective-permute-start.1
  9.7 0.0 collective-permute-start
  9.7 0.0 copy-done
  9.7 0.0 copy-start.2
  9.7 10.3 %inner.1 = (f32[2048,1024]{1,0:T(8,128)S(1)}, bf16[2048,1024]{1,0:T(8,128)(2,1)S(1)}, f32[8,128]{1,0:T(8,128)}) custom-call(bf16[2048,1024]{1,0:T(8,128)(2,1)S(1)} %get-tuple-element.26.keys, bf16[2048,1024]{1,0:T(8,128)(2,1)S(1)} %get-tuple-element.27.values, bf16[2048,1024]{1,0:T(8,128)(2,1)S(1)} %copy-done, f32[8,2048]{1,0:T(8,128)S(1)} %get-tuple-element.28.cum_ref, ...), custom_call_target="tpu_custom_call" | custom-call | flops 1 | bytes 1 | tf_op jit(solution)/shard_map/inner/pallas_call | solution.py:193
  20.0 0.0 collective-permute-done.5.refs_6_
  20.0 0.5 %collective-permute-start.6 = (bf16[1072,128]{1,0:T(8,128)(2,1)S(1)}, bf16[1072,128]{1,0:T(8,128)(2,1)S(1)}, u32[]{:S(2)}, u32[]{:S(2)}) collective-permute-start(bf16[1072,128]{1,0:T(8,128)(2,1)S(1)} %collective-permute-done.5.refs_6_), channel_id=1, source_target_pairs={{0,4},{4,0},{8,12},{12,8},{16,20},{20,16},{24,28},{28,24},{1,5},{5... | collective-permute-start | bytes 823304 | tf_op jit(solution)/shard_map/ppermute | solution.py:452
  20.5 0.0 collective-permute-start.9
  20.5 1.0 %collective-permute-done.3.refs_4_ = bf16[1072,128]{1,0:T(8,128)(2,1)S(1)} collective-permute-done((bf16[1072,128]{1,0:T(8,128)(2,1)S(1)}, bf16[1072,128]{1,0:T(8,128)(2,1)S(1)}, u32[]{:S(2)}, u32[]{:S(2)}) %collective-permute-start.3) | collective-permute-done | bytes 274464 | tf_op jit(solution)/shard_map/ppermute | solution.py:452
  21.5 0.0 collective-permute-start.4
  21.5 0.3 collective-permute-done.1.refs_2_
  21.8 0.2 collective-permute-start.2
  22.0 0.0 collective-permute-done.9.refs_1_
  22.1 0.0 collective-permute-done.refs_1_
  22.1 1.9 %collective-permute-start.12 = (bf16[1024,128]{1,0:T(8,128)(2,1)S(1)}, bf16[1024,128]{1,0:T(8,128)(2,1)S(1)}, u32[]{:S(2)}, u32[]{:S(2)}) collective-permute-start(bf16[1024,128]{1,0:T(8,128)(2,1)S(1)} %get-tuple-element.46.refs_0_), channel_id=1, source_target_pairs={{0,16},{4,20},{8,24},{12,28},{16,0},{20,4},{24,8},{28,12},{1,17},{... | collective-permute-start | bytes 786440 | tf_op jit(solution)/shard_map/ppermute | solution.py:452
  24.0 1.5 %collective-permute-start.10 = (bf16[1024,128]{1,0:T(8,128)(2,1)S(1)}, bf16[1024,128]{1,0:T(8,128)(2,1)S(1)}, u32[]{:S(2)}, u32[]{:S(2)}) collective-permute-start(bf16[1024,128]{1,0:T(8,128)(2,1)S(1)} %get-tuple-element.46.refs_0_), channel_id=1, source_target_pairs={{0,8},{4,12},{8,0},{12,4},{16,24},{20,28},{24,16},{28,20},{1,9},{5... | collective-permute-start | bytes 786440 | tf_op jit(solution)/shard_map/ppermute | solution.py:452
  25.5 0.0 collective-permute-done.6.refs_7_
  25.5 0.1 collective-permute-start.14
  25.6 0.0 collective-permute-done.4.refs_5_
  25.6 0.0 collective-permute-done.2.refs_3_
  25.6 0.0 copy-done.2
  25.6 0.0 copy-start.1
  25.6 3.2 %finish.1 = (f32[2048,1024]{1,0:T(8,128)S(1)}, f32[16,128]{1,0:T(8,128)S(1)}) custom-call(f32[2048,1024]{1,0:T(8,128)S(1)} %get-tuple-element.32.inner_ref, bf16[2048,1024]{1,0:T(8,128)(2,1)S(1)} %get-tuple-element.33.grown, f32[1,1024]{1,0:T(1,128)S(1)} %bitcast.2, bf16[1072,128]{1,0:T(8,128)(2,1)S(1)} %get-tuple-element.34.refs_0_, ...), custom_call_target="tpu_custom_call" | custom-call | flops 1 | bytes 1 | tf_op jit(solution)/shard_map/finish/pallas_call | solution.py:276
  28.8 2.0 %collective-permute-start.7 = (f32[16,128]{1,0:T(8,128)S(1)}, f32[16,128]{1,0:T(8,128)S(1)}, u32[]{:S(2)}, u32[]{:S(2)}) collective-permute-start(f32[16,128]{1,0:T(8,128)S(1)} %get-tuple-element.40.one_ref), channel_id=1, source_target_pairs={{0,1},{1,0},{2,3},{3,2},{4,5},{5,4},{6,7},{7,6},{8,9},{9,8},{10,11... | collective-permute-start | bytes 24584 | tf_op jit(solution)/shard_map/ppermute | solution.py:452
  30.8 0.0 copy-done.1
  30.8 1.3 %reach.2.refs_8_ = f32[3,1024,128]{2,1,0:T(8,128)S(1)} custom-call(s32[16]{0:T(128)S(1)} %copy-done.1, bf16[1072,128]{1,0:T(8,128)(2,1)S(1)} %get-tuple-element.34.refs_0_, bf16[1072,128]{1,0:T(8,128)(2,1)S(1)} %collective-permute-done.refs_1_, bf16[1072,128]{1,0:T(8,128)(2,1)S(1)} %collective-permute-done.1.refs_2_, ...), custom_call_target="tpu_custom_call" | custom-call | flops 1 | bytes 1 | tf_op jit(solution)/shard_map/reach/pallas_call | solution.py:388
  32.2 0.3 collective-permute-done.7.two_ref
  32.5 3.0 %collective-permute-start.8 = (f32[16,128]{1,0:T(8,128)S(1)}, f32[16,128]{1,0:T(8,128)S(1)}, u32[]{:S(2)}, u32[]{:S(2)}) collective-permute-start(f32[16,128]{1,0:T(8,128)S(1)} %add.2.one_ref), channel_id=1, source_target_pairs={{0,2},{1,3},{2,0},{3,1},{4,6},{5,7},{6,4},{7,5},{8,10},{9,11},{10,... | collective-permute-start | bytes 24584 | tf_op jit(solution)/shard_map/ppermute | solution.py:452
  35.5 0.0 collective-permute-done.12.refs_4_
  35.5 0.0 collective-permute-start.13
  35.5 0.0 collective-permute-done.10.refs_2_
  35.5 0.5 %collective-permute-start.11 = (bf16[1024,128]{1,0:T(8,128)(2,1)S(1)}, bf16[1024,128]{1,0:T(8,128)(2,1)S(1)}, u32[]{:S(2)}, u32[]{:S(2)}) collective-permute-start(bf16[1024,128]{1,0:T(8,128)(2,1)S(1)} %collective-permute-done.10.refs_2_), channel_id=1, source_target_pairs={{0,4},{4,0},{8,12},{12,8},{16,20},{20,16},{24,28},{28,24},{1,5},{5... | collective-permute-start | bytes 786440 | tf_op jit(solution)/shard_map/ppermute | solution.py:452
  36.0 0.8 %reach.3.refs_9_ = f32[2,1024,128]{2,1,0:T(8,128)S(1)} custom-call(s32[16]{0:T(128)S(1)} %copy-done.1, bf16[1072,128]{1,0:T(8,128)(2,1)S(1)} %get-tuple-element.34.refs_0_, bf16[1072,128]{1,0:T(8,128)(2,1)S(1)} %collective-permute-done.refs_1_, bf16[1072,128]{1,0:T(8,128)(2,1)S(1)} %collective-permute-done.1.refs_2_, ...), custom_call_target="tpu_custom_call" | custom-call | flops 1 | bytes 1 | tf_op jit(solution)/shard_map/reach/pallas_call | solution.py:388
  36.9 0.3 collective-permute-done.8.two_ref
  37.2 0.5 %collective-permute-done.14.refs_6_ = bf16[1024,128]{1,0:T(8,128)(2,1)S(1)} collective-permute-done((bf16[1024,128]{1,0:T(8,128)(2,1)S(1)}, bf16[1024,128]{1,0:T(8,128)(2,1)S(1)}, u32[]{:S(2)}, u32[]{:S(2)}) %collective-permute-start.14) | collective-permute-done | bytes 262176 | tf_op jit(solution)/shard_map/ppermute | solution.py:452
  37.7 0.0 collective-permute-start.15
  37.7 2.4 %scale.1 = bf16[2048,1024]{1,0:T(8,128)(2,1)} custom-call(f32[2048,1024]{1,0:T(8,128)S(1)} %get-tuple-element.39.out_ref, f32[16,128]{1,0:T(8,128)S(1)} %add.3.square), custom_call_target="tpu_custom_call" | custom-call | flops 1 | bytes 1 | tf_op jit(solution)/shard_map/scale/pallas_call | solution.py:322
  40.1 0.0 collective-permute-done.13.refs_5_
  40.1 0.0 collective-permute-done.11.refs_3_
  40.1 0.0 collective-permute-done.15.refs_7_
  40.1 2.0 %cache.1 = bf16[5,1024,128]{2,1,0:T(8,128)(2,1)} custom-call(s32[16]{0:T(128)S(1)} %copy-done.1, bf16[1024,128]{1,0:T(8,128)(2,1)S(1)} %get-tuple-element.46.refs_0_, bf16[1024,128]{1,0:T(8,128)(2,1)S(1)} %collective-permute-done.9.refs_1_, bf16[1024,128]{1,0:T(8,128)(2,1)S(1)} %collective-permute-done.10.refs_2_, ...), custom_call_target="tpu_custom_call" | custom-call | flops 1 | bytes 1 | tf_op jit(solution)/shard_map/cache/pallas_call | solution.py:435
  (2 shorter events, 0.0 us)
Async XLA Ops:
  0.6 9.1 %copy-start = (bf16[2048,1024]{1,0:T(8,128)(2,1)S(1)}, bf16[2048,1024]{1,0:T(8,128)(2,1)}, u32[]{:S(2)}) copy-start(bf16[2048,1024]{1,0:T(8,128)(2,1)} %queries) | copy-start | bytes 12582916
  5.1 14.9 %collective-permute-start.5 = (bf16[1072,128]{1,0:T(8,128)(2,1)S(1)}, bf16[1072,128]{1,0:T(8,128)(2,1)S(1)}, u32[]{:S(2)}, u32[]{:S(2)}) collective-permute-start(bf16[1072,128]{1,0:T(8,128)(2,1)S(1)} %get-tuple-element.34.refs_0_), channel_id=1, source_target_pairs={{0,24},{4,28},{8,16},{12,20},{16,8},{20,12},{24,0},{28,4},{1,25},{... | collective-permute-start | bytes 823304 | tf_op jit(solution)/shard_map/ppermute | solution.py:452
  9.1 12.5 %collective-permute-start.3 = (bf16[1072,128]{1,0:T(8,128)(2,1)S(1)}, bf16[1072,128]{1,0:T(8,128)(2,1)S(1)}, u32[]{:S(2)}, u32[]{:S(2)}) collective-permute-start(bf16[1072,128]{1,0:T(8,128)(2,1)S(1)} %get-tuple-element.34.refs_0_), channel_id=1, source_target_pairs={{0,16},{4,20},{8,24},{12,28},{16,0},{20,4},{24,8},{28,12},{1,17},{... | collective-permute-start | bytes 823304 | tf_op jit(solution)/shard_map/ppermute | solution.py:452
  9.6 12.2 %collective-permute-start.1 = (bf16[1072,128]{1,0:T(8,128)(2,1)S(1)}, bf16[1072,128]{1,0:T(8,128)(2,1)S(1)}, u32[]{:S(2)}, u32[]{:S(2)}) collective-permute-start(bf16[1072,128]{1,0:T(8,128)(2,1)S(1)} %get-tuple-element.34.refs_0_), channel_id=1, source_target_pairs={{0,8},{4,12},{8,0},{12,4},{16,24},{20,28},{24,16},{28,20},{1,9},{5... | collective-permute-start | bytes 823304 | tf_op jit(solution)/shard_map/ppermute | solution.py:452
  9.7 12.4 %collective-permute-start = (bf16[1072,128]{1,0:T(8,128)(2,1)S(1)}, bf16[1072,128]{1,0:T(8,128)(2,1)S(1)}, u32[]{:S(2)}, u32[]{:S(2)}) collective-permute-start(bf16[1072,128]{1,0:T(8,128)(2,1)S(1)} %get-tuple-element.34.refs_0_), channel_id=1, source_target_pairs={{0,4},{4,0},{8,12},{12,8},{16,20},{20,16},{24,28},{28,24},{1,5},{5... | collective-permute-start | bytes 823304 | tf_op jit(solution)/shard_map/ppermute | solution.py:452
  9.7 15.9 %copy-start.2 = (f32[1024]{0:T(1024)S(1)}, f32[1024]{0:T(1024)}, u32[]{:S(2)}) copy-start(f32[1024]{0:T(1024)} %param.10) | copy-start | bytes 12292
  20.0 5.5 %collective-permute-start.6 = (bf16[1072,128]{1,0:T(8,128)(2,1)S(1)}, bf16[1072,128]{1,0:T(8,128)(2,1)S(1)}, u32[]{:S(2)}, u32[]{:S(2)}) collective-permute-start(bf16[1072,128]{1,0:T(8,128)(2,1)S(1)} %collective-permute-done.5.refs_6_), channel_id=1, source_target_pairs={{0,4},{4,0},{8,12},{12,8},{16,20},{20,16},{24,28},{28,24},{1,5},{5... | collective-permute-start | bytes 823304 | tf_op jit(solution)/shard_map/ppermute | solution.py:452
  20.5 1.6 %collective-permute-start.9 = (bf16[1024,128]{1,0:T(8,128)(2,1)S(1)}, bf16[1024,128]{1,0:T(8,128)(2,1)S(1)}, u32[]{:S(2)}, u32[]{:S(2)}) collective-permute-start(bf16[1024,128]{1,0:T(8,128)(2,1)S(1)} %get-tuple-element.46.refs_0_), channel_id=1, source_target_pairs={{0,4},{4,0},{8,12},{12,8},{16,20},{20,16},{24,28},{28,24},{1,5},{5... | collective-permute-start | bytes 786440 | tf_op jit(solution)/shard_map/ppermute | solution.py:452
  21.5 4.1 %collective-permute-start.4 = (bf16[1072,128]{1,0:T(8,128)(2,1)S(1)}, bf16[1072,128]{1,0:T(8,128)(2,1)S(1)}, u32[]{:S(2)}, u32[]{:S(2)}) collective-permute-start(bf16[1072,128]{1,0:T(8,128)(2,1)S(1)} %collective-permute-done.3.refs_4_), channel_id=1, source_target_pairs={{0,4},{4,0},{8,12},{12,8},{16,20},{20,16},{24,28},{28,24},{1,5},{5... | collective-permute-start | bytes 823304 | tf_op jit(solution)/shard_map/ppermute | solution.py:452
  21.8 3.8 %collective-permute-start.2 = (bf16[1072,128]{1,0:T(8,128)(2,1)S(1)}, bf16[1072,128]{1,0:T(8,128)(2,1)S(1)}, u32[]{:S(2)}, u32[]{:S(2)}) collective-permute-start(bf16[1072,128]{1,0:T(8,128)(2,1)S(1)} %collective-permute-done.1.refs_2_), channel_id=1, source_target_pairs={{0,4},{4,0},{8,12},{12,8},{16,20},{20,16},{24,28},{28,24},{1,5},{5... | collective-permute-start | bytes 823304 | tf_op jit(solution)/shard_map/ppermute | solution.py:452
  22.1 13.4 %collective-permute-start.12 = (bf16[1024,128]{1,0:T(8,128)(2,1)S(1)}, bf16[1024,128]{1,0:T(8,128)(2,1)S(1)}, u32[]{:S(2)}, u32[]{:S(2)}) collective-permute-start(bf16[1024,128]{1,0:T(8,128)(2,1)S(1)} %get-tuple-element.46.refs_0_), channel_id=1, source_target_pairs={{0,16},{4,20},{8,24},{12,28},{16,0},{20,4},{24,8},{28,12},{1,17},{... | collective-permute-start | bytes 786440 | tf_op jit(solution)/shard_map/ppermute | solution.py:452
  24.0 11.5 %collective-permute-start.10 = (bf16[1024,128]{1,0:T(8,128)(2,1)S(1)}, bf16[1024,128]{1,0:T(8,128)(2,1)S(1)}, u32[]{:S(2)}, u32[]{:S(2)}) collective-permute-start(bf16[1024,128]{1,0:T(8,128)(2,1)S(1)} %get-tuple-element.46.refs_0_), channel_id=1, source_target_pairs={{0,8},{4,12},{8,0},{12,4},{16,24},{20,28},{24,16},{28,20},{1,9},{5... | collective-permute-start | bytes 786440 | tf_op jit(solution)/shard_map/ppermute | solution.py:452
  25.5 12.1 %collective-permute-start.14 = (bf16[1024,128]{1,0:T(8,128)(2,1)S(1)}, bf16[1024,128]{1,0:T(8,128)(2,1)S(1)}, u32[]{:S(2)}, u32[]{:S(2)}) collective-permute-start(bf16[1024,128]{1,0:T(8,128)(2,1)S(1)} %get-tuple-element.46.refs_0_), channel_id=1, source_target_pairs={{0,24},{4,28},{8,16},{12,20},{16,8},{20,12},{24,0},{28,4},{1,25},{... | collective-permute-start | bytes 786440 | tf_op jit(solution)/shard_map/ppermute | solution.py:452
  25.6 5.2 %copy-start.1 = (s32[16]{0:T(128)S(1)}, s32[16]{0:T(128)}, u32[]{:S(2)}) copy-start(s32[16]{0:T(128)} %owner_ref.3) | copy-start | bytes 196
  28.8 3.7 %collective-permute-start.7 = (f32[16,128]{1,0:T(8,128)S(1)}, f32[16,128]{1,0:T(8,128)S(1)}, u32[]{:S(2)}, u32[]{:S(2)}) collective-permute-start(f32[16,128]{1,0:T(8,128)S(1)} %get-tuple-element.40.one_ref), channel_id=1, source_target_pairs={{0,1},{1,0},{2,3},{3,2},{4,5},{5,4},{6,7},{7,6},{8,9},{9,8},{10,11... | collective-permute-start | bytes 24584 | tf_op jit(solution)/shard_map/ppermute | solution.py:452
  32.5 4.6 %collective-permute-start.8 = (f32[16,128]{1,0:T(8,128)S(1)}, f32[16,128]{1,0:T(8,128)S(1)}, u32[]{:S(2)}, u32[]{:S(2)}) collective-permute-start(f32[16,128]{1,0:T(8,128)S(1)} %add.2.one_ref), channel_id=1, source_target_pairs={{0,2},{1,3},{2,0},{3,1},{4,6},{5,7},{6,4},{7,5},{8,10},{9,11},{10,... | collective-permute-start | bytes 24584 | tf_op jit(solution)/shard_map/ppermute | solution.py:452
  35.5 4.5 %collective-permute-start.13 = (bf16[1024,128]{1,0:T(8,128)(2,1)S(1)}, bf16[1024,128]{1,0:T(8,128)(2,1)S(1)}, u32[]{:S(2)}, u32[]{:S(2)}) collective-permute-start(bf16[1024,128]{1,0:T(8,128)(2,1)S(1)} %collective-permute-done.12.refs_4_), channel_id=1, source_target_pairs={{0,4},{4,0},{8,12},{12,8},{16,20},{20,16},{24,28},{28,24},{1,5},{5... | collective-permute-start | bytes 786440 | tf_op jit(solution)/shard_map/ppermute | solution.py:452
  35.5 4.5 %collective-permute-start.11 = (bf16[1024,128]{1,0:T(8,128)(2,1)S(1)}, bf16[1024,128]{1,0:T(8,128)(2,1)S(1)}, u32[]{:S(2)}, u32[]{:S(2)}) collective-permute-start(bf16[1024,128]{1,0:T(8,128)(2,1)S(1)} %collective-permute-done.10.refs_2_), channel_id=1, source_target_pairs={{0,4},{4,0},{8,12},{12,8},{16,20},{20,16},{24,28},{28,24},{1,5},{5... | collective-permute-start | bytes 786440 | tf_op jit(solution)/shard_map/ppermute | solution.py:452
  37.7 2.4 %collective-permute-start.15 = (bf16[1024,128]{1,0:T(8,128)(2,1)S(1)}, bf16[1024,128]{1,0:T(8,128)(2,1)S(1)}, u32[]{:S(2)}, u32[]{:S(2)}) collective-permute-start(bf16[1024,128]{1,0:T(8,128)(2,1)S(1)} %collective-permute-done.14.refs_6_), channel_id=1, source_target_pairs={{0,4},{4,0},{8,12},{12,8},{16,20},{20,16},{24,28},{28,24},{1,5},{5... | collective-permute-start | bytes 786440 | tf_op jit(solution)/shard_map/ppermute | solution.py:452

commit v6 on v5

--- a/solution.py
+++ b/solution.py
@@ -152,7 +152,7 @@
     cums = [cum_ref[:, rows] for rows in here]
     cum_cols = [cum.T for cum in cums]
     reached = [jnp.where(blk > 0, reached_ref[last], 0.0) for blk, last in zip(blks, before)]
-    items = [(head, part) for head in range(heads) for part in range(len(blks))]
+    items = [(pair + which, part) for pair in range(0, heads, 2) for part in range(len(blks)) for which in range(2)]
 
     def scores_of(head, part):
         lanes = slice(head * dim, (head + 1) * dim)
@@ -230,7 +230,8 @@
 def finish_kernel(heads, inner_ref, grown, gain_ref, *refs):
     *ends, out_ref, square_ref, entry, entry_low = refs
     blk = pl.program_id(0)
-    width = grown.shape[1]
+    tokens, width = grown.shape
+    length = PAGE
     dim = width // heads
     size = heads * dim
 
@@ -242,31 +243,31 @@
         gather_states(entry, ends, places, logs, place, jnp.zeros((heads, dim), jnp.float32), heads, dim)
         entry_low[...] = entry[...].astype(jnp.bfloat16)
 
-    here = pl.ds(pl.multiple_of(blk * ROWS, ROWS), ROWS)
+    here = pl.ds(pl.multiple_of(blk * length, length), length)
 
     def carried_of(pair):
         rows = [slice(head * dim, (head + 1) * dim) for head in (2 * pair, 2 * pair + 1)]
         query = grown[here, 2 * pair * dim : 2 * (pair + 1) * dim]
         return jnp.dot(query, pair_of(entry_low[rows[0]], entry_low[rows[1]]), preferred_element_type=jnp.float32)
 
-    total = jnp.zeros((ROWS, dim), jnp.float32)
+    total = jnp.zeros((length, dim), jnp.float32)
     ahead = carried_of(0)
     for pair in range(heads // 2):
         carried = ahead
         if pair + 1 < heads // 2:
             ahead = carried_of(pair + 1)
-        for which in range(2):
-            lanes = slice((2 * pair + which) * dim, (2 * pair + which + 1) * dim)
-            out = inner_ref[here, lanes] + carried[:, which * dim : (which + 1) * dim]
-            total += out * out
-            out_ref[here, lanes] = out * gain_ref[:, lanes]
+        lanes = slice(2 * pair * dim, 2 * (pair + 1) * dim)
+        out = inner_ref[here, lanes] + carried
+        squares = out * out
+        total += squares[:, :dim] + squares[:, dim:]
+        out_ref[here, lanes] = out * gain_ref[:, lanes]
     high = total.astype(jnp.bfloat16)
     low = (total - high.astype(jnp.float32)).astype(jnp.bfloat16)
     ones = jnp.ones((8, dim), jnp.bfloat16)
     sums = lax.dot_general(ones, high, NT, preferred_element_type=jnp.float32)
     sums = sums + lax.dot_general(ones, low, NT, preferred_element_type=jnp.float32)
-    for row in range(ROWS // 128):
-        square_ref[pl.ds(blk * (ROWS // 128) + row, 1)] = sums[:1, row * 128 : (row + 1) * 128]
+    for row in range(length // 128):
+        square_ref[pl.ds(blk * (length // 128) + row, 1)] = sums[:1, row * 128 : (row + 1) * 128]
 
 
 def run_finish(inner, grown, gain, ends, heads):
@@ -275,7 +276,7 @@
     size = heads * dim
     return pl.pallas_call(
         functools.partial(finish_kernel, heads),
-        grid=(tokens // ROWS,),
+        grid=(tokens // PAGE,),
         in_specs=[VMEM] * (3 + len(ends)),
         out_specs=[VMEM, VMEM],
         out_shape=[pltpu.VMEM((tokens, width), jnp.float32), pltpu.VMEM((tokens // 128, 128), jnp.float32)],

time: 42.3 us -> 41.9 us (level)
  waiting for transfers between devices: 2.41 us -> 3.66 us
  Pallas kernels: 24.5 us -> 23.4 us
  starting transfers between devices: 14.4 us -> 13.9 us
    ppermute x16, waiting for transfers between devices: 2.41 us -> 3.66 us  [swap(): lax.ppermute(value, axis, [(place, place ^ offset) for place in range(lax...]
    pallas_call x1, Pallas kernels: 10.3 us -> 9.22 us  [run_inner(): pl.pallas_call(functools.partial(inner_kernel, heads), grid=(tokens // RO...]
    ppermute x16, starting transfers between devices: 14.4 us -> 13.9 us  [swap(): lax.ppermute(value, axis, [(place, place ^ offset) for place in range(lax...]
    pallas_call x1, Pallas kernels: 3.21 us -> 2.77 us  [run_finish(): pl.pallas_call(functools.partial(finish_kernel, heads), grid=(tokens // P...]
    pallas_call x2, Pallas kernels: 2.18 us -> 2.62 us  [run_reach(): pl.pallas_call(functools.partial(reach_kernel, heads, first), in_specs=[S...]
  transfers between devices with their start and end apart: 16 -> 16, of which waited for: 5 -> 5; matrix products, arithmetic and copies ran while one was open for 0% -> 0% of each run, Pallas kernels for 43% -> 41%
where the time goes in v6:
time: 41.9 us; the launch traced here: 41.7 us
  Pallas kernels  23.4 us (56%)
  starting transfers between devices  13.9 us (33%)
  waiting for transfers between devices  3.66 us (9%)
  between operations  0.73 us (2%)
    ppermute x16, starting transfers between devices, swap(): lax.ppermute(value, axis, [(place, place ^ offset) for place in range(lax...  13.9 us
    pallas_call x1, Pallas kernels, run_inner(): pl.pallas_call(functools.partial(inner_kernel, heads), grid=(tokens // RO...  9.22 us
    pallas_call x1, Pallas kernels, run_states(): pl.pallas_call(functools.partial(state_kernel, heads), in_specs=[HBM] * 3...  4.47 us
    ppermute x16, waiting for transfers between devices, swap(): lax.ppermute(value, axis, [(place, place ^ offset) for place in range(lax...  3.66 us
    pallas_call x1, Pallas kernels, run_finish(): pl.pallas_call(functools.partial(finish_kernel, heads), grid=(tokens // P...  2.77 us
    pallas_call x2, Pallas kernels, run_reach(): pl.pallas_call(functools.partial(reach_kernel, heads, first), in_specs=[S...  2.62 us
    pallas_call x1, Pallas kernels, run_scale(): pl.pallas_call(functools.partial(scale_kernel, whole_width), grid=(tokens...  2.38 us
    pallas_call x1, Pallas kernels, run_cache(): pl.pallas_call(functools.partial(cache_kernel, count), in_specs=[SMEM] +...  1.95 us
  transfers between devices with their start and end apart: 16, of which 5 were waited for; matrix products, arithmetic and copies ran while one was open for 0% of the time, Pallas kernels for 41%

profile of v6, /device:TPU:0, one launch (start us, length us, event | category | flops | bytes accessed | tf_op | source)
XLA Modules:
  0.0 41.7 jit_solution(2216679581786279498)
XLA Ops:
  0.6 0.0 copy-start
  0.6 4.5 %states.1 = (f32[8,2048]{1,0:T(8,128)S(1)}, bf16[8,1024,128]{2,1,0:T(8,128)(2,1)S(1)}, f32[8,8,128]{2,1,0:T(8,128)S(1)}, bf16[1072,128]{1,0:T(8,128)(2,1)S(1)}, ...) custom-call(bf16[2048,1024]{1,0:T(8,128)(2,1)} %key_hbm.1, ...), custom_call_target="tpu_custom_call" | custom-call | flops 1 | bytes 1 | tf_op jit(solution)/shard_map/states/pallas_call | solution.py:115
  5.1 4.0 %collective-permute-start.5 = (bf16[1072,128]{1,0:T(8,128)(2,1)S(1)}, bf16[1072,128]{1,0:T(8,128)(2,1)S(1)}, u32[]{:S(2)}, u32[]{:S(2)}) collective-permute-start(bf16[1072,128]{1,0:T(8,128)(2,1)S(1)} %get-tuple-element.34.refs_0_), channel_id=1, source_target_pairs={{0,24},{4,28},{8,16},{12,20},{16,8},{20,12},{24,0},{28,4},{1,25},{... | collective-permute-start | bytes 823304 | tf_op jit(solution)/shard_map/ppermute | solution.py:453
  9.1 0.5 %collective-permute-start.3 = (bf16[1072,128]{1,0:T(8,128)(2,1)S(1)}, bf16[1072,128]{1,0:T(8,128)(2,1)S(1)}, u32[]{:S(2)}, u32[]{:S(2)}) collective-permute-start(bf16[1072,128]{1,0:T(8,128)(2,1)S(1)} %get-tuple-element.34.refs_0_), channel_id=1, source_target_pairs={{0,16},{4,20},{8,24},{12,28},{16,0},{20,4},{24,8},{28,12},{1,17},{... | collective-permute-start | bytes 823304 | tf_op jit(solution)/shard_map/ppermute | solution.py:453
  9.6 0.1 collective-permute-start.1
  9.7 0.0 collective-permute-start
  9.7 0.0 copy-done
  9.7 0.0 copy-start.2
  9.7 9.2 %inner.1 = (f32[2048,1024]{1,0:T(8,128)S(1)}, bf16[2048,1024]{1,0:T(8,128)(2,1)S(1)}, f32[8,128]{1,0:T(8,128)}) custom-call(bf16[2048,1024]{1,0:T(8,128)(2,1)S(1)} %get-tuple-element.26.keys, bf16[2048,1024]{1,0:T(8,128)(2,1)S(1)} %get-tuple-element.27.values, bf16[2048,1024]{1,0:T(8,128)(2,1)S(1)} %copy-done, f32[8,2048]{1,0:T(8,128)S(1)} %get-tuple-element.28.cum_ref, ...), custom_call_target="tpu_custom_call" | custom-call | flops 1 | bytes 1 | tf_op jit(solution)/shard_map/inner/pallas_call | solution.py:193
  18.9 0.0 collective-permute-done.5.refs_6_
  19.0 0.5 %collective-permute-start.6 = (bf16[1072,128]{1,0:T(8,128)(2,1)S(1)}, bf16[1072,128]{1,0:T(8,128)(2,1)S(1)}, u32[]{:S(2)}, u32[]{:S(2)}) collective-permute-start(bf16[1072,128]{1,0:T(8,128)(2,1)S(1)} %collective-permute-done.5.refs_6_), channel_id=1, source_target_pairs={{0,4},{4,0},{8,12},{12,8},{16,20},{20,16},{24,28},{28,24},{1,5},{5... | collective-permute-start | bytes 823304 | tf_op jit(solution)/shard_map/ppermute | solution.py:453
  19.4 0.0 collective-permute-start.9
  19.5 2.1 %collective-permute-done.3.refs_4_ = bf16[1072,128]{1,0:T(8,128)(2,1)S(1)} collective-permute-done((bf16[1072,128]{1,0:T(8,128)(2,1)S(1)}, bf16[1072,128]{1,0:T(8,128)(2,1)S(1)}, u32[]{:S(2)}, u32[]{:S(2)}) %collective-permute-start.3) | collective-permute-done | bytes 274464 | tf_op jit(solution)/shard_map/ppermute | solution.py:453
  21.5 0.0 collective-permute-start.4
  21.5 0.3 collective-permute-done.1.refs_2_
  21.8 0.2 collective-permute-start.2
  22.0 0.0 collective-permute-done.9.refs_1_
  22.0 0.0 collective-permute-done.refs_1_
  22.1 1.7 %collective-permute-start.12 = (bf16[1024,128]{1,0:T(8,128)(2,1)S(1)}, bf16[1024,128]{1,0:T(8,128)(2,1)S(1)}, u32[]{:S(2)}, u32[]{:S(2)}) collective-permute-start(bf16[1024,128]{1,0:T(8,128)(2,1)S(1)} %get-tuple-element.46.refs_0_), channel_id=1, source_target_pairs={{0,16},{4,20},{8,24},{12,28},{16,0},{20,4},{24,8},{28,12},{1,17},{... | collective-permute-start | bytes 786440 | tf_op jit(solution)/shard_map/ppermute | solution.py:453
  23.8 0.7 %collective-permute-start.10 = (bf16[1024,128]{1,0:T(8,128)(2,1)S(1)}, bf16[1024,128]{1,0:T(8,128)(2,1)S(1)}, u32[]{:S(2)}, u32[]{:S(2)}) collective-permute-start(bf16[1024,128]{1,0:T(8,128)(2,1)S(1)} %get-tuple-element.46.refs_0_), channel_id=1, source_target_pairs={{0,8},{4,12},{8,0},{12,4},{16,24},{20,28},{24,16},{28,20},{1,9},{5... | collective-permute-start | bytes 786440 | tf_op jit(solution)/shard_map/ppermute | solution.py:453
  24.4 0.0 collective-permute-done.6.refs_7_
  24.4 1.1 %collective-permute-start.14 = (bf16[1024,128]{1,0:T(8,128)(2,1)S(1)}, bf16[1024,128]{1,0:T(8,128)(2,1)S(1)}, u32[]{:S(2)}, u32[]{:S(2)}) collective-permute-start(bf16[1024,128]{1,0:T(8,128)(2,1)S(1)} %get-tuple-element.46.refs_0_), channel_id=1, source_target_pairs={{0,24},{4,28},{8,16},{12,20},{16,8},{20,12},{24,0},{28,4},{1,25},{... | collective-permute-start | bytes 786440 | tf_op jit(solution)/shard_map/ppermute | solution.py:453
  25.5 0.0 collective-permute-done.4.refs_5_
  25.5 0.0 collective-permute-done.2.refs_3_
  25.6 0.0 copy-done.2
  25.6 0.0 copy-start.1
  25.6 2.8 %finish.1 = (f32[2048,1024]{1,0:T(8,128)S(1)}, f32[16,128]{1,0:T(8,128)S(1)}) custom-call(f32[2048,1024]{1,0:T(8,128)S(1)} %get-tuple-element.32.inner_ref, bf16[2048,1024]{1,0:T(8,128)(2,1)S(1)} %get-tuple-element.33.grown, f32[1,1024]{1,0:T(1,128)S(1)} %bitcast.2, bf16[1072,128]{1,0:T(8,128)(2,1)S(1)} %get-tuple-element.34.refs_0_, ...), custom_call_target="tpu_custom_call" | custom-call | flops 1 | bytes 1 | tf_op jit(solution)/shard_map/finish/pallas_call | solution.py:277
  28.3 1.8 %collective-permute-start.7 = (f32[16,128]{1,0:T(8,128)S(1)}, f32[16,128]{1,0:T(8,128)S(1)}, u32[]{:S(2)}, u32[]{:S(2)}) collective-permute-start(f32[16,128]{1,0:T(8,128)S(1)} %get-tuple-element.40.one_ref), channel_id=1, source_target_pairs={{0,1},{1,0},{2,3},{3,2},{4,5},{5,4},{6,7},{7,6},{8,9},{9,8},{10,11... | collective-permute-start | bytes 24584 | tf_op jit(solution)/shard_map/ppermute | solution.py:453
  30.1 0.0 copy-done.1
  30.1 1.8 %reach.2.refs_8_ = f32[3,1024,128]{2,1,0:T(8,128)S(1)} custom-call(s32[16]{0:T(128)S(1)} %copy-done.1, bf16[1072,128]{1,0:T(8,128)(2,1)S(1)} %get-tuple-element.34.refs_0_, bf16[1072,128]{1,0:T(8,128)(2,1)S(1)} %collective-permute-done.refs_1_, bf16[1072,128]{1,0:T(8,128)(2,1)S(1)} %collective-permute-done.1.refs_2_, ...), custom_call_target="tpu_custom_call" | custom-call | flops 1 | bytes 1 | tf_op jit(solution)/shard_map/reach/pallas_call | solution.py:389
  31.9 0.1 collective-permute-done.7.two_ref
  32.0 2.8 %collective-permute-start.8 = (f32[16,128]{1,0:T(8,128)S(1)}, f32[16,128]{1,0:T(8,128)S(1)}, u32[]{:S(2)}, u32[]{:S(2)}) collective-permute-start(f32[16,128]{1,0:T(8,128)S(1)} %add.2.one_ref), channel_id=1, source_target_pairs={{0,2},{1,3},{2,0},{3,1},{4,6},{5,7},{6,4},{7,5},{8,10},{9,11},{10,... | collective-permute-start | bytes 24584 | tf_op jit(solution)/shard_map/ppermute | solution.py:453
  34.8 0.0 collective-permute-done.12.refs_4_
  34.8 0.0 collective-permute-start.13
  34.8 0.0 collective-permute-done.10.refs_2_
  34.8 0.5 %collective-permute-start.11 = (bf16[1024,128]{1,0:T(8,128)(2,1)S(1)}, bf16[1024,128]{1,0:T(8,128)(2,1)S(1)}, u32[]{:S(2)}, u32[]{:S(2)}) collective-permute-start(bf16[1024,128]{1,0:T(8,128)(2,1)S(1)} %collective-permute-done.10.refs_2_), channel_id=1, source_target_pairs={{0,4},{4,0},{8,12},{12,8},{16,20},{20,16},{24,28},{28,24},{1,5},{5... | collective-permute-start | bytes 786440 | tf_op jit(solution)/shard_map/ppermute | solution.py:453
  35.3 0.8 %reach.3.refs_9_ = f32[2,1024,128]{2,1,0:T(8,128)S(1)} custom-call(s32[16]{0:T(128)S(1)} %copy-done.1, bf16[1072,128]{1,0:T(8,128)(2,1)S(1)} %get-tuple-element.34.refs_0_, bf16[1072,128]{1,0:T(8,128)(2,1)S(1)} %collective-permute-done.refs_1_, bf16[1072,128]{1,0:T(8,128)(2,1)S(1)} %collective-permute-done.1.refs_2_, ...), custom_call_target="tpu_custom_call" | custom-call | flops 1 | bytes 1 | tf_op jit(solution)/shard_map/reach/pallas_call | solution.py:389
  36.2 0.4 collective-permute-done.8.two_ref
  36.6 0.8 %collective-permute-done.14.refs_6_ = bf16[1024,128]{1,0:T(8,128)(2,1)S(1)} collective-permute-done((bf16[1024,128]{1,0:T(8,128)(2,1)S(1)}, bf16[1024,128]{1,0:T(8,128)(2,1)S(1)}, u32[]{:S(2)}, u32[]{:S(2)}) %collective-permute-start.14) | collective-permute-done | bytes 262176 | tf_op jit(solution)/shard_map/ppermute | solution.py:453
  37.4 0.0 collective-permute-start.15
  37.4 2.4 %scale.1 = bf16[2048,1024]{1,0:T(8,128)(2,1)} custom-call(f32[2048,1024]{1,0:T(8,128)S(1)} %get-tuple-element.39.out_ref, f32[16,128]{1,0:T(8,128)S(1)} %add.3.square), custom_call_target="tpu_custom_call" | custom-call | flops 1 | bytes 1 | tf_op jit(solution)/shard_map/scale/pallas_call | solution.py:323
  39.8 0.0 collective-permute-done.13.refs_5_
  39.8 0.0 collective-permute-done.11.refs_3_
  39.8 0.0 collective-permute-done.15.refs_7_
  39.8 1.9 %cache.1 = bf16[5,1024,128]{2,1,0:T(8,128)(2,1)} custom-call(s32[16]{0:T(128)S(1)} %copy-done.1, bf16[1024,128]{1,0:T(8,128)(2,1)S(1)} %get-tuple-element.46.refs_0_, bf16[1024,128]{1,0:T(8,128)(2,1)S(1)} %collective-permute-done.9.refs_1_, bf16[1024,128]{1,0:T(8,128)(2,1)S(1)} %collective-permute-done.10.refs_2_, ...), custom_call_target="tpu_custom_call" | custom-call | flops 1 | bytes 1 | tf_op jit(solution)/shard_map/cache/pallas_call | solution.py:436
  (2 shorter events, 0.0 us)
Async XLA Ops:
  0.6 9.1 %copy-start = (bf16[2048,1024]{1,0:T(8,128)(2,1)S(1)}, bf16[2048,1024]{1,0:T(8,128)(2,1)}, u32[]{:S(2)}) copy-start(bf16[2048,1024]{1,0:T(8,128)(2,1)} %queries) | copy-start | bytes 12582916
  5.1 13.8 %collective-permute-start.5 = (bf16[1072,128]{1,0:T(8,128)(2,1)S(1)}, bf16[1072,128]{1,0:T(8,128)(2,1)S(1)}, u32[]{:S(2)}, u32[]{:S(2)}) collective-permute-start(bf16[1072,128]{1,0:T(8,128)(2,1)S(1)} %get-tuple-element.34.refs_0_), channel_id=1, source_target_pairs={{0,24},{4,28},{8,16},{12,20},{16,8},{20,12},{24,0},{28,4},{1,25},{... | collective-permute-start | bytes 823304 | tf_op jit(solution)/shard_map/ppermute | solution.py:453
  9.1 12.5 %collective-permute-start.3 = (bf16[1072,128]{1,0:T(8,128)(2,1)S(1)}, bf16[1072,128]{1,0:T(8,128)(2,1)S(1)}, u32[]{:S(2)}, u32[]{:S(2)}) collective-permute-start(bf16[1072,128]{1,0:T(8,128)(2,1)S(1)} %get-tuple-element.34.refs_0_), channel_id=1, source_target_pairs={{0,16},{4,20},{8,24},{12,28},{16,0},{20,4},{24,8},{28,12},{1,17},{... | collective-permute-start | bytes 823304 | tf_op jit(solution)/shard_map/ppermute | solution.py:453
  9.6 12.2 %collective-permute-start.1 = (bf16[1072,128]{1,0:T(8,128)(2,1)S(1)}, bf16[1072,128]{1,0:T(8,128)(2,1)S(1)}, u32[]{:S(2)}, u32[]{:S(2)}) collective-permute-start(bf16[1072,128]{1,0:T(8,128)(2,1)S(1)} %get-tuple-element.34.refs_0_), channel_id=1, source_target_pairs={{0,8},{4,12},{8,0},{12,4},{16,24},{20,28},{24,16},{28,20},{1,9},{5... | collective-permute-start | bytes 823304 | tf_op jit(solution)/shard_map/ppermute | solution.py:453
  9.7 12.3 %collective-permute-start = (bf16[1072,128]{1,0:T(8,128)(2,1)S(1)}, bf16[1072,128]{1,0:T(8,128)(2,1)S(1)}, u32[]{:S(2)}, u32[]{:S(2)}) collective-permute-start(bf16[1072,128]{1,0:T(8,128)(2,1)S(1)} %get-tuple-element.34.refs_0_), channel_id=1, source_target_pairs={{0,4},{4,0},{8,12},{12,8},{16,20},{20,16},{24,28},{28,24},{1,5},{5... | collective-permute-start | bytes 823304 | tf_op jit(solution)/shard_map/ppermute | solution.py:453
  9.7 15.8 %copy-start.2 = (f32[1024]{0:T(1024)S(1)}, f32[1024]{0:T(1024)}, u32[]{:S(2)}) copy-start(f32[1024]{0:T(1024)} %param.10) | copy-start | bytes 12292
  19.0 5.5 %collective-permute-start.6 = (bf16[1072,128]{1,0:T(8,128)(2,1)S(1)}, bf16[1072,128]{1,0:T(8,128)(2,1)S(1)}, u32[]{:S(2)}, u32[]{:S(2)}) collective-permute-start(bf16[1072,128]{1,0:T(8,128)(2,1)S(1)} %collective-permute-done.5.refs_6_), channel_id=1, source_target_pairs={{0,4},{4,0},{8,12},{12,8},{16,20},{20,16},{24,28},{28,24},{1,5},{5... | collective-permute-start | bytes 823304 | tf_op jit(solution)/shard_map/ppermute | solution.py:453
  19.4 2.6 %collective-permute-start.9 = (bf16[1024,128]{1,0:T(8,128)(2,1)S(1)}, bf16[1024,128]{1,0:T(8,128)(2,1)S(1)}, u32[]{:S(2)}, u32[]{:S(2)}) collective-permute-start(bf16[1024,128]{1,0:T(8,128)(2,1)S(1)} %get-tuple-element.46.refs_0_), channel_id=1, source_target_pairs={{0,4},{4,0},{8,12},{12,8},{16,20},{20,16},{24,28},{28,24},{1,5},{5... | collective-permute-start | bytes 786440 | tf_op jit(solution)/shard_map/ppermute | solution.py:453
  21.5 4.0 %collective-permute-start.4 = (bf16[1072,128]{1,0:T(8,128)(2,1)S(1)}, bf16[1072,128]{1,0:T(8,128)(2,1)S(1)}, u32[]{:S(2)}, u32[]{:S(2)}) collective-permute-start(bf16[1072,128]{1,0:T(8,128)(2,1)S(1)} %collective-permute-done.3.refs_4_), channel_id=1, source_target_pairs={{0,4},{4,0},{8,12},{12,8},{16,20},{20,16},{24,28},{28,24},{1,5},{5... | collective-permute-start | bytes 823304 | tf_op jit(solution)/shard_map/ppermute | solution.py:453
  21.8 3.7 %collective-permute-start.2 = (bf16[1072,128]{1,0:T(8,128)(2,1)S(1)}, bf16[1072,128]{1,0:T(8,128)(2,1)S(1)}, u32[]{:S(2)}, u32[]{:S(2)}) collective-permute-start(bf16[1072,128]{1,0:T(8,128)(2,1)S(1)} %collective-permute-done.1.refs_2_), channel_id=1, source_target_pairs={{0,4},{4,0},{8,12},{12,8},{16,20},{20,16},{24,28},{28,24},{1,5},{5... | collective-permute-start | bytes 823304 | tf_op jit(solution)/shard_map/ppermute | solution.py:453
  22.1 12.8 %collective-permute-start.12 = (bf16[1024,128]{1,0:T(8,128)(2,1)S(1)}, bf16[1024,128]{1,0:T(8,128)(2,1)S(1)}, u32[]{:S(2)}, u32[]{:S(2)}) collective-permute-start(bf16[1024,128]{1,0:T(8,128)(2,1)S(1)} %get-tuple-element.46.refs_0_), channel_id=1, source_target_pairs={{0,16},{4,20},{8,24},{12,28},{16,0},{20,4},{24,8},{28,12},{1,17},{... | collective-permute-start | bytes 786440 | tf_op jit(solution)/shard_map/ppermute | solution.py:453
  23.8 11.0 %collective-permute-start.10 = (bf16[1024,128]{1,0:T(8,128)(2,1)S(1)}, bf16[1024,128]{1,0:T(8,128)(2,1)S(1)}, u32[]{:S(2)}, u32[]{:S(2)}) collective-permute-start(bf16[1024,128]{1,0:T(8,128)(2,1)S(1)} %get-tuple-element.46.refs_0_), channel_id=1, source_target_pairs={{0,8},{4,12},{8,0},{12,4},{16,24},{20,28},{24,16},{28,20},{1,9},{5... | collective-permute-start | bytes 786440 | tf_op jit(solution)/shard_map/ppermute | solution.py:453
  24.4 12.9 %collective-permute-start.14 = (bf16[1024,128]{1,0:T(8,128)(2,1)S(1)}, bf16[1024,128]{1,0:T(8,128)(2,1)S(1)}, u32[]{:S(2)}, u32[]{:S(2)}) collective-permute-start(bf16[1024,128]{1,0:T(8,128)(2,1)S(1)} %get-tuple-element.46.refs_0_), channel_id=1, source_target_pairs={{0,24},{4,28},{8,16},{12,20},{16,8},{20,12},{24,0},{28,4},{1,25},{... | collective-permute-start | bytes 786440 | tf_op jit(solution)/shard_map/ppermute | solution.py:453
  25.6 4.6 %copy-start.1 = (s32[16]{0:T(128)S(1)}, s32[16]{0:T(128)}, u32[]{:S(2)}) copy-start(s32[16]{0:T(128)} %owner_ref.3) | copy-start | bytes 196
  28.3 3.7 %collective-permute-start.7 = (f32[16,128]{1,0:T(8,128)S(1)}, f32[16,128]{1,0:T(8,128)S(1)}, u32[]{:S(2)}, u32[]{:S(2)}) collective-permute-start(f32[16,128]{1,0:T(8,128)S(1)} %get-tuple-element.40.one_ref), channel_id=1, source_target_pairs={{0,1},{1,0},{2,3},{3,2},{4,5},{5,4},{6,7},{7,6},{8,9},{9,8},{10,11... | collective-permute-start | bytes 24584 | tf_op jit(solution)/shard_map/ppermute | solution.py:453
  32.0 4.5 %collective-permute-start.8 = (f32[16,128]{1,0:T(8,128)S(1)}, f32[16,128]{1,0:T(8,128)S(1)}, u32[]{:S(2)}, u32[]{:S(2)}) collective-permute-start(f32[16,128]{1,0:T(8,128)S(1)} %add.2.one_ref), channel_id=1, source_target_pairs={{0,2},{1,3},{2,0},{3,1},{4,6},{5,7},{6,4},{7,5},{8,10},{9,11},{10,... | collective-permute-start | bytes 24584 | tf_op jit(solution)/shard_map/ppermute | solution.py:453
  34.8 4.9 %collective-permute-start.13 = (bf16[1024,128]{1,0:T(8,128)(2,1)S(1)}, bf16[1024,128]{1,0:T(8,128)(2,1)S(1)}, u32[]{:S(2)}, u32[]{:S(2)}) collective-permute-start(bf16[1024,128]{1,0:T(8,128)(2,1)S(1)} %collective-permute-done.12.refs_4_), channel_id=1, source_target_pairs={{0,4},{4,0},{8,12},{12,8},{16,20},{20,16},{24,28},{28,24},{1,5},{5... | collective-permute-start | bytes 786440 | tf_op jit(solution)/shard_map/ppermute | solution.py:453
  34.8 4.9 %collective-permute-start.11 = (bf16[1024,128]{1,0:T(8,128)(2,1)S(1)}, bf16[1024,128]{1,0:T(8,128)(2,1)S(1)}, u32[]{:S(2)}, u32[]{:S(2)}) collective-permute-start(bf16[1024,128]{1,0:T(8,128)(2,1)S(1)} %collective-permute-done.10.refs_2_), channel_id=1, source_target_pairs={{0,4},{4,0},{8,12},{12,8},{16,20},{20,16},{24,28},{28,24},{1,5},{5... | collective-permute-start | bytes 786440 | tf_op jit(solution)/shard_map/ppermute | solution.py:453
  37.4 2.4 %collective-permute-start.15 = (bf16[1024,128]{1,0:T(8,128)(2,1)S(1)}, bf16[1024,128]{1,0:T(8,128)(2,1)S(1)}, u32[]{:S(2)}, u32[]{:S(2)}) collective-permute-start(bf16[1024,128]{1,0:T(8,128)(2,1)S(1)} %collective-permute-done.14.refs_6_), channel_id=1, source_target_pairs={{0,4},{4,0},{8,12},{12,8},{16,20},{20,16},{24,28},{28,24},{1,5},{5... | collective-permute-start | bytes 786440 | tf_op jit(solution)/shard_map/ppermute | solution.py:453

commit v7 on v6

--- a/solution.py
+++ b/solution.py
@@ -402,11 +402,20 @@
     )(page_owner, *ends)
 
 
-def cache_kernel(count, owner_ref, *refs):
+def cache_kernel(paired, count, owner_ref, *refs):
     mids, totals = refs[:count], refs[count:-4]
     cache_hbm, made, page_of, sems = refs[-4:]
     place = lax.axis_index("seq")
-    places = [place ^ offset for offset in range(count)]
+    size = made.shape[1]
+    if paired:
+        odd = place % 2 == 1
+        chips = [place, place ^ jnp.where(odd, 4, 2), place ^ jnp.where(odd, 2, 4)]
+        sources = [
+            (mids[number], core * size, chip - chip % 2 + core) for number, chip in enumerate(chips) for core in range(2)
+        ]
+        sources += [(mids[3], 0, place ^ 6), (mids[4], 0, place ^ 7)]
+    else:
+        sources = [(mids[offset], 0, place ^ offset) for offset in range(count)]
     own_pages(owner_ref, place, page_of)
     parts = [(total, slot) for total in totals for slot in range(total.shape[0])]
     copies = []
@@ -418,11 +427,11 @@
         def _():
             made[slot] = total[row].astype(jnp.bfloat16)
 
-        for source in range(count):
-
-            @pl.when(halfway & (places[source] == page // 2))
+        for source, start, owner in sources:
+
+            @pl.when(halfway & (owner == page // 2))
             def _():
-                made[slot] = (total[row] + mids[source][...].astype(jnp.float32)).astype(jnp.bfloat16)
+                made[slot] = (total[row] + source[start : start + size].astype(jnp.float32)).astype(jnp.bfloat16)
 
         copies.append(pltpu.make_async_copy(made.at[slot], cache_hbm.at[slot], sems.at[slot]))
         copies[-1].start()
@@ -430,11 +439,11 @@
         copy.wait()
 
 
-def run_cache(page_owner, mids, totals):
-    size, dim = mids[0].shape
+def run_cache(page_owner, mids, totals, paired):
+    size, dim = totals[0].shape[1:]
     count = len(mids)
     return pl.pallas_call(
-        functools.partial(cache_kernel, count),
+        functools.partial(cache_kernel, paired, count),
         in_specs=[SMEM] + [VMEM] * (count + len(totals)),
         out_specs=HBM,
         out_shape=jax.ShapeDtypeStruct((SLOTS, size, dim), jnp.bfloat16),
@@ -451,6 +460,25 @@
 
 def swap(value, axis, offset):
     return lax.ppermute(value, axis, [(place, place ^ offset) for place in range(lax.axis_size(axis))])
+
+
+def pack_kernel(mine_ref, other_ref, both_ref):
+    core = lax.axis_index("seq") % 2
+    size = mine_ref.shape[0]
+    both_ref[pl.ds(pl.multiple_of(core * size, size), size)] = mine_ref[...]
+    both_ref[pl.ds(pl.multiple_of((1 - core) * size, size), size)] = other_ref[...]
+
+
+def pack(mine, other):
+    return pl.pallas_call(
+        pack_kernel,
+        in_specs=[VMEM, VMEM],
+        out_specs=VMEM,
+        out_shape=pltpu.VMEM((2 * mine.shape[0], mine.shape[1]), mine.dtype),
+        compiler_params=pltpu.CompilerParams(vmem_limit_bytes=4 * MIB),
+        cost_estimate=SMALL,
+        name="pack",
+    )(mine, other)
 
 
 def tie(value, *after):
@@ -486,9 +514,14 @@
     ends[1] = swap(end, "seq", 1)
     mids[1] = swap(mid, "seq", 1)
     inner, grown, done = run_inner(keys, values, held, cumulative, states, reached)
-    mid = tie(mid, done, ends[1], mids[1])
-    for offset in range(2, count, 2):
-        mids[offset] = swap(mid, "seq", offset)
+    paired = count == 8
+    if paired:
+        both = pack(mid, mids[1])
+        crossed = lax.ppermute(both, "seq", [(place, place ^ (4 if place % 2 else 2)) for place in range(count)])
+        far = swap(mid, "seq", 6)
+    else:
+        for offset in range(2, count, 2):
+            mids[offset] = swap(mid, "seq", offset)
     for offset in range(2, count, 2):
         ends[offset + 1] = swap(tie(ends[offset], done), "seq", 1)
     ends = [ends[offset] for offset in range(count)]
@@ -502,17 +535,19 @@
             totals.append(run_reach(tie(page_owner, square), ends, heads, *shares.pop(0)))
             other = tie(other, totals[-1])
         square = add(square, other)
-        if offset == 1:
-            for part in range(2, count, 2):
-                if part != count - 2:
-                    mids[part + 1] = swap(tie(mids[part], square), "seq", 1)
+        if offset == 1 and paired:
+            crossed_other = swap(tie(crossed, square), "seq", 1)
         offset *= 2
     for first, slots in shares:
         totals.append(run_reach(tie(page_owner, square), ends, heads, first, slots))
-    mids[count - 1] = swap(tie(mids[count - 2], square), "seq", 1)
-    mids = [mids[offset] for offset in range(count)]
+    if paired:
+        mids = [both, crossed, crossed_other, far, swap(tie(far, square), "seq", 1)]
+    else:
+        for offset in range(2, count, 2):
+            mids[offset + 1] = swap(mids[offset], "seq", 1)
+        mids = [mids[offset] for offset in range(count)]
     attended = run_scale(out, square, width * lax.axis_size("head"))
-    page_cache = run_cache(page_owner, mids, totals)
+    page_cache = run_cache(page_owner, mids, totals, paired)
     return attended, page_cache.reshape(SLOTS, heads, dim, dim)
 
 

time: 41.9 us -> 42.5 us (1.014)
  starting transfers between devices: 13.9 us -> 14.7 us
    ppermute x0 -> x1, starting transfers between devices: none -> 1.96 us  [shards(): lax.ppermute(both, 'seq', [(place, place ^ (4 if place % 2 else 2)) for p...]
    ppermute x16 -> x13, starting transfers between devices: 13.9 us -> 12.8 us  [swap(): lax.ppermute(value, axis, [(place, place ^ offset) for place in range(lax...]
    pallas_call x2, Pallas kernels: 2.62 us -> 2.18 us  [run_reach(): pl.pallas_call(functools.partial(reach_kernel, heads, first), in_specs=[S...]
    ppermute x16 -> x13, waiting for transfers between devices: 3.66 us -> 3.62 us  [swap(): lax.ppermute(value, axis, [(place, place ^ offset) for place in range(lax...]
    pallas_call x1 -> x2, Pallas kernels: 1.95 us -> 1.97 us  [the longest x1 1.91 us: run_cache(): pl.pallas_call(functools.partial(cache_kernel, paired, count), in_specs=[...]
  transfers between devices with their start and end apart: 16 -> 14, of which waited for: 5 -> 6; matrix products, arithmetic and copies ran while one was open for 0% -> 0% of each run, Pallas kernels for 41% -> 39%
where the time goes in v7:
time: 42.5 us; the launch traced here: 42.1 us
  Pallas kernels  23 us (54%)
  starting transfers between devices  14.7 us (35%)
  waiting for transfers between devices  3.62 us (9%)
  between operations  0.73 us (2%)
    ppermute x13, starting transfers between devices, swap(): lax.ppermute(value, axis, [(place, place ^ offset) for place in range(lax...  12.8 us
    pallas_call x1, Pallas kernels, run_inner(): pl.pallas_call(functools.partial(inner_kernel, heads), grid=(tokens // RO...  9.22 us
    pallas_call x1, Pallas kernels, run_states(): pl.pallas_call(functools.partial(state_kernel, heads), in_specs=[HBM] * 3...  4.47 us
    ppermute x13, waiting for transfers between devices, swap(): lax.ppermute(value, axis, [(place, place ^ offset) for place in range(lax...  3.62 us
    pallas_call x1, Pallas kernels, run_finish(): pl.pallas_call(functools.partial(finish_kernel, heads), grid=(tokens // P...  2.75 us
    pallas_call x1, Pallas kernels, run_scale(): pl.pallas_call(functools.partial(scale_kernel, whole_width), grid=(tokens...  2.38 us
    pallas_call x2, Pallas kernels, run_reach(): pl.pallas_call(functools.partial(reach_kernel, heads, first), in_specs=[S...  2.18 us
    ppermute x1, starting transfers between devices, shards(): lax.ppermute(both, 'seq', [(place, place ^ (4 if place % 2 else 2)) for p...  1.96 us
  transfers between devices with their start and end apart: 14, of which 6 were waited for; matrix products, arithmetic and copies ran while one was open for 0% of the time, Pallas kernels for 39%

profile of v7, /device:TPU:0, one launch (start us, length us, event | category | flops | bytes accessed | tf_op | source)
XLA Modules:
  0.0 42.1 jit_solution(8082574254753245106)
XLA Ops:
  0.6 0.0 copy-start
  0.6 4.5 %states.1 = (f32[8,2048]{1,0:T(8,128)S(1)}, bf16[8,1024,128]{2,1,0:T(8,128)(2,1)S(1)}, f32[8,8,128]{2,1,0:T(8,128)S(1)}, bf16[1072,128]{1,0:T(8,128)(2,1)S(1)}, ...) custom-call(bf16[2048,1024]{1,0:T(8,128)(2,1)} %key_hbm.1, ...), custom_call_target="tpu_custom_call" | custom-call | flops 1 | bytes 1 | tf_op jit(solution)/shard_map/states/pallas_call | solution.py:115
  5.1 0.5 %collective-permute-start.9 = (bf16[1024,128]{1,0:T(8,128)(2,1)S(1)}, bf16[1024,128]{1,0:T(8,128)(2,1)S(1)}, u32[]{:S(2)}, u32[]{:S(2)}) collective-permute-start(bf16[1024,128]{1,0:T(8,128)(2,1)S(1)} %get-tuple-element.43.mine_ref), channel_id=1, source_target_pairs={{0,4},{4,0},{8,12},{12,8},{16,20},{20,16},{24,28},{28,24},{1,5},{5... | collective-permute-start | bytes 786440 | tf_op jit(solution)/shard_map/ppermute | solution.py:462
  5.6 3.5 %collective-permute-start.5 = (bf16[1072,128]{1,0:T(8,128)(2,1)S(1)}, bf16[1072,128]{1,0:T(8,128)(2,1)S(1)}, u32[]{:S(2)}, u32[]{:S(2)}) collective-permute-start(bf16[1072,128]{1,0:T(8,128)(2,1)S(1)} %get-tuple-element.32.refs_0_), channel_id=1, source_target_pairs={{0,24},{4,28},{8,16},{12,20},{16,8},{20,12},{24,0},{28,4},{1,25},{... | collective-permute-start | bytes 823304 | tf_op jit(solution)/shard_map/ppermute | solution.py:462
  9.2 0.5 %collective-permute-start.3 = (bf16[1072,128]{1,0:T(8,128)(2,1)S(1)}, bf16[1072,128]{1,0:T(8,128)(2,1)S(1)}, u32[]{:S(2)}, u32[]{:S(2)}) collective-permute-start(bf16[1072,128]{1,0:T(8,128)(2,1)S(1)} %get-tuple-element.32.refs_0_), channel_id=1, source_target_pairs={{0,16},{4,20},{8,24},{12,28},{16,0},{20,4},{24,8},{28,12},{1,17},{... | collective-permute-start | bytes 823304 | tf_op jit(solution)/shard_map/ppermute | solution.py:462
  9.7 0.1 collective-permute-start.1
  9.8 0.0 collective-permute-done.9.other_ref
  9.8 0.1 pack.1.refs_0_
  9.9 2.0 %collective-permute-start.10 = (bf16[2048,128]{1,0:T(8,128)(2,1)S(1)}, bf16[2048,128]{1,0:T(8,128)(2,1)S(1)}, u32[]{:S(2)}, u32[]{:S(2)}) collective-permute-start(bf16[2048,128]{1,0:T(8,128)(2,1)S(1)} %pack.1.refs_0_), channel_id=1, source_target_pairs={{0,8},{4,20},{8,0},{12,28},{16,24},{20,4},{24,16},{28,12},{1,9},{5... | collective-permute-start | bytes 1572872 | tf_op jit(solution)/shard_map/ppermute | solution.py:520
  11.8 0.0 collective-permute-start
  11.8 0.0 copy-done
  11.8 0.0 copy-start.2
  11.8 9.2 %inner.1 = (f32[2048,1024]{1,0:T(8,128)S(1)}, bf16[2048,1024]{1,0:T(8,128)(2,1)S(1)}, f32[8,128]{1,0:T(8,128)}) custom-call(bf16[2048,1024]{1,0:T(8,128)(2,1)S(1)} %get-tuple-element.24.keys, bf16[2048,1024]{1,0:T(8,128)(2,1)S(1)} %get-tuple-element.25.values, bf16[2048,1024]{1,0:T(8,128)(2,1)S(1)} %copy-done, f32[8,2048]{1,0:T(8,128)S(1)} %get-tuple-element.26.cum_ref, ...), custom_call_target="tpu_custom_call" | custom-call | flops 1 | bytes 1 | tf_op jit(solution)/shard_map/inner/pallas_call | solution.py:193
  21.0 0.0 collective-permute-done.5.refs_6_
  21.0 0.5 %collective-permute-start.6 = (bf16[1072,128]{1,0:T(8,128)(2,1)S(1)}, bf16[1072,128]{1,0:T(8,128)(2,1)S(1)}, u32[]{:S(2)}, u32[]{:S(2)}) collective-permute-start(bf16[1072,128]{1,0:T(8,128)(2,1)S(1)} %collective-permute-done.5.refs_6_), channel_id=1, source_target_pairs={{0,4},{4,0},{8,12},{12,8},{16,20},{20,16},{24,28},{28,24},{1,5},{5... | collective-permute-start | bytes 823304 | tf_op jit(solution)/shard_map/ppermute | solution.py:462
  21.5 0.7 %collective-permute-done.3.refs_4_ = bf16[1072,128]{1,0:T(8,128)(2,1)S(1)} collective-permute-done((bf16[1072,128]{1,0:T(8,128)(2,1)S(1)}, bf16[1072,128]{1,0:T(8,128)(2,1)S(1)}, u32[]{:S(2)}, u32[]{:S(2)}) %collective-permute-start.3) | collective-permute-done | bytes 274464 | tf_op jit(solution)/shard_map/ppermute | solution.py:462
  22.3 0.0 collective-permute-start.4
  22.3 0.2 collective-permute-done.1.refs_2_
  22.5 0.3 collective-permute-start.2
  22.8 0.0 collective-permute-done.refs_1_
  22.8 0.0 collective-permute-done.6.refs_7_
  22.8 1.0 %collective-permute-done.4.refs_5_ = bf16[1072,128]{1,0:T(8,128)(2,1)S(1)} collective-permute-done((bf16[1072,128]{1,0:T(8,128)(2,1)S(1)}, bf16[1072,128]{1,0:T(8,128)(2,1)S(1)}, u32[]{:S(2)}, u32[]{:S(2)}) %collective-permute-start.4) | collective-permute-done | bytes 274464 | tf_op jit(solution)/shard_map/ppermute | solution.py:462
  23.8 0.4 collective-permute-done.2.refs_3_
  24.2 0.0 copy-done.2
  24.2 0.0 copy-start.1
  24.2 2.7 %finish.1 = (f32[2048,1024]{1,0:T(8,128)S(1)}, f32[16,128]{1,0:T(8,128)S(1)}) custom-call(f32[2048,1024]{1,0:T(8,128)S(1)} %get-tuple-element.30.inner_ref, bf16[2048,1024]{1,0:T(8,128)(2,1)S(1)} %get-tuple-element.31.grown, f32[1,1024]{1,0:T(1,128)S(1)} %bitcast.2, bf16[1072,128]{1,0:T(8,128)(2,1)S(1)} %get-tuple-element.32.refs_0_, ...), custom_call_target="tpu_custom_call" | custom-call | flops 1 | bytes 1 | tf_op jit(solution)/shard_map/finish/pallas_call | solution.py:277
  27.0 1.8 %collective-permute-start.7 = (f32[16,128]{1,0:T(8,128)S(1)}, f32[16,128]{1,0:T(8,128)S(1)}, u32[]{:S(2)}, u32[]{:S(2)}) collective-permute-start(f32[16,128]{1,0:T(8,128)S(1)} %get-tuple-element.38.one_ref), channel_id=1, source_target_pairs={{0,1},{1,0},{2,3},{3,2},{4,5},{5,4},{6,7},{7,6},{8,9},{9,8},{10,11... | collective-permute-start | bytes 24584 | tf_op jit(solution)/shard_map/ppermute | solution.py:462
  28.8 2.4 %collective-permute-start.12 = (bf16[1024,128]{1,0:T(8,128)(2,1)S(1)}, bf16[1024,128]{1,0:T(8,128)(2,1)S(1)}, u32[]{:S(2)}, u32[]{:S(2)}) collective-permute-start(bf16[1024,128]{1,0:T(8,128)(2,1)S(1)} %get-tuple-element.43.mine_ref), channel_id=1, source_target_pairs={{0,24},{4,28},{8,16},{12,20},{16,8},{20,12},{24,0},{28,4},{1,25},{... | collective-permute-start | bytes 786440 | tf_op jit(solution)/shard_map/ppermute | solution.py:462
  31.2 0.0 copy-done.1
  31.2 1.3 %reach.2.refs_5_ = f32[3,1024,128]{2,1,0:T(8,128)S(1)} custom-call(s32[16]{0:T(128)S(1)} %copy-done.1, bf16[1072,128]{1,0:T(8,128)(2,1)S(1)} %get-tuple-element.32.refs_0_, bf16[1072,128]{1,0:T(8,128)(2,1)S(1)} %collective-permute-done.refs_1_, bf16[1072,128]{1,0:T(8,128)(2,1)S(1)} %collective-permute-done.1.refs_2_, ...), custom_call_target="tpu_custom_call" | custom-call | flops 1 | bytes 1 | tf_op jit(solution)/shard_map/reach/pallas_call | solution.py:389
  32.6 0.0 collective-permute-done.7.two_ref
  32.6 0.0 collective-permute-done.10.refs_1_
  32.6 0.5 %collective-permute-start.11 = (bf16[2048,128]{1,0:T(8,128)(2,1)S(1)}, bf16[2048,128]{1,0:T(8,128)(2,1)S(1)}, u32[]{:S(2)}, u32[]{:S(2)}) collective-permute-start(bf16[2048,128]{1,0:T(8,128)(2,1)S(1)} %collective-permute-done.10.refs_1_), channel_id=1, source_target_pairs={{0,4},{4,0},{8,12},{12,8},{16,20},{20,16},{24,28},{28,24},{1,5},{5... | collective-permute-start | bytes 1572872 | tf_op jit(solution)/shard_map/ppermute | solution.py:462
  33.1 2.6 %collective-permute-start.8 = (f32[16,128]{1,0:T(8,128)S(1)}, f32[16,128]{1,0:T(8,128)S(1)}, u32[]{:S(2)}, u32[]{:S(2)}) collective-permute-start(f32[16,128]{1,0:T(8,128)S(1)} %add.2.one_ref), channel_id=1, source_target_pairs={{0,2},{1,3},{2,0},{3,1},{4,6},{5,7},{6,4},{7,5},{8,10},{9,11},{10,... | collective-permute-start | bytes 24584 | tf_op jit(solution)/shard_map/ppermute | solution.py:462
  35.7 0.8 %reach.3.refs_6_ = f32[2,1024,128]{2,1,0:T(8,128)S(1)} custom-call(s32[16]{0:T(128)S(1)} %copy-done.1, bf16[1072,128]{1,0:T(8,128)(2,1)S(1)} %get-tuple-element.32.refs_0_, bf16[1072,128]{1,0:T(8,128)(2,1)S(1)} %collective-permute-done.refs_1_, bf16[1072,128]{1,0:T(8,128)(2,1)S(1)} %collective-permute-done.1.refs_2_, ...), custom_call_target="tpu_custom_call" | custom-call | flops 1 | bytes 1 | tf_op jit(solution)/shard_map/reach/pallas_call | solution.py:389
  36.5 1.1 %collective-permute-done.8.two_ref = f32[16,128]{1,0:T(8,128)S(1)} collective-permute-done((f32[16,128]{1,0:T(8,128)S(1)}, f32[16,128]{1,0:T(8,128)S(1)}, u32[]{:S(2)}, u32[]{:S(2)}) %collective-permute-start.8) | collective-permute-done | bytes 8224 | tf_op jit(solution)/shard_map/ppermute | solution.py:462
  37.7 0.1 collective-permute-done.12.refs_3_
  37.7 0.0 collective-permute-start.13
  37.8 2.4 %scale.1 = bf16[2048,1024]{1,0:T(8,128)(2,1)} custom-call(f32[2048,1024]{1,0:T(8,128)S(1)} %get-tuple-element.37.out_ref, f32[16,128]{1,0:T(8,128)S(1)} %add.3.square), custom_call_target="tpu_custom_call" | custom-call | flops 1 | bytes 1 | tf_op jit(solution)/shard_map/scale/pallas_call | solution.py:323
  40.1 0.0 collective-permute-done.13.refs_4_
  40.2 0.0 collective-permute-done.11.refs_2_
  40.2 1.9 %cache.1 = bf16[5,1024,128]{2,1,0:T(8,128)(2,1)} custom-call(s32[16]{0:T(128)S(1)} %copy-done.1, bf16[2048,128]{1,0:T(8,128)(2,1)S(1)} %pack.1.refs_0_, bf16[2048,128]{1,0:T(8,128)(2,1)S(1)} %collective-permute-done.10.refs_1_, bf16[2048,128]{1,0:T(8,128)(2,1)S(1)} %collective-permute-done.11.refs_2_, bf16[1024,128]{1,0:T(8,128)(2,1)S(1)} %collective-permute-done.12.refs_3_, ...), custom_call_target="tpu_custom_call" | custom-call | flops 1 | bytes 1 | tf_op jit(solution)/shard_map/cache/pallas_call | solution.py:445
  (2 shorter events, 0.0 us)
Async XLA Ops:
  0.6 11.2 %copy-start = (bf16[2048,1024]{1,0:T(8,128)(2,1)S(1)}, bf16[2048,1024]{1,0:T(8,128)(2,1)}, u32[]{:S(2)}) copy-start(bf16[2048,1024]{1,0:T(8,128)(2,1)} %queries) | copy-start | bytes 12582916
  5.1 4.7 %collective-permute-start.9 = (bf16[1024,128]{1,0:T(8,128)(2,1)S(1)}, bf16[1024,128]{1,0:T(8,128)(2,1)S(1)}, u32[]{:S(2)}, u32[]{:S(2)}) collective-permute-start(bf16[1024,128]{1,0:T(8,128)(2,1)S(1)} %get-tuple-element.43.mine_ref), channel_id=1, source_target_pairs={{0,4},{4,0},{8,12},{12,8},{16,20},{20,16},{24,28},{28,24},{1,5},{5... | collective-permute-start | bytes 786440 | tf_op jit(solution)/shard_map/ppermute | solution.py:462
  5.6 15.4 %collective-permute-start.5 = (bf16[1072,128]{1,0:T(8,128)(2,1)S(1)}, bf16[1072,128]{1,0:T(8,128)(2,1)S(1)}, u32[]{:S(2)}, u32[]{:S(2)}) collective-permute-start(bf16[1072,128]{1,0:T(8,128)(2,1)S(1)} %get-tuple-element.32.refs_0_), channel_id=1, source_target_pairs={{0,24},{4,28},{8,16},{12,20},{16,8},{20,12},{24,0},{28,4},{1,25},{... | collective-permute-start | bytes 823304 | tf_op jit(solution)/shard_map/ppermute | solution.py:462
  9.2 13.1 %collective-permute-start.3 = (bf16[1072,128]{1,0:T(8,128)(2,1)S(1)}, bf16[1072,128]{1,0:T(8,128)(2,1)S(1)}, u32[]{:S(2)}, u32[]{:S(2)}) collective-permute-start(bf16[1072,128]{1,0:T(8,128)(2,1)S(1)} %get-tuple-element.32.refs_0_), channel_id=1, source_target_pairs={{0,16},{4,20},{8,24},{12,28},{16,0},{20,4},{24,8},{28,12},{1,17},{... | collective-permute-start | bytes 823304 | tf_op jit(solution)/shard_map/ppermute | solution.py:462
  9.7 12.8 %collective-permute-start.1 = (bf16[1072,128]{1,0:T(8,128)(2,1)S(1)}, bf16[1072,128]{1,0:T(8,128)(2,1)S(1)}, u32[]{:S(2)}, u32[]{:S(2)}) collective-permute-start(bf16[1072,128]{1,0:T(8,128)(2,1)S(1)} %get-tuple-element.32.refs_0_), channel_id=1, source_target_pairs={{0,8},{4,12},{8,0},{12,4},{16,24},{20,28},{24,16},{28,20},{1,9},{5... | collective-permute-start | bytes 823304 | tf_op jit(solution)/shard_map/ppermute | solution.py:462
  9.9 22.7 %collective-permute-start.10 = (bf16[2048,128]{1,0:T(8,128)(2,1)S(1)}, bf16[2048,128]{1,0:T(8,128)(2,1)S(1)}, u32[]{:S(2)}, u32[]{:S(2)}) collective-permute-start(bf16[2048,128]{1,0:T(8,128)(2,1)S(1)} %pack.1.refs_0_), channel_id=1, source_target_pairs={{0,8},{4,20},{8,0},{12,28},{16,24},{20,4},{24,16},{28,12},{1,9},{5... | collective-permute-start | bytes 1572872 | tf_op jit(solution)/shard_map/ppermute | solution.py:520
  11.8 11.0 %collective-permute-start = (bf16[1072,128]{1,0:T(8,128)(2,1)S(1)}, bf16[1072,128]{1,0:T(8,128)(2,1)S(1)}, u32[]{:S(2)}, u32[]{:S(2)}) collective-permute-start(bf16[1072,128]{1,0:T(8,128)(2,1)S(1)} %get-tuple-element.32.refs_0_), channel_id=1, source_target_pairs={{0,4},{4,0},{8,12},{12,8},{16,20},{20,16},{24,28},{28,24},{1,5},{5... | collective-permute-start | bytes 823304 | tf_op jit(solution)/shard_map/ppermute | solution.py:462
  11.8 12.4 %copy-start.2 = (f32[1024]{0:T(1024)S(1)}, f32[1024]{0:T(1024)}, u32[]{:S(2)}) copy-start(f32[1024]{0:T(1024)} %param.10) | copy-start | bytes 12292
  21.0 1.7 %collective-permute-start.6 = (bf16[1072,128]{1,0:T(8,128)(2,1)S(1)}, bf16[1072,128]{1,0:T(8,128)(2,1)S(1)}, u32[]{:S(2)}, u32[]{:S(2)}) collective-permute-start(bf16[1072,128]{1,0:T(8,128)(2,1)S(1)} %collective-permute-done.5.refs_6_), channel_id=1, source_target_pairs={{0,4},{4,0},{8,12},{12,8},{16,20},{20,16},{24,28},{28,24},{1,5},{5... | collective-permute-start | bytes 823304 | tf_op jit(solution)/shard_map/ppermute | solution.py:462
  22.3 1.6 %collective-permute-start.4 = (bf16[1072,128]{1,0:T(8,128)(2,1)S(1)}, bf16[1072,128]{1,0:T(8,128)(2,1)S(1)}, u32[]{:S(2)}, u32[]{:S(2)}) collective-permute-start(bf16[1072,128]{1,0:T(8,128)(2,1)S(1)} %collective-permute-done.3.refs_4_), channel_id=1, source_target_pairs={{0,4},{4,0},{8,12},{12,8},{16,20},{20,16},{24,28},{28,24},{1,5},{5... | collective-permute-start | bytes 823304 | tf_op jit(solution)/shard_map/ppermute | solution.py:462
  22.5 1.7 %collective-permute-start.2 = (bf16[1072,128]{1,0:T(8,128)(2,1)S(1)}, bf16[1072,128]{1,0:T(8,128)(2,1)S(1)}, u32[]{:S(2)}, u32[]{:S(2)}) collective-permute-start(bf16[1072,128]{1,0:T(8,128)(2,1)S(1)} %collective-permute-done.1.refs_2_), channel_id=1, source_target_pairs={{0,4},{4,0},{8,12},{12,8},{16,20},{20,16},{24,28},{28,24},{1,5},{5... | collective-permute-start | bytes 823304 | tf_op jit(solution)/shard_map/ppermute | solution.py:462
  24.2 7.0 %copy-start.1 = (s32[16]{0:T(128)S(1)}, s32[16]{0:T(128)}, u32[]{:S(2)}) copy-start(s32[16]{0:T(128)} %owner_ref.3) | copy-start | bytes 196
  27.0 5.6 %collective-permute-start.7 = (f32[16,128]{1,0:T(8,128)S(1)}, f32[16,128]{1,0:T(8,128)S(1)}, u32[]{:S(2)}, u32[]{:S(2)}) collective-permute-start(f32[16,128]{1,0:T(8,128)S(1)} %get-tuple-element.38.one_ref), channel_id=1, source_target_pairs={{0,1},{1,0},{2,3},{3,2},{4,5},{5,4},{6,7},{7,6},{8,9},{9,8},{10,11... | collective-permute-start | bytes 24584 | tf_op jit(solution)/shard_map/ppermute | solution.py:462
  28.8 9.0 %collective-permute-start.12 = (bf16[1024,128]{1,0:T(8,128)(2,1)S(1)}, bf16[1024,128]{1,0:T(8,128)(2,1)S(1)}, u32[]{:S(2)}, u32[]{:S(2)}) collective-permute-start(bf16[1024,128]{1,0:T(8,128)(2,1)S(1)} %get-tuple-element.43.mine_ref), channel_id=1, source_target_pairs={{0,24},{4,28},{8,16},{12,20},{16,8},{20,12},{24,0},{28,4},{1,25},{... | collective-permute-start | bytes 786440 | tf_op jit(solution)/shard_map/ppermute | solution.py:462
  32.6 7.6 %collective-permute-start.11 = (bf16[2048,128]{1,0:T(8,128)(2,1)S(1)}, bf16[2048,128]{1,0:T(8,128)(2,1)S(1)}, u32[]{:S(2)}, u32[]{:S(2)}) collective-permute-start(bf16[2048,128]{1,0:T(8,128)(2,1)S(1)} %collective-permute-done.10.refs_1_), channel_id=1, source_target_pairs={{0,4},{4,0},{8,12},{12,8},{16,20},{20,16},{24,28},{28,24},{1,5},{5... | collective-permute-start | bytes 1572872 | tf_op jit(solution)/shard_map/ppermute | solution.py:462
  33.1 4.5 %collective-permute-start.8 = (f32[16,128]{1,0:T(8,128)S(1)}, f32[16,128]{1,0:T(8,128)S(1)}, u32[]{:S(2)}, u32[]{:S(2)}) collective-permute-start(f32[16,128]{1,0:T(8,128)S(1)} %add.2.one_ref), channel_id=1, source_target_pairs={{0,2},{1,3},{2,0},{3,1},{4,6},{5,7},{6,4},{7,5},{8,10},{9,11},{10,... | collective-permute-start | bytes 24584 | tf_op jit(solution)/shard_map/ppermute | solution.py:462
  37.7 2.4 %collective-permute-start.13 = (bf16[1024,128]{1,0:T(8,128)(2,1)S(1)}, bf16[1024,128]{1,0:T(8,128)(2,1)S(1)}, u32[]{:S(2)}, u32[]{:S(2)}) collective-permute-start(bf16[1024,128]{1,0:T(8,128)(2,1)S(1)} %collective-permute-done.12.refs_3_), channel_id=1, source_target_pairs={{0,4},{4,0},{8,12},{12,8},{16,20},{20,16},{24,28},{28,24},{1,5},{5... | collective-permute-start | bytes 786440 | tf_op jit(solution)/shard_map/ppermute | solution.py:462
